TPU v7x, 128 devices: a whole 4x4x4 slice. The times are simulated.
128 devices in a mesh: dp: 32 (over y, x, z_lo), pool: 4 (over z_hi, core).
Axes of the slice: x: 4, y: 4, z: 4 (z_hi: 2, z_lo: 2; z = z_hi * 2 + z_lo), core: 2. Of those that a mesh axis runs over, the one named last changes fastest.
Arguments:
- hidden_in: bfloat16 [2048, 3584], P(('dp', 'pool')), may hold values from -6 to 6
- expert_ids: int32 [2048, 8], P(('dp', 'pool')), may hold values from 0 to 31, all different within a row; in each aligned block of 16 rows (0 to 15, 16 to 31, ...) at most 8 rows name the same one
- gate_vals: float32 [2048, 8], P(('dp', 'pool')), may hold values from 0.05 to 0.6
- w_gate: bfloat16 [32, 3584, 2048], P('dp', None, 'pool'), may hold values from -0.09375 to 0.09375
- w_up: bfloat16 [32, 3584, 2048], P('dp', None, 'pool'), may hold values from -0.09375 to 0.09375
- w_down: bfloat16 [32, 2048, 3584], P('dp', 'pool'), may hold values from -0.125 to 0.125
- w_latent: bfloat16 [3584, 512], replicated, may hold values from -0.09375 to 0.09375
- w_rope: bfloat16 [3584, 64], replicated, may hold values from -0.09375 to 0.09375
- latent_gain: float32 [512], replicated, may hold values from 0.5 to 1.5
- cache_latent: bfloat16 [1024, 128, 512], P(('dp', 'pool')), may hold values from -6 to 6
- cache_rope: bfloat16 [1024, 64, 128], P(('dp', 'pool')), may hold values from -6 to 6
- send_index: int32 [128, 32], P(('dp', 'pool')), may hold values from 0 to 7
- block_table: int32 [32, 4, 32], P('dp'), may hold values from 0 to 127, as said below
- cached_len: int32 [32, 4], P('dp'), may hold values from 1 to 4096, as said below
- new_counts: int32 [32, 4], P('dp'), may hold values from 1 to 32, 64 in all within a row
- q_latent: bfloat16 [2048, 64, 512], P('dp', 'pool'), may hold values from -7 to 7
- q_rope: bfloat16 [2048, 4096], P('dp', 'pool'), may hold values from -6 to 6
Outputs:
- hidden_out: bfloat16 [2048, 3584], P(('dp', 'pool'))
- new_latent: bfloat16 [2048, 512], P(('dp', 'pool'))
- new_rope: bfloat16 [2048, 64], P(('dp', 'pool'))
- context: bfloat16 [2048, 64, 512], P('dp', 'pool')
Inputs may be any that keep to these rules, and one draw needn't show every extreme that they name: `expert_ids`: each row names 8 different experts; among the 16 rows of one device at most 8 name one expert, a bound that some block reaches of them. `new_counts`: the 4 counts of a rank sum to 64, and one of them is 32. `cached_len`: every rank has a chat of exactly 4096 cached tokens. `block_table`: entry j of chat c of rank r, for j below the chat's number of cached blocks, is the index along dp+pool of the holder device that serves that block; no holder device appears twice among one rank's blocks; all other entries are 0.
All inputs are finite; a program needn't handle non-finite values.
Results may differ from a plain program's by a relative error of at most 0.015.
Values may be sent and summed in bfloat16 or wider, within the bound.
A program may use at most 192 MiB of HBM per device.

v0:
```python
import jax
import jax.numpy as jnp
from jax import lax
from jax.sharding import PartitionSpec as P

SCORE_SCALE = 192.0 ** (-0.5)
ROPE_BASE = 10000.0
NORM_EPS = 1e-06


def rotate(values, positions):
    half = values.shape[-1] // 2
    exponent = jnp.arange(half).astype(jnp.float32) * (-2.0 / values.shape[-1])
    frequency = jnp.power(jnp.float32(ROPE_BASE), exponent)
    angle = positions.astype(jnp.float32)[:, None] * frequency[None, :]
    first = values[:, :half]
    second = values[:, half:]
    cosine = jnp.cos(angle)
    sine = jnp.sin(angle)
    return jnp.concatenate([first * cosine - second * sine, second * cosine + first * sine], axis=1)


def chat_positions(counts, lengths, local):
    ends = jnp.cumsum(counts)
    chat_of = jnp.sum((local[:, None] >= ends[None, :]).astype(jnp.int32), axis=1)
    starts = ends - counts
    onehot = (chat_of[:, None] == jnp.arange(counts.shape[0])[None, :]).astype(jnp.int32)
    return jnp.sum(onehot * (lengths - starts)[None, :], axis=1) + local


def expert_rows(flat_rows, gate_matrix, up_matrix, down_matrix):
    gate = jnp.dot(flat_rows, gate_matrix, preferred_element_type=jnp.float32)
    lifted = jnp.dot(flat_rows, up_matrix, preferred_element_type=jnp.float32)
    activated = (jax.nn.silu(gate) * lifted).astype(jnp.bfloat16)
    return jnp.dot(activated, down_matrix, preferred_element_type=jnp.float32).astype(jnp.bfloat16)


def shards(
    hidden_in,
    expert_ids,
    gate_vals,
    w_gate,
    w_up,
    w_down,
    w_latent,
    w_rope,
    latent_gain,
    cache_latent,
    cache_rope,
    send_index,
    block_table,
    cached_len,
    new_counts,
    q_latent,
    q_rope,
):
    n_dp = lax.axis_size("dp")
    n_pool = lax.axis_size("pool")
    wanted = send_index[0]
    sent_latent = cache_latent[wanted]
    sent_rope = cache_rope[wanted]
    table = block_table[0]
    copies_latent = jnp.broadcast_to(
        sent_latent[:, None], (n_dp, n_pool) + sent_latent.shape[1:]
    ).reshape((n_dp * n_pool,) + sent_latent.shape[1:])
    copies_rope = jnp.broadcast_to(
        sent_rope[:, None], (n_dp, n_pool) + sent_rope.shape[1:]
    ).reshape((n_dp * n_pool,) + sent_rope.shape[1:])
    held_latent, held_rope = (
        lax.all_to_all(copies_latent, ("dp", "pool"), split_axis=0, concat_axis=0, tiled=True),
        lax.all_to_all(copies_rope, ("dp", "pool"), split_axis=0, concat_axis=0, tiled=True),
    )
    rows, width = hidden_in.shape
    fan_count = expert_ids.shape[1]
    capacity = min(rows, 2 * rows * fan_count // n_dp)
    slots = n_dp * capacity
    flat_ids = expert_ids.reshape(-1)
    onehot = (flat_ids[:, None] == jnp.arange(n_dp)[None, :]).astype(jnp.int32)
    before = jnp.cumsum(onehot, axis=0) - onehot
    target = flat_ids * capacity + jnp.sum(before * onehot, axis=1)
    match = (target[:, None] == jnp.arange(slots)[None, :]).astype(jnp.float32)
    picks = jnp.sum(match.reshape(rows, fan_count, slots), axis=1)
    weights = jnp.sum(
        (match * gate_vals.reshape(-1)[:, None]).reshape(rows, fan_count, slots), axis=1
    )
    outgoing = lax.dot_general(
        picks.astype(jnp.bfloat16),
        hidden_in,
        (((0,), (0,)), ((), ())),
        preferred_element_type=jnp.float32,
    ).astype(jnp.bfloat16)
    gate_matrix = w_gate[0]
    up_matrix = w_up[0]
    down_matrix = w_down[0]
    spread = jnp.broadcast_to(
        outgoing.reshape(n_dp, 1, capacity, width), (n_dp, n_pool, capacity, width)
    ).reshape(n_dp * n_pool, capacity, width)
    arrived = lax.all_to_all(spread, ("dp", "pool"), split_axis=0, concat_axis=0, tiled=True)
    partial_value = expert_rows(
        arrived.reshape(-1, width), gate_matrix, up_matrix, down_matrix
    ).reshape(arrived.shape)
    returned = lax.all_to_all(
        partial_value, ("dp", "pool"), split_axis=0, concat_axis=0, tiled=True
    )
    summed = jnp.sum(returned.reshape(n_dp, n_pool, capacity, width), axis=1, dtype=jnp.float32)
    mixed = jnp.dot(
        weights,
        summed.reshape(slots, width),
        precision=lax.Precision.HIGHEST,
        preferred_element_type=jnp.float32,
    )
    hidden_out = (hidden_in.astype(jnp.float32) + mixed).astype(jnp.bfloat16)
    latent = jnp.dot(hidden_out, w_latent, preferred_element_type=jnp.float32)
    norm_scale = lax.rsqrt(jnp.mean(latent * latent, axis=1, keepdims=True) + NORM_EPS)
    new_latent = (latent * norm_scale * latent_gain[None, :]).astype(jnp.bfloat16)
    counts = new_counts[0]
    lengths = cached_len[0]
    local = lax.axis_index("pool") * rows + jnp.arange(rows, dtype=jnp.int32)
    positions = chat_positions(counts, lengths, local)
    new_rope = rotate(
        jnp.dot(hidden_out, w_rope, preferred_element_type=jnp.float32), positions
    ).astype(jnp.bfloat16)
    fresh_latent, fresh_rope = (
        lax.all_gather(new_latent, "pool", axis=0, tiled=True),
        lax.all_gather(new_rope, "pool", axis=0, tiled=True),
    )
    tok_rank, heads_dev, lat_width = q_latent.shape
    rope_width = w_rope.shape[1]
    new_most = tok_rank // 2
    block_len = held_latent.shape[1]
    key_count = table.shape[1] * block_len
    starts = jnp.cumsum(counts) - counts
    query_latent = jnp.concatenate(
        [q_latent, jnp.zeros((new_most, heads_dev, lat_width), jnp.bfloat16)], axis=0
    )
    query_rope = jnp.concatenate(
        [
            q_rope.reshape(tok_rank, heads_dev, rope_width),
            jnp.zeros((new_most, heads_dev, rope_width), jnp.bfloat16),
        ],
        axis=0,
    )
    padded_latent = jnp.concatenate(
        [fresh_latent, jnp.zeros((new_most, lat_width), jnp.bfloat16)], axis=0
    )
    padded_rope = jnp.concatenate(
        [fresh_rope, jnp.zeros((new_most, rope_width), jnp.bfloat16)], axis=0
    )
    offsets = jnp.arange(new_most, dtype=jnp.int32)
    row_offset = jnp.arange(new_most * heads_dev, dtype=jnp.int32) // heads_dev
    contract = (((1,), (1,)), ((), ()))
    context = jnp.zeros((tok_rank + new_most, heads_dev, lat_width), jnp.bfloat16)
    for chat in range(table.shape[0]):
        start = starts[chat]
        place = table[chat]
        keys_latent = held_latent[place].reshape(key_count, lat_width)
        keys_rope = held_rope[place]
        asks_latent = lax.dynamic_slice_in_dim(query_latent, start, new_most, 0).reshape(
            -1, lat_width
        )
        asks_rope = lax.dynamic_slice_in_dim(query_rope, start, new_most, 0).reshape(-1, rope_width)
        mine_latent = lax.dynamic_slice_in_dim(padded_latent, start, new_most, 0)
        mine_rope = lax.dynamic_slice_in_dim(padded_rope, start, new_most, 0)
        rope_part = jnp.einsum(
            "nr,brk->nbk", asks_rope, keys_rope, preferred_element_type=jnp.float32
        ).reshape(-1, key_count)
        old_scores = (
            lax.dot_general(asks_latent, keys_latent, contract, preferred_element_type=jnp.float32)
            + rope_part
        ) * SCORE_SCALE
        new_scores = (
            lax.dot_general(asks_latent, mine_latent, contract, preferred_element_type=jnp.float32)
            + lax.dot_general(asks_rope, mine_rope, contract, preferred_element_type=jnp.float32)
        ) * SCORE_SCALE
        old_ok = (jnp.arange(key_count) < lengths[chat])[None, :]
        new_ok = (offsets[None, :] <= row_offset[:, None]) & (offsets[None, :] < counts[chat])
        row_max = jnp.maximum(
            jnp.max(jnp.where(old_ok, old_scores, -jnp.inf), axis=1),
            jnp.max(jnp.where(new_ok, new_scores, -jnp.inf), axis=1),
        )
        old_weight = jnp.where(old_ok, jnp.exp(old_scores - row_max[:, None]), 0.0)
        new_weight = jnp.where(new_ok, jnp.exp(new_scores - row_max[:, None]), 0.0)
        total = jnp.sum(old_weight, axis=1) + jnp.sum(new_weight, axis=1)
        blended = jnp.dot(
            old_weight.astype(jnp.bfloat16), keys_latent, preferred_element_type=jnp.float32
        ) + jnp.dot(
            new_weight.astype(jnp.bfloat16), mine_latent, preferred_element_type=jnp.float32
        )
        result = (
            (blended / total[:, None]).astype(jnp.bfloat16).reshape(new_most, heads_dev, lat_width)
        )
        old_rows = lax.dynamic_slice_in_dim(context, start, new_most, 0)
        keep = (offsets < counts[chat])[:, None, None]
        context = lax.dynamic_update_slice_in_dim(
            context, jnp.where(keep, result, old_rows), start, 0
        )
    return (hidden_out, new_latent, new_rope, context[:tok_rank])


def solution(mesh):
    return jax.shard_map(
        shards,
        mesh=mesh,
        in_specs=(
            P(("dp", "pool"), None),
            P(("dp", "pool"), None),
            P(("dp", "pool"), None),
            P("dp", None, "pool"),
            P("dp", None, "pool"),
            P("dp", "pool", None),
            P(),
            P(),
            P(),
            P(("dp", "pool"), None, None),
            P(("dp", "pool"), None, None),
            P(("dp", "pool"), None),
            P("dp", None, None),
            P("dp", None),
            P("dp", None),
            P("dp", "pool", None),
            P("dp", "pool"),
        ),
        out_specs=(
            P(("dp", "pool"), None),
            P(("dp", "pool"), None),
            P(("dp", "pool"), None),
            P("dp", "pool", None),
        ),
        check_vma=False,
    )
```

profile of v0, /device:TPU:34, one launch (start us, length us, event | category | flops | bytes accessed | tf_op | source)
XLA Modules:
  0.0 583.2 jit_solution(11586234165507116891)
XLA Ops:
  4.6 3.5 broadcast_in_dim.164
  8.1 10.6 %all-to-all-start = ((bf16[128,8,3584]{2,1,0:T(8,128)(2,1)}), bf16[128,8,3584]{2,1,0:T(8,128)(2,1)}, u32[]{:S(2)}, u32[]{:S(2)}) async-start(bf16[128,8,3584]{2,1,0:T(8,128)(2,1)} %bitcast.168), calls=%async_computation | async-start | bytes 14680064 | tf_op jit(solution)/shard_map/all_to_all | solution.py:98
  19.5 87.7 %all-to-all-done = bf16[128,8,3584]{2,1,0:T(8,128)(2,1)} async-done(((bf16[128,8,3584]{2,1,0:T(8,128)(2,1)}), bf16[128,8,3584]{2,1,0:T(8,128)(2,1)}, u32[]{:S(2)}, u32[]{:S(2)}) %all-to-all-start) | async-done | bytes 7340064 | tf_op jit(solution)/shard_map/all_to_all | solution.py:98
  109.1 11.7 %all-to-all-start.3 = ((bf16[128,64,128]{2,1,0:T(8,128)(2,1)}), bf16[128,64,128]{2,1,0:T(8,128)(2,1)S(1)}, u32[]{:S(2)}, u32[]{:S(2)}) async-start(bf16[128,64,128]{2,1,0:T(8,128)(2,1)} %bitcast.25), calls=%async_computation.3 | async-start | bytes 4194304 | tf_op jit(solution)/shard_map/all_to_all | solution.py:71
  120.8 9.4 %fusion = f32[1024,512]{1,0:T(8,128)} fusion(bf16[128,8,3584]{2,1,0:T(8,128)(2,1)} %all-to-all-done, bf16[1,3584,512]{2,1,0:T(8,128)(2,1)} %param.21), kind=kOutput, calls=%fused_computation.24 | convolution fusion | flops 3758096384 | bytes 13107200 | tf_op jit(solution)/shard_map/dot_general | solution.py:33
  130.2 14.6 %fusion.12 = bf16[128,8,3584]{2,1,0:T(8,128)(2,1)} fusion(bf16[1,512,3584]{2,1,0:T(8,128)(2,1)} %param.22, f32[1024,512]{1,0:T(8,128)} %fusion, bf16[1,3584,512]{2,1,0:T(8,128)(2,1)} %param.20, bf16[128,8,3584]{2,1,0:T(8,128)(2,1)} %all-to-all-done), kind=kOutput, calls=%fused_computation.36 | convolution fusion | flops 7523008512 | bytes 24117248 | tf_op jit(solution)/shard_map/dot_general | solution.py:35
  144.8 3.5 all-to-all-done.3
  148.3 8.7 %all-to-all-start.1 = ((bf16[128,8,3584]{2,1,0:T(8,128)(2,1)}), bf16[128,8,3584]{2,1,0:T(8,128)(2,1)}, u32[]{:S(2)}, u32[]{:S(2)}) async-start(bf16[128,8,3584]{2,1,0:T(8,128)(2,1)} %fusion.12), calls=%async_computation.1 | async-start | bytes 14680064 | tf_op jit(solution)/shard_map/all_to_all | solution.py:102
  159.9 85.5 %all-to-all-done.1 = bf16[128,8,3584]{2,1,0:T(8,128)(2,1)} async-done(((bf16[128,8,3584]{2,1,0:T(8,128)(2,1)}), bf16[128,8,3584]{2,1,0:T(8,128)(2,1)}, u32[]{:S(2)}, u32[]{:S(2)}) %all-to-all-start.1) | async-done | bytes 7340064 | tf_op jit(solution)/shard_map/all_to_all | solution.py:102
  245.5 7.4 %broadcast_in_dim.168 = bf16[32,4,128,512]{3,2,1,0:T(8,128)(2,1)} broadcast(bf16[32,128,512]{2,1,0:T(8,128)(2,1)} %gather_fusion), dimensions={0,2,3} | broadcast | bytes 20971520 | tf_op jit(solution)/shard_map/broadcast_in_dim | solution.py:63
  252.9 12.6 %all-to-all-start.2 = ((bf16[128,128,512]{2,1,0:T(8,128)(2,1)}), bf16[128,128,512]{2,1,0:T(8,128)(2,1)}, u32[]{:S(2)}, u32[]{:S(2)}) async-start(bf16[128,128,512]{2,1,0:T(8,128)(2,1)} %bitcast.167), calls=%async_computation.2 | async-start | bytes 33554432 | tf_op jit(solution)/shard_map/all_to_all | solution.py:70
  299.5 4.8 convert_reduce_fusion
  306.7 70.6 %all_gather.7 = bf16[64,64]{1,0:T(8,128)(2,1)S(1)} all-gather(bf16[16,64]{1,0:T(8,128)(2,1)S(1)} %pad_maximum_fusion), channel_id=1, replica_groups=mesh['dp'=32,'pool'=4] {'pool'}, dimensions={0}, use_global_device_ids=true | all-gather | bytes 10240 | tf_op jit(solution)/shard_map/all_gather | solution.py:125
  378.1 61.7 %all_gather.6 = bf16[64,512]{1,0:T(8,128)(2,1)S(1)} all-gather(bf16[16,512]{1,0:T(8,128)(2,1)S(1)} %multiply_convert_fusion.1), channel_id=1, replica_groups=mesh['dp'=32,'pool'=4] {'pool'}, dimensions={0}, use_global_device_ids=true | all-gather | bytes 81920 | tf_op jit(solution)/shard_map/all_gather | solution.py:124
  441.3 55.7 %all-to-all-done.2 = bf16[128,128,512]{2,1,0:T(8,128)(2,1)} async-done(((bf16[128,128,512]{2,1,0:T(8,128)(2,1)}), bf16[128,128,512]{2,1,0:T(8,128)(2,1)}, u32[]{:S(2)}, u32[]{:S(2)}) %all-to-all-start.2) | async-done | bytes 16777248 | tf_op jit(solution)/shard_map/all_to_all | solution.py:70
  497.0 8.6 %gather_fusion.1 = bf16[32,128,512]{2,1,0:T(8,128)(2,1)} fusion(bf16[128,128,512]{2,1,0:T(8,128)(2,1)} %all-to-all-done.2, s32[1024]{0:T(1024)} %pad_clamp_fusion.3), kind=kCustom, calls=%fused_computation.1 | custom fusion | bytes 8388736 | tf_op jit(solution)/shard_map/gather | solution.py:156
  505.7 4.6 fusion.161
  517.5 8.6 %gather_fusion.8 = bf16[32,128,512]{2,1,0:T(8,128)(2,1)} fusion(bf16[128,128,512]{2,1,0:T(8,128)(2,1)} %all-to-all-done.2, s32[1024]{0:T(1024)} %pad_clamp_fusion), kind=kCustom, calls=%fused_computation.8 | custom fusion | bytes 8388736 | tf_op jit(solution)/shard_map/gather | solution.py:156
  526.1 4.6 fusion.164
  533.0 3.8 fusion.15
  538.4 8.6 %gather_fusion.4 = bf16[32,128,512]{2,1,0:T(8,128)(2,1)} fusion(bf16[128,128,512]{2,1,0:T(8,128)(2,1)} %all-to-all-done.2, s32[1024]{0:T(1024)} %pad_clamp_fusion.2), kind=kCustom, calls=%fused_computation.4 | custom fusion | bytes 8388736 | tf_op jit(solution)/shard_map/gather | solution.py:156
  547.1 4.6 fusion.162
  559.0 8.6 %gather_fusion.6 = bf16[32,128,512]{2,1,0:T(8,128)(2,1)} fusion(bf16[128,128,512]{2,1,0:T(8,128)(2,1)} %all-to-all-done.2, s32[1024]{0:T(1024)} %pad_clamp_fusion.1), kind=kCustom, calls=%fused_computation.6 | custom fusion | bytes 8388736 | tf_op jit(solution)/shard_map/gather | solution.py:156
  567.7 4.8 fusion.163
  (170 shorter events, 68.9 us)
Async XLA Ops:
  0.6 156.4 %copy-start = (bf16[8,128,512]{2,1,0:T(8,128)(2,1)S(1)}, bf16[8,128,512]{2,1,0:T(8,128)(2,1)}, u32[]{:S(2)}) copy-start(bf16[8,128,512]{2,1,0:T(8,128)(2,1)} %param.26) | copy-start | bytes 3145732
  8.1 10.6 %copy-start.33 = (s32[1,4,32]{2,1,0:T(4,128)S(1)}, s32[1,4,32]{2,1,0:T(4,128)}, u32[]{:S(2)}) copy-start(s32[1,4,32]{2,1,0:T(4,128)} %param.29) | copy-start | bytes 1540
  8.1 10.6 %copy-start.34 = (s32[1,32]{1,0:T(1,128)S(1)}, s32[1,32]{1,0:T(1,128)}, u32[]{:S(2)}) copy-start(s32[1,32]{1,0:T(1,128)} %param.28) | copy-start | bytes 388
  8.1 10.7 %copy-start.13 = (bf16[8,64,128]{2,1,0:T(8,128)(2,1)S(1)}, bf16[8,64,128]{2,1,0:T(8,128)(2,1)}, u32[]{:S(2)}) copy-start(bf16[8,64,128]{2,1,0:T(8,128)(2,1)} %param.27) | copy-start | bytes 393220
  8.1 99.0 %all-to-all-start = ((bf16[128,8,3584]{2,1,0:T(8,128)(2,1)}), bf16[128,8,3584]{2,1,0:T(8,128)(2,1)}, u32[]{:S(2)}, u32[]{:S(2)}) async-start(bf16[128,8,3584]{2,1,0:T(8,128)(2,1)} %bitcast.168), calls=%async_computation | async-start | bytes 14680064 | tf_op jit(solution)/shard_map/all_to_all | solution.py:98
  109.1 39.2 %all-to-all-start.3 = ((bf16[128,64,128]{2,1,0:T(8,128)(2,1)}), bf16[128,64,128]{2,1,0:T(8,128)(2,1)S(1)}, u32[]{:S(2)}, u32[]{:S(2)}) async-start(bf16[128,64,128]{2,1,0:T(8,128)(2,1)} %bitcast.25), calls=%async_computation.3 | async-start | bytes 4194304 | tf_op jit(solution)/shard_map/all_to_all | solution.py:71
  148.3 97.2 %all-to-all-start.1 = ((bf16[128,8,3584]{2,1,0:T(8,128)(2,1)}), bf16[128,8,3584]{2,1,0:T(8,128)(2,1)}, u32[]{:S(2)}, u32[]{:S(2)}) async-start(bf16[128,8,3584]{2,1,0:T(8,128)(2,1)} %fusion.12), calls=%async_computation.1 | async-start | bytes 14680064 | tf_op jit(solution)/shard_map/all_to_all | solution.py:102
  252.9 12.6 %copy-start.27 = (s32[1,4]{1,0:T(1,128)S(1)}, s32[1,4]{1,0:T(1,128)}, u32[]{:S(2)}) copy-start(s32[1,4]{1,0:T(1,128)} %param.31) | copy-start | bytes 52
  252.9 18.6 %copy-start.18 = (bf16[64,1024]{1,0:T(8,128)(2,1)S(1)}, bf16[64,1024]{1,0:T(8,128)(2,1)}, u32[]{:S(2)}) copy-start(bf16[64,1024]{1,0:T(8,128)(2,1)} %param.33) | copy-start | bytes 393220
  252.9 27.2 %copy-start.26 = (s32[1,4]{1,0:T(1,128)S(1)}, s32[1,4]{1,0:T(1,128)}, u32[]{:S(2)}) copy-start(s32[1,4]{1,0:T(1,128)} %param.30) | copy-start | bytes 52
  252.9 244.1 %all-to-all-start.2 = ((bf16[128,128,512]{2,1,0:T(8,128)(2,1)}), bf16[128,128,512]{2,1,0:T(8,128)(2,1)}, u32[]{:S(2)}, u32[]{:S(2)}) async-start(bf16[128,128,512]{2,1,0:T(8,128)(2,1)} %bitcast.167), calls=%async_computation.2 | async-start | bytes 33554432 | tf_op jit(solution)/shard_map/all_to_all | solution.py:70
  299.5 4.9 copy-start.17
  299.5 6.7 %copy-start.16 = (bf16[3584,64]{0,1:T(8,128)(2,1)S(1)}, bf16[3584,64]{0,1:T(8,128)(2,1)}, u32[]{:S(2)}) copy-start(bf16[3584,64]{0,1:T(8,128)(2,1)} %param.24) | copy-start | bytes 1376260
  304.3 72.9 %copy-start.8 = (bf16[3584,512]{1,0:T(8,128)(2,1)S(1)}, bf16[3584,512]{1,0:T(8,128)(2,1)}, u32[]{:S(2)}) copy-start(bf16[3584,512]{1,0:T(8,128)(2,1)} %param.23) | copy-start | bytes 11010052
  304.4 73.6 %copy-start.32 = (f32[512]{0:T(512)S(1)}, f32[512]{0:T(512)}, u32[]{:S(2)}) copy-start(f32[512]{0:T(512)} %param.25) | copy-start | bytes 6148
  304.4 135.8 %copy-start.7 = (bf16[32,16,512]{2,1,0:T(8,128)(2,1)S(1)}, bf16[32,16,512]{2,1,0:T(8,128)(2,1)}, u32[]{:S(2)}) copy-start(bf16[32,16,512]{2,1,0:T(8,128)(2,1)} %get-tuple-element.17) | copy-start | bytes 1572868
  306.2 199.4 %copy-start.14 = (bf16[16,3584]{1,0:T(8,128)(2,1)}, bf16[16,3584]{1,0:T(8,128)(2,1)S(1)}, u32[]{:S(2)}) copy-start(bf16[16,3584]{1,0:T(8,128)(2,1)S(1)} %fusion.14) | copy-start | bytes 344068
  306.2 134.4 %copy-start.6 = (bf16[32,16,512]{2,1,0:T(8,128)(2,1)S(1)}, bf16[32,16,512]{2,1,0:T(8,128)(2,1)}, u32[]{:S(2)}) copy-start(bf16[32,16,512]{2,1,0:T(8,128)(2,1)} %get-tuple-element.16) | copy-start | bytes 1572868
  306.2 134.6 %copy-start.24 = (s32[512]{0:T(512)S(1)}, s32[512]{0:T(512)}, u32[]{:S(2)}) copy-start(s32[512]{0:T(512)} %add_select_fusion) | copy-start | bytes 6148
  306.3 134.6 %copy-start.28 = (pred[32]{0:T(512)(128)(4,1)S(1)}, pred[32]{0:T(512)(128)(4,1)}, u32[]{:S(2)}) copy-start(pred[32]{0:T(512)(128)(4,1)} %get-tuple-element.54) | copy-start | bytes 100
  306.3 134.6 %copy-start.29 = (pred[32]{0:T(512)(128)(4,1)S(1)}, pred[32]{0:T(512)(128)(4,1)}, u32[]{:S(2)}) copy-start(pred[32]{0:T(512)(128)(4,1)} %get-tuple-element.53) | copy-start | bytes 100
  306.7 198.9 %copy-start.25 = (bf16[16,64]{1,0:T(8,128)(2,1)}, bf16[16,64]{1,0:T(8,128)(2,1)S(1)}, u32[]{:S(2)}) copy-start(bf16[16,64]{1,0:T(8,128)(2,1)S(1)} %pad_maximum_fusion) | copy-start | bytes 6148
  378.1 127.6 %copy-start.19 = (bf16[16,512]{1,0:T(8,128)(2,1)}, bf16[16,512]{1,0:T(8,128)(2,1)S(1)}, u32[]{:S(2)}) copy-start(bf16[16,512]{1,0:T(8,128)(2,1)S(1)} %multiply_convert_fusion.1) | copy-start | bytes 49156
  567.7 4.8 copy-start.20
  (20 other events, 57.0 us)
where the time goes:
time: 591 us; the launch traced here: 583 us
  waiting for transfers between devices  232 us (39%)
  blocking collectives  132 us (22%)
  local copies, waits for them, and re-layouts  69.5 us (12%)
  matrix products  69.5 us (12%)
  starting transfers between devices  43.6 us (7%)
  other arithmetic  26.7 us (5%)
  between operations  9.27 us (2%)
    all_to_all x1, waiting for transfers between devices, shards(): lax.all_to_all(spread, ('dp', 'pool'), split_axis=0, concat_axis=0, tiled...  87.7 us
    all_to_all x1, waiting for transfers between devices, shards(): lax.all_to_all(partial_value, ('dp', 'pool'), split_axis=0, concat_axis=0...  85.5 us
    all_gather x1, blocking collectives, shards(): lax.all_gather(new_rope, 'pool', axis=0, tiled=True)  70.6 us
    all_gather x1, blocking collectives, shards(): lax.all_gather(new_latent, 'pool', axis=0, tiled=True)  61.7 us
    all_to_all x1, waiting for transfers between devices, shards(): lax.all_to_all(copies_latent, ('dp', 'pool'), split_axis=0, concat_axis=0...  55.7 us
    gather x4, local copies, waits for them, and re-layouts, shards(): keys_latent = held_latent[place].reshape(key_count, lat_width)  34.5 us
    dot_general x4, matrix products, shards(): lax.dot_general(asks_latent, keys_latent, contract, preferred_element_typ...  18.6 us
    dot_general x1, matrix products, expert_rows(): jnp.dot(activated, down_matrix, preferred_element_type=jnp.float32)  14.6 us
  transfers between devices with their start and end apart: 4, of which 4 were waited for; matrix products, arithmetic and copies ran while one was open for 11% of the time, Pallas kernels for 0%

commit v1 on v0

v1 whole, which is shorter than its diff:
```python
import functools

import jax
import jax.numpy as jnp
from jax import lax
from jax.experimental import pallas as pl
from jax.experimental.pallas import tpu as pltpu
from jax.sharding import Mesh
from jax.sharding import PartitionSpec as P

SCORE_SCALE = 192.0 ** (-0.5)
LOG2E = 1.4426950408889634
ROPE_BASE = 10000.0
NORM_EPS = 1e-06
BIG = -1e30

N_DP = 32
CHATS = 4
MAXB = 32
BLOCK = 128
LAT = 512
ROPE = 64
TOK = 64
HEADS_DEV = 16
GROUP = 2
TILE = 16
SLOTS = 2 * N_DP + CHATS * (GROUP - 1) + 2


def rotate(values, positions):
    half = values.shape[-1] // 2
    exponent = jnp.arange(half).astype(jnp.float32) * (-2.0 / values.shape[-1])
    frequency = jnp.power(jnp.float32(ROPE_BASE), exponent)
    angle = positions.astype(jnp.float32)[:, None] * frequency[None, :]
    first = values[:, :half]
    second = values[:, half:]
    cosine = jnp.cos(angle)
    sine = jnp.sin(angle)
    return jnp.concatenate([first * cosine - second * sine, second * cosine + first * sine], axis=1)


def chat_positions(counts, lengths, local):
    ends = jnp.cumsum(counts)
    chat_of = jnp.sum((local[:, None] >= ends[None, :]).astype(jnp.int32), axis=1)
    starts = ends - counts
    onehot = (chat_of[:, None] == jnp.arange(counts.shape[0])[None, :]).astype(jnp.int32)
    return jnp.sum(onehot * (lengths - starts)[None, :], axis=1) + local


def attend_kernel(
    table, lengths, counts, where, own_kv, sib_kv, q_own, q_par, r_own, r_par,
    o_own, o_par, s_own, s_par, held, place, sems,
):
    zh, core = where[0], where[1]
    heads = q_own.shape[1]
    rows = TILE * heads

    def copy_in(ref, source, slot):
        return pltpu.make_async_copy(ref.at[source], held.at[slot], sems.at[slot])

    def fetch(holder, slot):
        source = lax.shift_right_logical(holder, 2)

        @pl.when((holder & 1) == core)
        def _():
            copy_in(own_kv, source, slot).start()

        @pl.when((holder & 1) != core)
        def _():
            copy_in(sib_kv, source, slot).start()

    begins, ends = [], []
    slot = jnp.int32(0)
    for chat in range(CHATS):
        length = lengths[0, chat]
        begins.append(slot)

        def step(j, carry):
            slot, last = carry
            holder = table[0, chat * MAXB + j]
            mine = (j * BLOCK < length) & ((lax.shift_right_logical(holder, 1) & 1) == zh)

            @pl.when(mine)
            def _():
                place[slot] = jnp.clip(length - j * BLOCK, 0, BLOCK)
                fetch(holder, slot)

            return jnp.where(mine, slot + 1, slot), jnp.where(mine, holder, last)

        slot, last = lax.fori_loop(0, MAXB, step, (slot, jnp.int32(0)))
        pad = lax.rem(GROUP - lax.rem(slot, GROUP), GROUP)

        def fill(i, carry):
            place[carry] = 0
            fetch(last, carry)
            return carry + 1

        slot = lax.fori_loop(0, pad, fill, slot)
        ends.append(slot)
    total_slots = slot

    def arrive(i, carry):
        copy_in(own_kv, 0, i).wait()
        return carry

    start = jnp.int32(0)
    arrived = jnp.int32(0)
    lane = lax.broadcasted_iota(jnp.int32, (1, BLOCK), 1)
    contract = (((1,), (1,)), ((), ()))
    for chat in range(CHATS):
        count = counts[0, chat]
        first_group = lax.div(begins[chat], GROUP)
        n_groups = lax.div(ends[chat] - begins[chat], GROUP)
        lax.fori_loop(begins[chat], ends[chat], arrive, 0)

        def tile(t, carry):
            base = jnp.minimum(start + t * TILE, TOK - TILE)
            queries = [
                (q[pl.ds(base, TILE)].reshape(rows, LAT), r[pl.ds(base, TILE)].reshape(rows, ROPE))
                for q, r in ((q_own, r_own), (q_par, r_par))
            ]

            def group(g, state):
                at = (first_group + g) * GROUP
                blocks = [held[at + i] for i in range(GROUP)]
                keys = jnp.concatenate([b[:BLOCK] for b in blocks], axis=0)
                ropes = jnp.concatenate(
                    [
                        jnp.concatenate(
                            [b[BLOCK:, k * BLOCK : (k + 1) * BLOCK] for k in range(LAT // BLOCK)],
                            axis=0,
                        )
                        for b in blocks
                    ],
                    axis=1,
                )
                valid = jnp.concatenate([lane < place[at + i] for i in range(GROUP)], axis=1)
                new = []
                for (ql, qr), (m, l, acc) in zip(queries, state):
                    s = lax.dot_general(ql, keys, contract, preferred_element_type=jnp.float32)
                    s = s + jnp.dot(qr, ropes, preferred_element_type=jnp.float32)
                    s = jnp.where(valid, s * (SCORE_SCALE * LOG2E), BIG)
                    m_new = jnp.maximum(m, jnp.max(s, axis=1, keepdims=True))
                    p = jnp.exp2(s - m_new)
                    alpha = jnp.exp2(m - m_new)
                    l = l * alpha + jnp.sum(p, axis=1, keepdims=True)
                    acc = acc * alpha + jnp.dot(
                        p.astype(jnp.bfloat16), keys, preferred_element_type=jnp.float32
                    )
                    new.append((m_new, l, acc))
                return tuple(new)

            empty = (
                jnp.full((rows, 1), BIG, jnp.float32),
                jnp.zeros((rows, 1), jnp.float32),
                jnp.zeros((rows, LAT), jnp.float32),
            )
            state = lax.fori_loop(0, n_groups, group, (empty, empty))
            token = base + lax.broadcasted_iota(jnp.int32, (TILE, 1, 1), 0)
            keep = (token >= start) & (token < start + count)
            for (m, l, acc), o, s in zip(state, (o_own, o_par), (s_own, s_par)):
                some = l > 0.0
                safe = jnp.where(some, l, 1.0)
                value = (acc / safe).astype(jnp.bfloat16).reshape(TILE, heads, LAT)
                lse = jnp.where(some, m + jnp.log2(safe), BIG)
                lse = jnp.broadcast_to(lse, (rows, BLOCK)).reshape(TILE, heads, BLOCK)
                o[pl.ds(base, TILE)] = jnp.where(keep, value, o[pl.ds(base, TILE)])
                s[pl.ds(base, TILE)] = jnp.where(keep, lse, s[pl.ds(base, TILE)])
            return carry

        lax.fori_loop(0, lax.div(count + TILE - 1, TILE), tile, 0)
        start = start + count


def attend(table, lengths, counts, where, own_kv, sib_kv, q_own, q_par, r_own, r_par):
    smem = pl.BlockSpec(memory_space=pltpu.SMEM)
    vmem = pl.BlockSpec(memory_space=pltpu.VMEM)
    hbm = pl.BlockSpec(memory_space=pl.ANY)
    tok, heads, width = q_own.shape
    out = jax.ShapeDtypeStruct((tok, heads, width), jnp.bfloat16)
    stat = jax.ShapeDtypeStruct((tok, heads, BLOCK), jnp.float32)
    return pl.pallas_call(
        attend_kernel,
        out_shape=(out, out, stat, stat),
        in_specs=[smem] * 4 + [hbm] * 2 + [vmem] * 4,
        out_specs=(vmem,) * 4,
        scratch_shapes=[
            pltpu.VMEM((SLOTS,) + own_kv.shape[1:], jnp.bfloat16),
            pltpu.SMEM((SLOTS,), jnp.int32),
            pltpu.SemaphoreType.DMA((SLOTS,)),
        ],
        compiler_params=pltpu.CompilerParams(vmem_limit_bytes=48 * 2**20),
        cost_estimate=pl.CostEstimate(
            flops=9 * 10**9, bytes_accessed=12 * 2**20, transcendentals=4 * 2**20
        ),
        name="attend",
    )(table, lengths, counts, where, own_kv, sib_kv, q_own, q_par, r_own, r_par)


def finish_kernel(q_ref, r_ref, fresh_ref, fresh_rope_ref, ok_ref, oa, ob, sa, sb, out_ref):
    heads = q_ref.shape[1]
    contract = (((1,), (1,)), ((), ()))
    fresh = fresh_ref[...]
    fresh_rope = fresh_rope_ref[...]

    def tile(t, carry):
        at = pl.ds(t * TILE, TILE)
        rows = TILE * heads
        s = lax.dot_general(
            q_ref[at].reshape(rows, LAT), fresh, contract, preferred_element_type=jnp.float32
        ) + lax.dot_general(
            r_ref[at].reshape(rows, ROPE), fresh_rope, contract, preferred_element_type=jnp.float32
        )
        ok = ok_ref[at]
        ok = jnp.broadcast_to(ok[:, None, :], (TILE, heads, TOK)).reshape(rows, TOK)
        s = jnp.where(ok > 0.0, s * (SCORE_SCALE * LOG2E), BIG)
        la = sa[at].reshape(rows, BLOCK)[:, :1]
        lb = sb[at].reshape(rows, BLOCK)[:, :1]
        m = jnp.maximum(jnp.maximum(la, lb), jnp.max(s, axis=1, keepdims=True))
        p = jnp.where(ok > 0.0, jnp.exp2(s - m), 0.0)
        wa = jnp.exp2(la - m)
        wb = jnp.exp2(lb - m)
        total = wa + wb + jnp.sum(p, axis=1, keepdims=True)
        mixed = jnp.dot(p.astype(jnp.bfloat16), fresh, preferred_element_type=jnp.float32)
        mixed = mixed + wa * oa[at].reshape(rows, LAT).astype(jnp.float32)
        mixed = mixed + wb * ob[at].reshape(rows, LAT).astype(jnp.float32)
        out_ref[at] = (mixed / total).astype(jnp.bfloat16).reshape(TILE, heads, LAT)
        return carry

    lax.fori_loop(0, TOK // TILE, tile, 0)


def finish(q_own, r_own, fresh, fresh_rope, ok, oa, ob, sa, sb):
    vmem = pl.BlockSpec(memory_space=pltpu.VMEM)
    return pl.pallas_call(
        finish_kernel,
        out_shape=jax.ShapeDtypeStruct(q_own.shape, jnp.bfloat16),
        in_specs=[vmem] * 9,
        out_specs=vmem,
        compiler_params=pltpu.CompilerParams(vmem_limit_bytes=32 * 2**20),
        name="finish",
    )(q_own, r_own, fresh, fresh_rope, ok, oa, ob, sa, sb)


def swap(value, axis):
    return lax.ppermute(value, axis, [(0, 1), (1, 0)])


def expert_rows(flat_rows, gate_matrix, up_matrix, down_matrix):
    gate = jnp.dot(flat_rows, gate_matrix, preferred_element_type=jnp.float32)
    lifted = jnp.dot(flat_rows, up_matrix, preferred_element_type=jnp.float32)
    activated = (jax.nn.silu(gate) * lifted).astype(jnp.bfloat16)
    return jnp.dot(activated, down_matrix, preferred_element_type=jnp.float32).astype(jnp.bfloat16)


def shards(
    hidden_in,
    expert_ids,
    gate_vals,
    w_gate,
    w_up,
    w_down,
    w_latent,
    w_rope,
    latent_gain,
    cache_latent,
    cache_rope,
    send_index,
    block_table,
    cached_len,
    new_counts,
    q_latent,
    q_rope,
):
    zh, core = lax.axis_index("zh"), lax.axis_index("core")
    rows, width = hidden_in.shape
    fan_count = expert_ids.shape[1]
    capacity = rows // 2
    slots = N_DP * capacity

    flat_ids = expert_ids.reshape(-1)
    onehot = (flat_ids[:, None] == jnp.arange(N_DP)[None, :]).astype(jnp.int32)
    before = jnp.cumsum(onehot, axis=0) - onehot
    target = flat_ids * capacity + jnp.sum(before * onehot, axis=1)
    match = (target[:, None] == jnp.arange(slots)[None, :]).astype(jnp.float32)
    picks = jnp.sum(match.reshape(rows, fan_count, slots), axis=1)
    weights = jnp.sum(
        (match * gate_vals.reshape(-1)[:, None]).reshape(rows, fan_count, slots), axis=1
    )
    outgoing = lax.dot_general(
        picks.astype(jnp.bfloat16),
        hidden_in,
        (((0,), (0,)), ((), ())),
        preferred_element_type=jnp.float32,
    ).astype(jnp.bfloat16)
    spread = jnp.broadcast_to(
        outgoing.reshape(N_DP, 1, capacity, width), (N_DP, 2, capacity, width)
    ).reshape(N_DP * 2, capacity, width)
    arrived = lax.all_to_all(spread, ("dp", "zh"), split_axis=0, concat_axis=0, tiled=True)
    arrived = arrived.reshape(-1, width)
    arrived_sib = swap(arrived, "core")

    packed = jnp.concatenate(
        [cache_rope[:, 16 * k : 16 * (k + 1), :] for k in range(LAT // BLOCK)], axis=2
    )
    blocks = jnp.concatenate([cache_latent, packed], axis=1)[send_index[0]]
    own_kv = lax.all_to_all(blocks, "dp", split_axis=0, concat_axis=0, tiled=True)
    sib_kv = swap(own_kv, "core")
    r_own = q_rope.reshape(TOK, HEADS_DEV, ROPE)
    q_par = swap(q_latent, "zh")
    r_par = swap(q_rope, "zh").reshape(TOK, HEADS_DEV, ROPE)

    matrices = (w_gate[0], w_up[0], w_down[0])
    theirs = expert_rows(arrived_sib, *matrices)
    mine = expert_rows(arrived, *matrices)
    partial = (mine.astype(jnp.float32) + swap(theirs, "core").astype(jnp.float32)).astype(
        jnp.bfloat16
    )
    returned = lax.all_to_all(
        partial.reshape(N_DP * 2, capacity, width),
        ("dp", "zh"),
        split_axis=0,
        concat_axis=0,
        tiled=True,
    )
    summed = jnp.sum(
        returned.reshape(N_DP, 2, capacity, width), axis=1, dtype=jnp.float32
    ).reshape(slots, width)
    mixed = jnp.dot(
        weights,
        summed,
        precision=lax.Precision.HIGHEST,
        preferred_element_type=jnp.float32,
    )
    hidden_out = (hidden_in.astype(jnp.float32) + mixed).astype(jnp.bfloat16)
    latent = jnp.dot(hidden_out, w_latent, preferred_element_type=jnp.float32)
    norm_scale = lax.rsqrt(jnp.mean(latent * latent, axis=1, keepdims=True) + NORM_EPS)
    new_latent = (latent * norm_scale * latent_gain[None, :]).astype(jnp.bfloat16)
    counts = new_counts[0]
    pool = zh * 2 + core
    local = pool * rows + jnp.arange(rows, dtype=jnp.int32)
    positions = chat_positions(counts, cached_len[0], local)
    new_rope = rotate(
        jnp.dot(hidden_out, w_rope, preferred_element_type=jnp.float32), positions
    ).astype(jnp.bfloat16)

    fresh = jnp.concatenate([new_latent, new_rope], axis=1)
    pair = jnp.stack([fresh, swap(fresh, "core")])
    pair = jnp.where(core == 0, pair, pair[::-1])
    quad = jnp.stack([pair, swap(pair, "zh")])
    quad = jnp.where(zh == 0, quad, quad[::-1]).reshape(TOK, LAT + ROPE)

    where = jnp.stack([zh, core]).astype(jnp.int32)
    o_own, o_par, s_own, s_par = attend(
        block_table.reshape(1, CHATS * MAXB),
        cached_len,
        new_counts,
        where,
        own_kv,
        sib_kv,
        q_latent,
        q_par,
        r_own,
        r_par,
    )
    o_back = swap(o_par, "zh")
    s_back = swap(s_par[:, :, 0], "zh")
    s_back = jnp.broadcast_to(s_back[:, :, None], s_own.shape)
    tokens = jnp.arange(TOK, dtype=jnp.int32)
    ends = jnp.cumsum(counts)
    chat_of = jnp.sum((tokens[:, None] >= ends[None, :]).astype(jnp.int32), axis=1)
    ok = (chat_of[:, None] == chat_of[None, :]) & (tokens[None, :] <= tokens[:, None])
    context = finish(
        q_latent,
        r_own,
        quad[:, :LAT],
        quad[:, LAT:],
        ok.astype(jnp.float32),
        o_own,
        o_back,
        s_own,
        s_back,
    )
    return (hidden_out, new_latent, new_rope, context)


def solution(mesh):
    whole = Mesh(mesh.devices.reshape(N_DP, 2, 2), ("dp", "zh", "core"))
    every = ("dp", "zh", "core")
    pool = ("zh", "core")
    return jax.shard_map(
        shards,
        mesh=whole,
        in_specs=(
            P(every, None),
            P(every, None),
            P(every, None),
            P("dp", None, pool),
            P("dp", None, pool),
            P("dp", pool, None),
            P(),
            P(),
            P(),
            P(every, None, None),
            P(every, None, None),
            P(every, None),
            P("dp", None, None),
            P("dp", None),
            P("dp", None),
            P("dp", pool, None),
            P("dp", pool),
        ),
        out_specs=(
            P(every, None),
            P(every, None),
            P(every, None),
            P("dp", pool, None),
        ),
        check_vma=False,
    )
```

time: 591 us -> 338 us (0.57)
  the two profiles are of different devices: /device:TPU:34 before, /device:TPU:23 now
where the time goes in v1:
time: 338 us; the launch traced here: 334 us
  waiting for transfers between devices  133 us (39%)
  Pallas kernels  56.6 us (17%)
  blocking collectives  52.6 us (16%)
  starting transfers between devices  36.6 us (11%)
  matrix products  35.9 us (11%)
  local copies, waits for them, and re-layouts  11.9 us (4%)
  other arithmetic  5.69 us (2%)
    ppermute x9, waiting for transfers between devices, swap(): return lax.ppermute(value, axis, [(0, 1), (1, 0)])  79.9 us
    all_to_all x1, waiting for transfers between devices, shards(): lax.all_to_all(blocks, 'dp', split_axis=0, concat_axis=0, tiled=True)  53.3 us
    all_to_all x1, blocking collectives, shards(): lax.all_to_all(spread, ('dp', 'zh'), split_axis=0, concat_axis=0, tiled=T...  52.6 us
    pallas_call x1, Pallas kernels, attend(): pl.pallas_call(attend_kernel, out_shape=(out, out, stat, stat), in_specs=...  51.8 us
    dot_general x2, matrix products, expert_rows(): jnp.dot(activated, down_matrix, preferred_element_type=jnp.float32)  21.2 us
    ppermute x9, starting transfers between devices, swap(): return lax.ppermute(value, axis, [(0, 1), (1, 0)])  16.6 us
    all_to_all x1, starting transfers between devices, shards(): lax.all_to_all(partial.reshape(N_DP * 2, capacity, width), ('dp', 'zh'),...  11.2 us
    all_to_all x1, starting transfers between devices, shards(): lax.all_to_all(blocks, 'dp', split_axis=0, concat_axis=0, tiled=True)  8.75 us
  transfers between devices with their start and end apart: 11, of which 5 were waited for; matrix products, arithmetic and copies ran while one was open for 13% of the time, Pallas kernels for 16%

profile of v1, /device:TPU:23, one launch (start us, length us, event | category | flops | bytes accessed | tf_op | source)
XLA Modules:
  0.0 333.5 jit_solution(15394687505500540201)
XLA Ops:
  3.0 1.6 fusion.1
  4.9 52.6 %all_to_all.15 = bf16[64,8,3584]{2,1,0:T(8,128)(2,1)} all-to-all(bf16[64,8,3584]{2,1,0:T(8,128)(2,1)S(1)} %bitcast.78), channel_id=1, replica_groups=mesh['dp'=32,'zh'=2,'core'=2] {'dp','zh'}, dimensions={0} | all-to-all | bytes 7340032 | tf_op jit(solution)/shard_map/all_to_all | solution.py:299
  57.5 2.1 collective-permute-start
  59.8 3.0 gather_fusion
  62.9 8.8 %all-to-all-start.2 = ((bf16[32,144,512]{2,1,0:T(8,128)(2,1)}), bf16[32,144,512]{2,1,0:T(8,128)(2,1)}, u32[]{:S(2)}, u32[]{:S(2)}) async-start(bf16[32,144,512]{2,1,0:T(8,128)(2,1)} %gather_fusion), calls=%async_computation.2 | async-start | bytes 9437184 | tf_op jit(solution)/shard_map/all_to_all | solution.py:307
  71.6 5.2 %fusion.6 = f32[512,512]{1,0:T(8,128)S(1)} fusion(bf16[512,3584]{1,0:T(8,128)(2,1)} %collective-permute-done, bf16[1,3584,512]{2,1,0:T(8,128)(2,1)} %param.21), kind=kOutput, calls=%fused_computation.13 | convolution fusion | flops 1879048192 | bytes 8388608 | tf_op jit(solution)/shard_map/dot_general | solution.py:251
  76.8 10.1 %convolution_convert_fusion = bf16[512,3584]{1,0:T(8,128)(2,1)} fusion(bf16[1,512,3584]{2,1,0:T(8,128)(2,1)} %param.22, f32[512,512]{1,0:T(8,128)S(1)} %fusion.6, bf16[512,3584]{1,0:T(8,128)(2,1)} %collective-permute-done, bf16[1,3584,512]{2,1,0:T(8,128)(2,1)} %param.20), kind=kOutput, calls=%fused_computation.3 | convolution fusion | flops 3761504256 | bytes 15728640 | tf_op jit(solution)/shard_map/dot_general | solution.py:253
  87.2 53.3 %all-to-all-done.2.own_kv = bf16[32,144,512]{2,1,0:T(8,128)(2,1)} async-done(((bf16[32,144,512]{2,1,0:T(8,128)(2,1)}), bf16[32,144,512]{2,1,0:T(8,128)(2,1)}, u32[]{:S(2)}, u32[]{:S(2)}) %all-to-all-start.2) | async-done | bytes 4718624 | tf_op jit(solution)/shard_map/all_to_all | solution.py:307
  140.5 1.1 collective-permute-start.4
  141.6 5.2 %fusion.12 = f32[512,512]{1,0:T(8,128)S(1)} fusion(bf16[1,3584,512]{2,1,0:T(8,128)(2,1)} %param.20, bf16[64,8,3584]{2,1,0:T(8,128)(2,1)} %all_to_all.15), kind=kOutput, calls=%fused_computation.19 | convolution fusion | flops 1879048192 | bytes 8388608 | tf_op jit(solution)/shard_map/dot_general | solution.py:250
  146.8 11.1 %fusion = bf16[64,8,3584]{2,1,0:T(8,128)(2,1)} fusion(bf16[512,3584]{1,0:T(8,128)(2,1)} %collective-permute-done.1, bf16[1,512,3584]{2,1,0:T(8,128)(2,1)} %param.22, bf16[1,3584,512]{2,1,0:T(8,128)(2,1)} %param.21, f32[512,512]{1,0:T(8,128)S(1)} %fusion.12, bf16[64,8,3584]{2,1,0:T(8,128)(2,1)} %all_to_all.15), kind=kOutput, calls=%fused_computation.6 | convolution fusion | flops 3768844288 | bytes 19398656 | tf_op jit(solution)/shard_map/dot_general | solution.py:253
  157.9 11.2 %all-to-all-start.1 = ((bf16[64,8,3584]{2,1,0:T(8,128)(2,1)}), bf16[64,8,3584]{2,1,0:T(8,128)(2,1)}, u32[]{:S(2)}, u32[]{:S(2)}) async-start(bf16[64,8,3584]{2,1,0:T(8,128)(2,1)} %fusion), calls=%async_computation.1 | async-start | bytes 7340032 | tf_op jit(solution)/shard_map/all_to_all | solution.py:319
  169.2 2.8 collective-permute-start.5
  173.1 65.7 %collective-permute-done.6 = bf16[64,1024]{1,0:T(8,128)(2,1)S(1)} collective-permute-done((bf16[64,1024]{1,0:T(8,128)(2,1)S(1)}, bf16[64,1024]{1,0:T(8,128)(2,1)S(1)}, u32[]{:S(2)}, u32[]{:S(2)}) %collective-permute-start.6) | collective-permute-done | bytes 131104 | tf_op jit(solution)/shard_map/ppermute | solution.py:246
  239.7 1.0 copy-done.8
  241.6 1.2 copy-done.9
  242.9 51.8 %attend.1 = (bf16[64,16,512]{2,1,0:T(8,128)(2,1)S(1)}, bf16[64,16,512]{2,1,0:T(8,128)(2,1)S(1)}, f32[64,16,128]{2,1,0:T(8,128)S(1)}, f32[64,16,128]{2,1,0:T(8,128)S(1)}) custom-call(s32[1,128]{1,0:T(1,128)S(1)} %reshape.146.table, s32[1,4]{1,0:T(1,128)S(1)} %copy-done.5, s32[1,4]{1,0:T(1,128)S(1)} %copy-done.6, s32[2]{0:T(128)S(1)} %pad_add_fusion.where, ...), custom_call_target="tpu_custom_call" | custom-call | flops 8999999488 | bytes 12582912 | tf_op jit(solution)/shard_map/attend/pallas_call | solution.py:182
  296.7 5.2 %collective-permute-start.8 = (f32[64,16]{0,1:T(8,128)S(1)}, f32[64,16]{0,1:T(8,128)S(1)}, u32[]{:S(2)}, u32[]{:S(2)}) collective-permute-start(f32[64,16]{0,1:T(8,128)S(1)} %bitcast.83), channel_id=1, source_target_pairs={{0,2},{2,0},{1,3},{3,1},{4,6},{6,4},{5,7},{7,5},{8,10},{10,8},{9,1... | collective-permute-start | bytes 12296 | tf_op jit(solution)/shard_map/ppermute | solution.py:246
  303.1 3.2 convert_reduce_fusion
  306.3 1.8 fusion.2
  309.7 1.4 collective-permute-start.2
  312.0 3.4 %collective-permute-start.3 = (bf16[2,16,576]{2,1,0:T(8,128)(2,1)S(1)}, bf16[2,16,576]{2,1,0:T(8,128)(2,1)S(1)}, u32[]{:S(2)}, u32[]{:S(2)}) collective-permute-start(bf16[2,16,576]{2,1,0:T(8,128)(2,1)S(1)} %reverse_select_fusion.1), channel_id=1, source_target_pairs={{0,2},{2,0},{1,3},{3,1},{4,6},{6,4},{5,7},{7,5},{8,10},{10,8},{9,1... | collective-permute-start | bytes 110600 | tf_op jit(solution)/shard_map/ppermute | solution.py:246
  315.4 13.1 %collective-permute-done.3 = bf16[2,16,576]{2,1,0:T(8,128)(2,1)S(1)} collective-permute-done((bf16[2,16,576]{2,1,0:T(8,128)(2,1)S(1)}, bf16[2,16,576]{2,1,0:T(8,128)(2,1)S(1)}, u32[]{:S(2)}, u32[]{:S(2)}) %collective-permute-start.3) | collective-permute-done | bytes 36896 | tf_op jit(solution)/shard_map/ppermute | solution.py:246
  328.8 4.8 %finish.1 = bf16[64,16,512]{2,1,0:T(8,128)(2,1)} custom-call(bf16[64,16,512]{2,1,0:T(8,128)(2,1)S(1)} %copy-done.1, bf16[64,16,64]{2,1,0:T(8,128)(2,1)S(1)} %reshape.144.r_own.r_ref, bf16[64,512]{1,0:T(8,128)(2,1)S(1)} %slice.40.fresh_ref, bf16[64,64]{1,0:T(8,128)(2,1)S(1)} %slice.41.fresh_rope_ref, f32[64,64]{1,0:T(8,128)S(1)} %fusion.30.ok_ref, ...), custom_call_target="tpu_custom_call" | custom-call | tf_op jit(solution)/shard_map/finish/pallas_call | solution.py:235
  (94 shorter events, 11.9 us)
Async XLA Ops:
  0.6 308.4 %copy-start = (bf16[3584,64]{0,1:T(8,128)(2,1)S(1)}, bf16[3584,64]{0,1:T(8,128)(2,1)}, u32[]{:S(2)}) copy-start(bf16[3584,64]{0,1:T(8,128)(2,1)} %param.24) | copy-start | bytes 1376260
  4.9 54.8 %copy-start.19 = (s32[1,32]{1,0:T(1,128)S(1)}, s32[1,32]{1,0:T(1,128)}, u32[]{:S(2)}) copy-start(s32[1,32]{1,0:T(1,128)} %param.28) | copy-start | bytes 388
  4.9 54.8 %copy-start.16 = (bf16[8,64,128]{2,1,0:T(8,128)(2,1)S(1)}, bf16[8,64,128]{2,1,0:T(8,128)(2,1)}, u32[]{:S(2)}) copy-start(bf16[8,64,128]{2,1,0:T(8,128)(2,1)} %param.27) | copy-start | bytes 393220
  4.9 54.8 %copy-start.11 = (bf16[8,128,512]{2,1,0:T(8,128)(2,1)S(1)}, bf16[8,128,512]{2,1,0:T(8,128)(2,1)}, u32[]{:S(2)}) copy-start(bf16[8,128,512]{2,1,0:T(8,128)(2,1)} %param.26) | copy-start | bytes 3145732
  57.5 14.1 %collective-permute-start = (bf16[512,3584]{1,0:T(8,128)(2,1)}, bf16[512,3584]{1,0:T(8,128)(2,1)}, u32[]{:S(2)}, u32[]{:S(2)}) collective-permute-start(bf16[512,3584]{1,0:T(8,128)(2,1)} %bitcast.2), channel_id=1, source_target_pairs={{0,1},{1,0},{2,3},{3,2},{4,5},{5,4},{6,7},{7,6},{8,9},{9,8},{10,11... | collective-permute-start | bytes 11010056 | tf_op jit(solution)/shard_map/ppermute | solution.py:246
  62.9 77.7 %all-to-all-start.2 = ((bf16[32,144,512]{2,1,0:T(8,128)(2,1)}), bf16[32,144,512]{2,1,0:T(8,128)(2,1)}, u32[]{:S(2)}, u32[]{:S(2)}) async-start(bf16[32,144,512]{2,1,0:T(8,128)(2,1)} %gather_fusion), calls=%async_computation.2 | async-start | bytes 9437184 | tf_op jit(solution)/shard_map/all_to_all | solution.py:307
  86.9 59.9 %collective-permute-start.1 = (bf16[512,3584]{1,0:T(8,128)(2,1)}, bf16[512,3584]{1,0:T(8,128)(2,1)}, u32[]{:S(2)}, u32[]{:S(2)}) collective-permute-start(bf16[512,3584]{1,0:T(8,128)(2,1)} %convolution_convert_fusion), channel_id=1, source_target_pairs={{0,1},{1,0},{2,3},{3,2},{4,5},{5,4},{6,7},{7,6},{8,9},{9,8},{10,11... | collective-permute-start | bytes 11010056 | tf_op jit(solution)/shard_map/ppermute | solution.py:246
  140.5 100.2 %collective-permute-start.4 = (bf16[32,144,512]{2,1,0:T(8,128)(2,1)}, bf16[32,144,512]{2,1,0:T(8,128)(2,1)}, u32[]{:S(2)}, u32[]{:S(2)}) collective-permute-start(bf16[32,144,512]{2,1,0:T(8,128)(2,1)} %all-to-all-done.2.own_kv), channel_id=1, source_target_pairs={{0,1},{1,0},{2,3},{3,2},{4,5},{5,4},{6,7},{7,6},{8,9},{9,8},{10,11... | collective-permute-start | bytes 14155784 | tf_op jit(solution)/shard_map/ppermute | solution.py:246
  157.9 11.3 %copy-start.1 = (bf16[64,16,512]{2,1,0:T(8,128)(2,1)S(1)}, bf16[64,16,512]{2,1,0:T(8,128)(2,1)}, u32[]{:S(2)}) copy-start(bf16[64,16,512]{2,1,0:T(8,128)(2,1)} %q_ref.1) | copy-start | bytes 3145732
  157.9 14.1 %copy-start.15 = (bf16[64,1024]{1,0:T(8,128)(2,1)S(1)}, bf16[64,1024]{1,0:T(8,128)(2,1)}, u32[]{:S(2)}) copy-start(bf16[64,1024]{1,0:T(8,128)(2,1)} %param.33) | copy-start | bytes 393220
  157.9 14.3 %copy-start.6 = (s32[1,4]{1,0:T(1,128)S(1)}, s32[1,4]{1,0:T(1,128)}, u32[]{:S(2)}) copy-start(s32[1,4]{1,0:T(1,128)} %counts.1) | copy-start | bytes 52
  157.9 14.7 %copy-start.5 = (s32[1,4]{1,0:T(1,128)S(1)}, s32[1,4]{1,0:T(1,128)}, u32[]{:S(2)}) copy-start(s32[1,4]{1,0:T(1,128)} %lengths.1) | copy-start | bytes 52
  157.9 15.0 %copy-start.18 = (s32[1,4,32]{2,1,0:T(4,128)S(1)}, s32[1,4,32]{2,1,0:T(4,128)}, u32[]{:S(2)}) copy-start(s32[1,4,32]{2,1,0:T(4,128)} %param.29) | copy-start | bytes 1540
  157.9 145.2 %all-to-all-start.1 = ((bf16[64,8,3584]{2,1,0:T(8,128)(2,1)}), bf16[64,8,3584]{2,1,0:T(8,128)(2,1)}, u32[]{:S(2)}, u32[]{:S(2)}) async-start(bf16[64,8,3584]{2,1,0:T(8,128)(2,1)} %fusion), calls=%async_computation.1 | async-start | bytes 7340032 | tf_op jit(solution)/shard_map/all_to_all | solution.py:319
  169.2 70.6 %collective-permute-start.5 = (bf16[64,16,512]{2,1,0:T(8,128)(2,1)S(1)}, bf16[64,16,512]{2,1,0:T(8,128)(2,1)S(1)}, u32[]{:S(2)}, u32[]{:S(2)}) collective-permute-start(bf16[64,16,512]{2,1,0:T(8,128)(2,1)S(1)} %copy-done.1), channel_id=1, source_target_pairs={{0,2},{2,0},{1,3},{3,1},{4,6},{6,4},{5,7},{7,5},{8,10},{10,8},{9,1... | collective-permute-start | bytes 3145736 | tf_op jit(solution)/shard_map/ppermute | solution.py:246
  171.9 66.9 %collective-permute-start.6 = (bf16[64,1024]{1,0:T(8,128)(2,1)S(1)}, bf16[64,1024]{1,0:T(8,128)(2,1)S(1)}, u32[]{:S(2)}, u32[]{:S(2)}) collective-permute-start(bf16[64,1024]{1,0:T(8,128)(2,1)S(1)} %copy-done.15), channel_id=1, source_target_pairs={{0,2},{2,0},{1,3},{3,1},{4,6},{6,4},{5,7},{7,5},{8,10},{10,8},{9,1... | collective-permute-start | bytes 393224 | tf_op jit(solution)/shard_map/ppermute | solution.py:246
  296.7 6.3 %collective-permute-start.8 = (f32[64,16]{0,1:T(8,128)S(1)}, f32[64,16]{0,1:T(8,128)S(1)}, u32[]{:S(2)}, u32[]{:S(2)}) collective-permute-start(f32[64,16]{0,1:T(8,128)S(1)} %bitcast.83), channel_id=1, source_target_pairs={{0,2},{2,0},{1,3},{3,1},{4,6},{6,4},{5,7},{7,5},{8,10},{10,8},{9,1... | collective-permute-start | bytes 12296 | tf_op jit(solution)/shard_map/ppermute | solution.py:246
  301.9 26.6 %collective-permute-start.7 = (bf16[64,16,512]{2,1,0:T(8,128)(2,1)}, bf16[64,16,512]{2,1,0:T(8,128)(2,1)}, u32[]{:S(2)}, u32[]{:S(2)}) collective-permute-start(bf16[64,16,512]{2,1,0:T(8,128)(2,1)} %copy-done.7), channel_id=1, source_target_pairs={{0,2},{2,0},{1,3},{3,1},{4,6},{6,4},{5,7},{7,5},{8,10},{10,8},{9,1... | collective-permute-start | bytes 3145736 | tf_op jit(solution)/shard_map/ppermute | solution.py:246
  303.1 3.3 copy-start.13
  308.4 25.2 %copy-start.12 = (bf16[16,3584]{1,0:T(8,128)(2,1)}, bf16[16,3584]{1,0:T(8,128)(2,1)S(1)}, u32[]{:S(2)}) copy-start(bf16[16,3584]{1,0:T(8,128)(2,1)S(1)} %fusion.2) | copy-start | bytes 344068
  308.4 20.4 %copy-start.3 = (f32[64,16,128]{2,1,0:T(8,128)S(1)}, f32[64,16,128]{2,1,0:T(8,128)}, u32[]{:S(2)}) copy-start(f32[64,16,128]{2,1,0:T(8,128)} %copy-done.2) | copy-start | bytes 1572868
  309.4 24.2 %copy-start.14 = (bf16[16,512]{1,0:T(8,128)(2,1)}, bf16[16,512]{1,0:T(8,128)(2,1)S(1)}, u32[]{:S(2)}) copy-start(bf16[16,512]{1,0:T(8,128)(2,1)S(1)} %multiply_convert_fusion.2) | copy-start | bytes 49156
  309.7 2.3 collective-permute-start.2
  312.0 16.5 %collective-permute-start.3 = (bf16[2,16,576]{2,1,0:T(8,128)(2,1)S(1)}, bf16[2,16,576]{2,1,0:T(8,128)(2,1)S(1)}, u32[]{:S(2)}, u32[]{:S(2)}) collective-permute-start(bf16[2,16,576]{2,1,0:T(8,128)(2,1)S(1)} %reverse_select_fusion.1), channel_id=1, source_target_pairs={{0,2},{2,0},{1,3},{3,1},{4,6},{6,4},{5,7},{7,5},{8,10},{10,8},{9,1... | collective-permute-start | bytes 110600 | tf_op jit(solution)/shard_map/ppermute | solution.py:246
  (7 other events, 9.9 us)

commit v2 on v1

--- a/solution.py
+++ b/solution.py
@@ -51,7 +51,7 @@
     table, lengths, counts, where, own_kv, sib_kv, q_own, q_par, r_own, r_par,
     o_own, o_par, s_own, s_par, held, place, sems,
 ):
-    zh, core = where[0], where[1]
+    zh, core, low = where[0], where[1], where[2]
     heads = q_own.shape[1]
     rows = TILE * heads
 
@@ -78,7 +78,11 @@
         def step(j, carry):
             slot, last = carry
             holder = table[0, chat * MAXB + j]
-            mine = (j * BLOCK < length) & ((lax.shift_right_logical(holder, 1) & 1) == zh)
+            z = (lax.shift_right_logical(holder, 1) & 1) * 2 + (
+                lax.shift_right_logical(holder, 2) & 1
+            )
+            step_z = jnp.where((z & 1) == low, 0, 1 + 2 * (holder & 1))
+            mine = (j * BLOCK < length) & (lax.shift_right_logical((z + step_z) & 3, 1) == zh)
 
             @pl.when(mine)
             def _():
@@ -241,16 +245,253 @@
         name="finish",
     )(q_own, r_own, fresh, fresh_rope, ok, oa, ob, sa, sb)
 
+MESH = pl.DeviceIdType.MESH
+SENDS = 2 * N_DP
+CHUNK = 32
+
+
+def shifted(dy, dx, dz, sign):
+    dp, zh = lax.axis_index("dp"), lax.axis_index("zh")
+    y, x, z = lax.div(dp, 8), lax.rem(lax.div(dp, 2), 4), zh * 2 + lax.rem(dp, 2)
+    y = lax.rem(y + 4 + sign * dy, 4)
+    x = lax.rem(x + 4 + sign * dx, 4)
+    z = lax.rem(z + 4 + sign * dz, 4)
+    return y * 8 + x * 2 + lax.rem(z, 2), lax.div(z, 2)
+
+
+def row_place(i, sign):
+    j = lax.rem(i * 37, SENDS)
+    return shifted(lax.div(j, 16), lax.rem(lax.div(j, 4), 4), lax.rem(j, 4), sign)
+
+
+def block_place(i, sign):
+    j = lax.rem(i * 11, N_DP)
+    core = lax.axis_index("core")
+    dz = lax.rem(j, 2) * (1 + 2 * core)
+    return shifted(lax.div(j, 8), lax.rem(lax.div(j, 2), 4), dz, sign)
+
+
+def feed_kernel(
+    rows, cache, send, q, r, wg_hbm, wu_hbm, wd_hbm,
+    own_kv, sib_kv, q_par, r_par, out,
+    wg, wu, wd, arr, arr_sib, stage, acts, part, part_sib, part_in,
+    w_sem, row_send, row_recv, fwd_send, fwd_recv, part_send, part_recv,
+    kv_send, kv_recv, kvf_send, kvf_recv, misc_send, misc_recv,
+):
+    dp, zh, core = lax.axis_index("dp"), lax.axis_index("zh"), lax.axis_index("core")
+    sibling = (dp, zh, 1 - core)
+    partner = (dp, 1 - zh, core)
+    loads = [
+        pltpu.make_async_copy(a, b, w_sem.at[i])
+        for i, (a, b) in enumerate(((wg_hbm, wg), (wu_hbm, wu), (wd_hbm, wd)))
+    ]
+    for load in loads:
+        load.start()
+
+    barrier = pltpu.get_barrier_semaphore()
+
+    def greet(i, carry):
+        to, to_zh = row_place(i, 1)
+        pl.semaphore_signal(barrier, inc=1, device_id=(to, to_zh, core), device_id_type=MESH)
+        return carry
+
+    lax.fori_loop(1, SENDS, greet, 0)
+    pl.semaphore_signal(barrier, inc=1, device_id=sibling, device_id_type=MESH)
+    pl.semaphore_wait(barrier, SENDS)
+
+    def remote(src, dst, send_sem, recv_sem, device):
+        return pltpu.make_async_remote_copy(
+            src_ref=src, dst_ref=dst, send_sem=send_sem, recv_sem=recv_sem,
+            device_id=device, device_id_type=MESH,
+        )
+
+    def row_copy(i):
+        to, to_zh = row_place(i, 1)
+        return remote(rows.at[to], arr.at[i], row_send.at[i], row_recv.at[i], (to, to_zh, core))
+
+    def fwd_copy(i):
+        return remote(arr.at[i], arr_sib.at[i], fwd_send.at[i], fwd_recv.at[i], sibling)
+
+    def part_copy(c):
+        at = pl.ds(c * CHUNK, CHUNK)
+        return remote(
+            part_sib.at[at], part_in.at[at], part_send.at[c], part_recv.at[c], sibling
+        )
+
+    def kv_copy(i):
+        to, to_zh = block_place(i, 1)
+        return remote(
+            stage.at[i], own_kv.at[dp], kv_send.at[i], kv_recv.at[i], (to, to_zh, core)
+        )
+
+    def kvf_copy(i):
+        source, _ = block_place(i, -1)
+        return remote(
+            own_kv.at[source], sib_kv.at[source], kvf_send.at[i], kvf_recv.at[i], sibling
+        )
+
+    def start_rows(i, carry):
+        row_copy(i).start()
+        return carry
+
+    lax.fori_loop(1, SENDS, start_rows, 0)
+    arr[0] = rows[dp]
+
+    q_copy = remote(q, q_par, misc_send.at[0], misc_recv.at[0], partner)
+    r_copy = remote(r, r_par, misc_send.at[1], misc_recv.at[1], partner)
+    q_copy.start()
+    r_copy.start()
+
+    def start_blocks(i, carry):
+        to, _ = block_place(i, 1)
+        stage[i] = cache[send[0, to]]
+        kv_copy(i).start()
+        return carry
+
+    lax.fori_loop(1, N_DP, start_blocks, 0)
+    stage[0] = cache[send[0, dp]]
+    mine = pltpu.make_async_copy(stage.at[0], own_kv.at[dp], kv_send.at[0])
+    mine.start()
+    mine_fwd = remote(stage.at[0], sib_kv.at[dp], kvf_send.at[0], kvf_recv.at[0], sibling)
+    mine_fwd.start()
+    for load in loads:
+        load.wait()
+
+    def experts(source, target, c):
+        at = pl.ds(c * CHUNK, CHUNK)
+        x = source[at].reshape(CHUNK * source.shape[1], source.shape[2])
+        for n in range(2):
+            cut = slice(n * 256, (n + 1) * 256)
+            gate = jnp.dot(x, wg[:, cut], preferred_element_type=jnp.float32)
+            lifted = jnp.dot(x, wu[:, cut], preferred_element_type=jnp.float32)
+            acts[:, cut] = (gate / (1.0 + jnp.exp(-gate)) * lifted).astype(jnp.bfloat16)
+
+        def down(n, carry):
+            cut = pl.ds(pl.multiple_of(n * 512, 512), 512)
+            value = jnp.dot(acts[...], wd[:, cut], preferred_element_type=jnp.float32)
+            target[at, :, cut] = value.astype(jnp.bfloat16).reshape(CHUNK, source.shape[1], 512)
+            return carry
+
+        lax.fori_loop(0, source.shape[2] // 512, down, 0)
+
+    def chunk(c, carry):
+        first = c * CHUNK
+
+        def pass_on(i, carry):
+            @pl.when(i > 0)
+            def _():
+                row_copy(i).wait_recv()
+
+            fwd_copy(i).start()
+            return carry
+
+        lax.fori_loop(first, first + CHUNK, pass_on, 0)
+        experts(arr, part, c)
+
+        def await_sib(i, carry):
+            fwd_copy(i).wait_recv()
+            return carry
+
+        lax.fori_loop(first, first + CHUNK, await_sib, 0)
+        experts(arr_sib, part_sib, c)
+        part_copy(c).start()
+        return carry
+
+    lax.fori_loop(0, SENDS // CHUNK, chunk, 0)
+
+    def pass_block(i, carry):
+        kv_copy(i).wait_recv()
+        kvf_copy(i).start()
+        return carry
+
+    lax.fori_loop(1, N_DP, pass_block, 0)
+
+    def add_up(i, carry):
+        source, source_zh = row_place(i, -1)
+        total = part[i].astype(jnp.float32) + part_in[i].astype(jnp.float32)
+        out[source * 2 + source_zh] = total.astype(jnp.bfloat16)
+        return carry
+
+    def add_chunk(c, carry):
+        part_copy(c).wait()
+        lax.fori_loop(c * CHUNK, (c + 1) * CHUNK, add_up, 0)
+        return carry
+
+    lax.fori_loop(0, SENDS // CHUNK, add_chunk, 0)
+
+    def end_rows(i, carry):
+        row_copy(i).wait_send()
+        return carry
+
+    lax.fori_loop(1, SENDS, end_rows, 0)
+
+    def end_fwd(i, carry):
+        fwd_copy(i).wait_send()
+        return carry
+
+    lax.fori_loop(0, SENDS, end_fwd, 0)
+
+    def end_blocks(i, carry):
+        kv_copy(i).wait_send()
+        kvf_copy(i).wait()
+        return carry
+
+    lax.fori_loop(1, N_DP, end_blocks, 0)
+    mine.wait()
+    mine_fwd.wait()
+    q_copy.wait()
+    r_copy.wait()
+
+
+def feed(rows, cache, send, q, r, wg, wu, wd):
+    smem = pl.BlockSpec(memory_space=pltpu.SMEM)
+    vmem = pl.BlockSpec(memory_space=pltpu.VMEM)
+    hbm = pl.BlockSpec(memory_space=pl.ANY)
+    bf16 = jnp.bfloat16
+    blocks = jax.ShapeDtypeStruct((N_DP,) + cache.shape[1:], bf16)
+    chips = (SENDS,) + rows.shape[1:]
+    dma = pltpu.SemaphoreType.DMA
+    chunks = SENDS // CHUNK
+    return pl.pallas_call(
+        feed_kernel,
+        out_shape=(
+            blocks,
+            blocks,
+            jax.ShapeDtypeStruct(q.shape, bf16),
+            jax.ShapeDtypeStruct(r.shape, bf16),
+            jax.ShapeDtypeStruct(chips, bf16),
+        ),
+        in_specs=[vmem, vmem, smem] + [hbm] * 5,
+        out_specs=(hbm, hbm, hbm, hbm, vmem),
+        scratch_shapes=[
+            pltpu.VMEM(wg.shape, bf16),
+            pltpu.VMEM(wu.shape, bf16),
+            pltpu.VMEM(wd.shape, bf16),
+            pltpu.VMEM(chips, bf16),
+            pltpu.VMEM(chips, bf16),
+            pltpu.VMEM(blocks.shape, bf16),
+            pltpu.VMEM((CHUNK * rows.shape[1], wg.shape[1]), bf16),
+            pltpu.VMEM(chips, bf16),
+            pltpu.VMEM(chips, bf16),
+            pltpu.VMEM(chips, bf16),
+            dma((3,)),
+            dma((SENDS,)), dma((SENDS,)), dma((SENDS,)), dma((SENDS,)),
+            dma((chunks,)), dma((chunks,)),
+            dma((N_DP,)), dma((N_DP,)), dma((N_DP,)), dma((N_DP,)),
+            dma((2,)), dma((2,)),
+        ],
+        compiler_params=pltpu.CompilerParams(
+            collective_id=1, has_side_effects=True, vmem_limit_bytes=56 * 2**20
+        ),
+        cost_estimate=pl.CostEstimate(
+            flops=11 * 10**9, bytes_accessed=24 * 2**20, transcendentals=2**19
+        ),
+        name="feed",
+    )(rows, cache, send, q, r, wg, wu, wd)
+
 
 def swap(value, axis):
     return lax.ppermute(value, axis, [(0, 1), (1, 0)])
-
-
-def expert_rows(flat_rows, gate_matrix, up_matrix, down_matrix):
-    gate = jnp.dot(flat_rows, gate_matrix, preferred_element_type=jnp.float32)
-    lifted = jnp.dot(flat_rows, up_matrix, preferred_element_type=jnp.float32)
-    activated = (jax.nn.silu(gate) * lifted).astype(jnp.bfloat16)
-    return jnp.dot(activated, down_matrix, preferred_element_type=jnp.float32).astype(jnp.bfloat16)
 
 
 def shards(
@@ -293,31 +534,24 @@
         (((0,), (0,)), ((), ())),
         preferred_element_type=jnp.float32,
     ).astype(jnp.bfloat16)
-    spread = jnp.broadcast_to(
-        outgoing.reshape(N_DP, 1, capacity, width), (N_DP, 2, capacity, width)
-    ).reshape(N_DP * 2, capacity, width)
-    arrived = lax.all_to_all(spread, ("dp", "zh"), split_axis=0, concat_axis=0, tiled=True)
-    arrived = arrived.reshape(-1, width)
-    arrived_sib = swap(arrived, "core")
-
     packed = jnp.concatenate(
         [cache_rope[:, 16 * k : 16 * (k + 1), :] for k in range(LAT // BLOCK)], axis=2
     )
-    blocks = jnp.concatenate([cache_latent, packed], axis=1)[send_index[0]]
-    own_kv = lax.all_to_all(blocks, "dp", split_axis=0, concat_axis=0, tiled=True)
-    sib_kv = swap(own_kv, "core")
+    cache = jnp.concatenate([cache_latent, packed], axis=1)
+    own_kv, sib_kv, q_par, r_par, partial = feed(
+        outgoing.reshape(N_DP, capacity, width),
+        cache,
+        send_index,
+        q_latent,
+        q_rope,
+        w_gate[0],
+        w_up[0],
+        w_down[0],
+    )
     r_own = q_rope.reshape(TOK, HEADS_DEV, ROPE)
-    q_par = swap(q_latent, "zh")
-    r_par = swap(q_rope, "zh").reshape(TOK, HEADS_DEV, ROPE)
-
-    matrices = (w_gate[0], w_up[0], w_down[0])
-    theirs = expert_rows(arrived_sib, *matrices)
-    mine = expert_rows(arrived, *matrices)
-    partial = (mine.astype(jnp.float32) + swap(theirs, "core").astype(jnp.float32)).astype(
-        jnp.bfloat16
-    )
+    r_par = r_par.reshape(TOK, HEADS_DEV, ROPE)
     returned = lax.all_to_all(
-        partial.reshape(N_DP * 2, capacity, width),
+        partial,
         ("dp", "zh"),
         split_axis=0,
         concat_axis=0,
@@ -350,7 +584,7 @@
     quad = jnp.stack([pair, swap(pair, "zh")])
     quad = jnp.where(zh == 0, quad, quad[::-1]).reshape(TOK, LAT + ROPE)
 
-    where = jnp.stack([zh, core]).astype(jnp.int32)
+    where = jnp.stack([zh, core, lax.axis_index("dp") % 2]).astype(jnp.int32)
     o_own, o_par, s_own, s_par = attend(
         block_table.reshape(1, CHATS * MAXB),
         cached_len,

time: 338 us -> 267 us (0.79)
  Pallas kernels: 56.6 us -> 186 us
  waiting for transfers between devices: 133 us -> 26.4 us
  blocking collectives: 52.6 us -> 0 us
  matrix products: 35.9 us -> 5.53 us
  starting transfers between devices: 36.6 us -> 26.9 us
  local copies, waits for them, and re-layouts: 11.9 us -> 7.51 us
    pallas_call x0 -> x1, Pallas kernels: none -> 118 us  [feed(): pl.pallas_call(feed_kernel, out_shape=(blocks, blocks, jax.ShapeDtypeStru...]
    ppermute x9 -> x4, waiting for transfers between devices: 79.9 us -> 26.4 us  [swap(): return lax.ppermute(value, axis, [(0, 1), (1, 0)])]
    all_to_all x2 -> x1, waiting for transfers between devices: 53.3 us -> 0.01 us  [shards(): lax.all_to_all(partial, ('dp', 'zh'), split_axis=0, concat_axis=0, tiled=...]
    all_to_all x1 -> x0, blocking collectives: 52.6 us -> none  [shards(): lax.all_to_all(spread, ('dp', 'zh'), split_axis=0, concat_axis=0, tiled=T...]
    dot_general x4 -> x0, matrix products: 31.6 us -> none  [the longest x2 21.2 us: expert_rows(): jnp.dot(activated, down_matrix, preferred_element_type=jnp.float32)]
    pallas_call x1, Pallas kernels: 51.8 us -> 63.9 us  [attend(): pl.pallas_call(attend_kernel, out_shape=(out, out, stat, stat), in_specs=...]
    ppermute x9 -> x4, starting transfers between devices: 16.6 us -> 4.85 us  [swap(): return lax.ppermute(value, axis, [(0, 1), (1, 0)])]
    all_to_all x2 -> x1, starting transfers between devices: 20 us -> 22.1 us  [shards(): lax.all_to_all(partial, ('dp', 'zh'), split_axis=0, concat_axis=0, tiled=...]
  transfers between devices with their start and end apart: 11 -> 5, of which waited for: 5 -> 3; matrix products, arithmetic and copies ran while one was open for 13% -> 4% of each run, Pallas kernels for 16% -> 24%
where the time goes in v2:
time: 267 us; the launch traced here: 262 us
  Pallas kernels  186 us (70%)
  starting transfers between devices  26.9 us (10%)
  waiting for transfers between devices  26.4 us (10%)
  other arithmetic  7.94 us (3%)
  local copies, waits for them, and re-layouts  7.51 us (3%)
  matrix products  5.53 us (2%)
    pallas_call x1, Pallas kernels, feed(): pl.pallas_call(feed_kernel, out_shape=(blocks, blocks, jax.ShapeDtypeStru...  118 us
    pallas_call x1, Pallas kernels, attend(): pl.pallas_call(attend_kernel, out_shape=(out, out, stat, stat), in_specs=...  63.9 us
    ppermute x4, waiting for transfers between devices, swap(): return lax.ppermute(value, axis, [(0, 1), (1, 0)])  26.4 us
    all_to_all x1, starting transfers between devices, shards(): lax.all_to_all(partial, ('dp', 'zh'), split_axis=0, concat_axis=0, tiled=...  22.1 us
  transfers between devices with their start and end apart: 5, of which 3 were waited for; matrix products, arithmetic and copies ran while one was open for 4% of the time, Pallas kernels for 24%

profile of v2, /device:TPU:23, one launch (start us, length us, event | category | flops | bytes accessed | tf_op | source)
XLA Modules:
  0.0 261.7 jit_solution(7755955870799673366)
XLA Ops:
  0.6 0.9 fusion.17
  1.5 0.8 copy.29
  2.9 0.8 copy.31
  3.8 2.8 %fusion.rows = bf16[32,8,3584]{2,1,0:T(8,128)(2,1)} fusion(bf16[16,3584]{1,0:T(8,128)(2,1)} %param.17, bf16[16,256]{1,0:T(8,128)(2,1)S(1)} %get-tuple-element.22), kind=kOutput, calls=%fused_computation.2 | convolution fusion | flops 30277632 | bytes 1957888 | tf_op jit(solution)/shard_map/dot_general | solution.py:531
  6.6 2.4 maximum_maximum_fusion.cache
  9.0 117.8 %feed.1 = (bf16[32,144,512]{2,1,0:T(8,128)(2,1)}, bf16[32,144,512]{2,1,0:T(8,128)(2,1)}, bf16[64,16,512]{2,1,0:T(8,128)(2,1)}, bf16[64,1024]{1,0:T(8,128)(2,1)}, bf16[64,8,3584]{2,1,0:T(8,128)(2,1)}) custom-call(bf16[32,8,3584]{2,1,0:T(8,128)(2,1)} %fusion.rows, bf16[8,144,512]{2,1,0:T(8,128)(2,1)} %maximum_maximum_fusion.cache, s32[1,32]{1,0:T(1,128)} %send.1, ...), custom_call_target="tpu_custom_call" | custom-call | flops 11000000512 | bytes 25165824 | tf_op jit(solution)/shard_map/feed/pallas_call | solution.py:455
  126.8 22.1 %all-to-all-start = ((bf16[64,8,3584]{2,1,0:T(8,128)(2,1)}), bf16[64,8,3584]{2,1,0:T(8,128)(2,1)}, u32[]{:S(2)}, u32[]{:S(2)}) async-start(bf16[64,8,3584]{2,1,0:T(8,128)(2,1)} %get-tuple-element.13), calls=%async_computation | async-start | bytes 7340032 | tf_op jit(solution)/shard_map/all_to_all | solution.py:553
  149.2 0.9 reshape.109.r_par
  150.2 0.9 copy-done.4
  151.2 1.2 copy-done.7
  152.4 63.9 %attend.1 = (bf16[64,16,512]{2,1,0:T(8,128)(2,1)S(1)}, bf16[64,16,512]{2,1,0:T(8,128)(2,1)}, f32[64,16,128]{2,1,0:T(8,128)S(1)}, f32[64,16,128]{2,1,0:T(8,128)S(1)}) custom-call(s32[1,128]{1,0:T(1,128)S(1)} %reshape.108.table, s32[1,4]{1,0:T(1,128)S(1)} %copy-done.5, s32[1,4]{1,0:T(1,128)S(1)} %copy-done.6, s32[3]{0:T(128)S(1)} %pad_add_fusion.where, ...), custom_call_target="tpu_custom_call" | custom-call | flops 8999999488 | bytes 12582912 | tf_op jit(solution)/shard_map/attend/pallas_call | solution.py:186
  216.3 0.8 copy-done.2
  217.1 0.3 copy.32
  217.4 3.0 %collective-permute-start.3 = (f32[64,16]{0,1:T(8,128)S(1)}, f32[64,16]{0,1:T(8,128)S(1)}, u32[]{:S(2)}, u32[]{:S(2)}) collective-permute-start(f32[64,16]{0,1:T(8,128)S(1)} %bitcast.46), channel_id=1, source_target_pairs={{0,2},{2,0},{1,3},{3,1},{4,6},{6,4},{5,7},{7,5},{8,10},{10,8},{9,1... | collective-permute-start | bytes 12296 | tf_op jit(solution)/shard_map/ppermute | solution.py:494
  220.9 21.9 %collective-permute-done.3 = f32[64,16]{0,1:T(8,128)S(1)} collective-permute-done((f32[64,16]{0,1:T(8,128)S(1)}, f32[64,16]{0,1:T(8,128)S(1)}, u32[]{:S(2)}, u32[]{:S(2)}) %collective-permute-start.3) | collective-permute-done | bytes 4128 | tf_op jit(solution)/shard_map/ppermute | solution.py:494
  242.9 3.2 %convert_reduce_fusion = f32[32,8,3584]{2,1,0:T(8,128)S(1)} fusion(bf16[64,8,3584]{2,1,0:T(8,128)(2,1)} %all-to-all-done), kind=kLoop, calls=%fused_computation | loop fusion | flops 2752512 | bytes 7340032 | tf_op jit(solution)/shard_map/reduce_sum | solution.py:560
  246.2 1.8 fusion.1
  248.2 0.7 multiply_reduce_fusion
  248.9 0.2 fusion.18
  249.5 1.8 collective-permute-start
  251.3 0.7 pad_maximum_fusion.3
  252.3 4.3 %collective-permute-done.1 = bf16[2,16,576]{2,1,0:T(8,128)(2,1)S(1)} collective-permute-done((bf16[2,16,576]{2,1,0:T(8,128)(2,1)S(1)}, bf16[2,16,576]{2,1,0:T(8,128)(2,1)S(1)}, u32[]{:S(2)}, u32[]{:S(2)}) %collective-permute-start.1) | collective-permute-done | bytes 36896 | tf_op jit(solution)/shard_map/ppermute | solution.py:494
  256.7 0.2 broadcast_in_dim.2.sb
  256.9 4.8 %finish.1 = bf16[64,16,512]{2,1,0:T(8,128)(2,1)} custom-call(bf16[64,16,512]{2,1,0:T(8,128)(2,1)S(1)} %copy-done.1, bf16[64,16,64]{2,1,0:T(8,128)(2,1)S(1)} %reshape.106.r_own.r_ref, bf16[64,512]{1,0:T(8,128)(2,1)S(1)} %slice.38.fresh_ref, bf16[64,64]{1,0:T(8,128)(2,1)S(1)} %slice.39.fresh_rope_ref, f32[64,64]{1,0:T(8,128)S(1)} %fusion.5.ok_ref, ...), custom_call_target="tpu_custom_call" | custom-call | tf_op jit(solution)/shard_map/finish/pallas_call | solution.py:239
  (66 shorter events, 2.7 us)
Async XLA Ops:
  0.6 248.3 %copy-start = (bf16[3584,64]{0,1:T(8,128)(2,1)S(1)}, bf16[3584,64]{0,1:T(8,128)(2,1)}, u32[]{:S(2)}) copy-start(bf16[3584,64]{0,1:T(8,128)(2,1)} %param.24) | copy-start | bytes 1376260
  126.8 22.2 %copy-start.12 = (bf16[64,1024]{1,0:T(8,128)(2,1)S(1)}, bf16[64,1024]{1,0:T(8,128)(2,1)}, u32[]{:S(2)}) copy-start(bf16[64,1024]{1,0:T(8,128)(2,1)} %r.1) | copy-start | bytes 393220
  126.8 22.4 %copy-start.13 = (bf16[64,1024]{1,0:T(8,128)(2,1)S(1)}, bf16[64,1024]{1,0:T(8,128)(2,1)}, u32[]{:S(2)}) copy-start(bf16[64,1024]{1,0:T(8,128)(2,1)} %get-tuple-element.17) | copy-start | bytes 393220
  126.8 23.3 %copy-start.15 = (s32[1,4,32]{2,1,0:T(4,128)S(1)}, s32[1,4,32]{2,1,0:T(4,128)}, u32[]{:S(2)}) copy-start(s32[1,4,32]{2,1,0:T(4,128)} %param.29) | copy-start | bytes 1540
  126.8 23.4 %copy-start.1 = (bf16[64,16,512]{2,1,0:T(8,128)(2,1)S(1)}, bf16[64,16,512]{2,1,0:T(8,128)(2,1)}, u32[]{:S(2)}) copy-start(bf16[64,16,512]{2,1,0:T(8,128)(2,1)} %q_ref.1) | copy-start | bytes 3145732
  126.8 23.4 %copy-start.5 = (s32[1,4]{1,0:T(1,128)S(1)}, s32[1,4]{1,0:T(1,128)}, u32[]{:S(2)}) copy-start(s32[1,4]{1,0:T(1,128)} %lengths.1) | copy-start | bytes 52
  126.8 23.4 %copy-start.6 = (s32[1,4]{1,0:T(1,128)S(1)}, s32[1,4]{1,0:T(1,128)}, u32[]{:S(2)}) copy-start(s32[1,4]{1,0:T(1,128)} %counts.1) | copy-start | bytes 52
  126.8 116.1 %all-to-all-start = ((bf16[64,8,3584]{2,1,0:T(8,128)(2,1)}), bf16[64,8,3584]{2,1,0:T(8,128)(2,1)}, u32[]{:S(2)}, u32[]{:S(2)}) async-start(bf16[64,8,3584]{2,1,0:T(8,128)(2,1)} %get-tuple-element.13), calls=%async_computation | async-start | bytes 7340032 | tf_op jit(solution)/shard_map/all_to_all | solution.py:553
  150.2 1.0 copy-start.4
  151.2 1.2 copy-start.7
  216.3 0.8 copy-start.2
  217.1 39.6 %collective-permute-start.2 = (bf16[64,16,512]{2,1,0:T(8,128)(2,1)}, bf16[64,16,512]{2,1,0:T(8,128)(2,1)}, u32[]{:S(2)}, u32[]{:S(2)}) collective-permute-start(bf16[64,16,512]{2,1,0:T(8,128)(2,1)} %get-tuple-element.19), channel_id=1, source_target_pairs={{0,2},{2,0},{1,3},{3,1},{4,6},{6,4},{5,7},{7,5},{8,10},{10,8},{9,1... | collective-permute-start | bytes 3145736 | tf_op jit(solution)/shard_map/ppermute | solution.py:494
  217.4 25.4 %collective-permute-start.3 = (f32[64,16]{0,1:T(8,128)S(1)}, f32[64,16]{0,1:T(8,128)S(1)}, u32[]{:S(2)}, u32[]{:S(2)}) collective-permute-start(f32[64,16]{0,1:T(8,128)S(1)} %bitcast.46), channel_id=1, source_target_pairs={{0,2},{2,0},{1,3},{3,1},{4,6},{6,4},{5,7},{7,5},{8,10},{10,8},{9,1... | collective-permute-start | bytes 12296 | tf_op jit(solution)/shard_map/ppermute | solution.py:494
  242.9 3.3 %copy-start.10 = (bf16[16,3584]{1,0:T(8,128)(2,1)S(1)}, bf16[16,3584]{1,0:T(8,128)(2,1)}, u32[]{:S(2)}) copy-start(bf16[16,3584]{1,0:T(8,128)(2,1)} %param.17) | copy-start | bytes 344068
  246.2 2.0 copy-start.8
  246.2 3.0 %copy-start.14 = (f32[512]{0:T(512)S(1)}, f32[512]{0:T(512)}, u32[]{:S(2)}) copy-start(f32[512]{0:T(512)} %param.25) | copy-start | bytes 6148
  248.2 13.5 %copy-start.9 = (bf16[16,3584]{1,0:T(8,128)(2,1)}, bf16[16,3584]{1,0:T(8,128)(2,1)S(1)}, u32[]{:S(2)}) copy-start(bf16[16,3584]{1,0:T(8,128)(2,1)S(1)} %fusion.1) | copy-start | bytes 344068
  248.2 8.7 %copy-start.3 = (f32[64,16,128]{2,1,0:T(8,128)S(1)}, f32[64,16,128]{2,1,0:T(8,128)}, u32[]{:S(2)}) copy-start(f32[64,16,128]{2,1,0:T(8,128)} %copy-done.2) | copy-start | bytes 1572868
  249.2 12.4 %copy-start.11 = (bf16[16,512]{1,0:T(8,128)(2,1)}, bf16[16,512]{1,0:T(8,128)(2,1)S(1)}, u32[]{:S(2)}) copy-start(bf16[16,512]{1,0:T(8,128)(2,1)S(1)} %multiply_convert_fusion) | copy-start | bytes 49156
  249.5 2.6 collective-permute-start
  252.2 4.4 %collective-permute-start.1 = (bf16[2,16,576]{2,1,0:T(8,128)(2,1)S(1)}, bf16[2,16,576]{2,1,0:T(8,128)(2,1)S(1)}, u32[]{:S(2)}, u32[]{:S(2)}) collective-permute-start(bf16[2,16,576]{2,1,0:T(8,128)(2,1)S(1)} %reverse_select_fusion.1), channel_id=1, source_target_pairs={{0,2},{2,0},{1,3},{3,1},{4,6},{6,4},{5,7},{7,5},{8,10},{10,8},{9,1... | collective-permute-start | bytes 110600 | tf_op jit(solution)/shard_map/ppermute | solution.py:494

commit v3 on v2

--- a/solution.py
+++ b/solution.py
@@ -22,7 +22,7 @@
 ROPE = 64
 TOK = 64
 HEADS_DEV = 16
-GROUP = 2
+GROUP = 4
 TILE = 16
 SLOTS = 2 * N_DP + CHATS * (GROUP - 1) + 2
 
@@ -48,11 +48,11 @@
 
 
 def attend_kernel(
-    table, lengths, counts, where, own_kv, sib_kv, q_own, q_par, r_own, r_par,
-    o_own, o_par, s_own, s_par, held, place, sems,
+    table, lengths, counts, where, own_kv, sib_kv, q_ref, r_ref, after,
+    o_ref, s_ref, held, place, sems, scores,
 ):
     zh, core, low = where[0], where[1], where[2]
-    heads = q_own.shape[1]
+    heads = q_ref.shape[1]
     rows = TILE * heads
 
     def copy_in(ref, source, slot):
@@ -119,15 +119,16 @@
 
         def tile(t, carry):
             base = jnp.minimum(start + t * TILE, TOK - TILE)
-            queries = [
-                (q[pl.ds(base, TILE)].reshape(rows, LAT), r[pl.ds(base, TILE)].reshape(rows, ROPE))
-                for q, r in ((q_own, r_own), (q_par, r_par))
-            ]
-
-            def group(g, state):
+            ql = q_ref[pl.ds(base, TILE)].reshape(rows, LAT)
+            qr = r_ref[pl.ds(base, TILE)].reshape(rows, ROPE)
+
+            def keys_of(g):
                 at = (first_group + g) * GROUP
                 blocks = [held[at + i] for i in range(GROUP)]
-                keys = jnp.concatenate([b[:BLOCK] for b in blocks], axis=0)
+                return blocks, jnp.concatenate([b[:BLOCK] for b in blocks], axis=0)
+
+            def score(g, best):
+                blocks, keys = keys_of(g)
                 ropes = jnp.concatenate(
                     [
                         jnp.concatenate(
@@ -138,67 +139,80 @@
                     ],
                     axis=1,
                 )
+                at = (first_group + g) * GROUP
                 valid = jnp.concatenate([lane < place[at + i] for i in range(GROUP)], axis=1)
-                new = []
-                for (ql, qr), (m, l, acc) in zip(queries, state):
-                    s = lax.dot_general(ql, keys, contract, preferred_element_type=jnp.float32)
-                    s = s + jnp.dot(qr, ropes, preferred_element_type=jnp.float32)
-                    s = jnp.where(valid, s * (SCORE_SCALE * LOG2E), BIG)
-                    m_new = jnp.maximum(m, jnp.max(s, axis=1, keepdims=True))
-                    p = jnp.exp2(s - m_new)
-                    alpha = jnp.exp2(m - m_new)
-                    l = l * alpha + jnp.sum(p, axis=1, keepdims=True)
-                    acc = acc * alpha + jnp.dot(
-                        p.astype(jnp.bfloat16), keys, preferred_element_type=jnp.float32
-                    )
-                    new.append((m_new, l, acc))
-                return tuple(new)
-
-            empty = (
-                jnp.full((rows, 1), BIG, jnp.float32),
-                jnp.zeros((rows, 1), jnp.float32),
-                jnp.zeros((rows, LAT), jnp.float32),
+                s = lax.dot_general(ql, keys, contract, preferred_element_type=jnp.float32)
+                s = s + jnp.dot(qr, ropes, preferred_element_type=jnp.float32)
+                s = jnp.where(valid, s * (SCORE_SCALE * LOG2E), BIG)
+                scores[g] = s
+                for i in range(GROUP):
+                    best = jnp.maximum(best, s[:, i * BLOCK : (i + 1) * BLOCK])
+                return best
+
+            def blend(g, state, top):
+                total, acc = state
+                _, keys = keys_of(g)
+                p = jnp.exp2(scores[g] - top)
+                for i in range(GROUP):
+                    total = total + p[:, i * BLOCK : (i + 1) * BLOCK]
+                acc = acc + jnp.dot(p.astype(jnp.bfloat16), keys, preferred_element_type=jnp.float32)
+                return total, acc
+
+            def over(step, state):
+                def two(g, state):
+                    return step(2 * g + 1, step(2 * g, state))
+
+                state = lax.fori_loop(0, lax.div(n_groups, 2), two, state)
+                return lax.fori_loop(n_groups - lax.rem(n_groups, 2), n_groups, step, state)
+
+            best = over(score, jnp.full((rows, BLOCK), BIG, jnp.float32))
+            top = jnp.max(best, axis=1, keepdims=True)
+            total, acc = over(
+                lambda g, state: blend(g, state, top),
+                (jnp.zeros((rows, BLOCK), jnp.float32), jnp.zeros((rows, LAT), jnp.float32)),
             )
-            state = lax.fori_loop(0, n_groups, group, (empty, empty))
+            total = jnp.sum(total, axis=1, keepdims=True)
             token = base + lax.broadcasted_iota(jnp.int32, (TILE, 1, 1), 0)
             keep = (token >= start) & (token < start + count)
-            for (m, l, acc), o, s in zip(state, (o_own, o_par), (s_own, s_par)):
-                some = l > 0.0
-                safe = jnp.where(some, l, 1.0)
-                value = (acc / safe).astype(jnp.bfloat16).reshape(TILE, heads, LAT)
-                lse = jnp.where(some, m + jnp.log2(safe), BIG)
-                lse = jnp.broadcast_to(lse, (rows, BLOCK)).reshape(TILE, heads, BLOCK)
-                o[pl.ds(base, TILE)] = jnp.where(keep, value, o[pl.ds(base, TILE)])
-                s[pl.ds(base, TILE)] = jnp.where(keep, lse, s[pl.ds(base, TILE)])
+            some = total > 0.0
+            safe = jnp.where(some, total, 1.0)
+            value = (acc / safe).astype(jnp.bfloat16).reshape(TILE, heads, LAT)
+            lse = jnp.where(some, top + jnp.log2(safe), BIG)
+            lse = jnp.broadcast_to(lse, (rows, BLOCK)).reshape(TILE, heads, BLOCK)
+            at = pl.ds(base, TILE)
+            o_ref[at] = jnp.where(keep, value, o_ref[at])
+            s_ref[at] = jnp.where(keep, lse, s_ref[at])
             return carry
 
         lax.fori_loop(0, lax.div(count + TILE - 1, TILE), tile, 0)
         start = start + count
 
 
-def attend(table, lengths, counts, where, own_kv, sib_kv, q_own, q_par, r_own, r_par):
+def attend(table, lengths, counts, where, own_kv, sib_kv, q, r, after, name):
     smem = pl.BlockSpec(memory_space=pltpu.SMEM)
     vmem = pl.BlockSpec(memory_space=pltpu.VMEM)
     hbm = pl.BlockSpec(memory_space=pl.ANY)
-    tok, heads, width = q_own.shape
-    out = jax.ShapeDtypeStruct((tok, heads, width), jnp.bfloat16)
-    stat = jax.ShapeDtypeStruct((tok, heads, BLOCK), jnp.float32)
+    tok, heads, width = q.shape
     return pl.pallas_call(
         attend_kernel,
-        out_shape=(out, out, stat, stat),
-        in_specs=[smem] * 4 + [hbm] * 2 + [vmem] * 4,
-        out_specs=(vmem,) * 4,
+        out_shape=(
+            jax.ShapeDtypeStruct((tok, heads, width), jnp.bfloat16),
+            jax.ShapeDtypeStruct((tok, heads, BLOCK), jnp.float32),
+        ),
+        in_specs=[smem] * 4 + [hbm] * 2 + [vmem] * 2 + [hbm],
+        out_specs=(vmem,) * 2,
         scratch_shapes=[
             pltpu.VMEM((SLOTS,) + own_kv.shape[1:], jnp.bfloat16),
             pltpu.SMEM((SLOTS,), jnp.int32),
             pltpu.SemaphoreType.DMA((SLOTS,)),
+            pltpu.VMEM((MAXB // GROUP, TILE * heads, GROUP * BLOCK), jnp.float32),
         ],
         compiler_params=pltpu.CompilerParams(vmem_limit_bytes=48 * 2**20),
         cost_estimate=pl.CostEstimate(
-            flops=9 * 10**9, bytes_accessed=12 * 2**20, transcendentals=4 * 2**20
+            flops=5 * 10**9, bytes_accessed=40 * 2**20, transcendentals=2 * 2**20
         ),
-        name="attend",
-    )(table, lengths, counts, where, own_kv, sib_kv, q_own, q_par, r_own, r_par)
+        name=name,
+    )(table, lengths, counts, where, own_kv, sib_kv, q, r, after)
 
 
 def finish_kernel(q_ref, r_ref, fresh_ref, fresh_rope_ref, ok_ref, oa, ob, sa, sb, out_ref):
@@ -261,20 +275,20 @@
 
 def row_place(i, sign):
     j = lax.rem(i * 37, SENDS)
+    sign = sign * (1 - 2 * lax.axis_index("core"))
     return shifted(lax.div(j, 16), lax.rem(lax.div(j, 4), 4), lax.rem(j, 4), sign)
 
 
 def block_place(i, sign):
-    j = lax.rem(i * 11, N_DP)
-    core = lax.axis_index("core")
-    dz = lax.rem(j, 2) * (1 + 2 * core)
-    return shifted(lax.div(j, 8), lax.rem(lax.div(j, 2), 4), dz, sign)
+    j = lax.rem(i * 15, N_DP)
+    sign = sign * (1 - 2 * lax.axis_index("core"))
+    return shifted(lax.div(j, 8), lax.rem(j, 4), lax.rem(lax.div(j, 4), 2), sign)
 
 
 def feed_kernel(
-    rows, cache, send, q, r, wg_hbm, wu_hbm, wd_hbm,
+    picks, hidden, latents, ropes, send, q, r, wg_hbm, wu_hbm, wd_hbm,
     own_kv, sib_kv, q_par, r_par, out,
-    wg, wu, wd, arr, arr_sib, stage, acts, part, part_sib, part_in,
+    rows, wg, wu, wd, arr, arr_sib, stage, acts, part, part_sib, part_in,
     w_sem, row_send, row_recv, fwd_send, fwd_recv, part_send, part_recv,
     kv_send, kv_recv, kvf_send, kvf_recv, misc_send, misc_recv,
 ):
@@ -297,6 +311,14 @@
 
     lax.fori_loop(1, SENDS, greet, 0)
     pl.semaphore_signal(barrier, inc=1, device_id=sibling, device_id_type=MESH)
+
+    def pick(n, carry):
+        cut = pl.ds(pl.multiple_of(n * 512, 512), 512)
+        value = jnp.dot(picks[...], hidden[:, cut], preferred_element_type=jnp.float32)
+        rows[:, :, cut] = value.astype(jnp.bfloat16).reshape(rows.shape[0], rows.shape[1], 512)
+        return carry
+
+    lax.fori_loop(0, hidden.shape[1] // 512, pick, 0)
     pl.semaphore_wait(barrier, SENDS)
 
     def remote(src, dst, send_sem, recv_sem, device):
@@ -342,14 +364,21 @@
     q_copy.start()
     r_copy.start()
 
+    def load_block(i, to):
+        index = send[0, to]
+        stage[i, :BLOCK] = latents[index]
+        rope = ropes[index]
+        for k in range(LAT // BLOCK):
+            stage[i, BLOCK:, k * BLOCK : (k + 1) * BLOCK] = rope[16 * k : 16 * (k + 1)]
+
     def start_blocks(i, carry):
         to, _ = block_place(i, 1)
-        stage[i] = cache[send[0, to]]
+        load_block(i, to)
         kv_copy(i).start()
         return carry
 
     lax.fori_loop(1, N_DP, start_blocks, 0)
-    stage[0] = cache[send[0, dp]]
+    load_block(0, dp)
     mine = pltpu.make_async_copy(stage.at[0], own_kv.at[dp], kv_send.at[0])
     mine.start()
     mine_fwd = remote(stage.at[0], sib_kv.at[dp], kvf_send.at[0], kvf_recv.at[0], sibling)
@@ -443,13 +472,16 @@
     r_copy.wait()
 
 
-def feed(rows, cache, send, q, r, wg, wu, wd):
+def feed(picks, hidden, latents, ropes, send, q, r, wg, wu, wd):
     smem = pl.BlockSpec(memory_space=pltpu.SMEM)
     vmem = pl.BlockSpec(memory_space=pltpu.VMEM)
     hbm = pl.BlockSpec(memory_space=pl.ANY)
     bf16 = jnp.bfloat16
-    blocks = jax.ShapeDtypeStruct((N_DP,) + cache.shape[1:], bf16)
-    chips = (SENDS,) + rows.shape[1:]
+    packed = BLOCK + ropes.shape[1] * BLOCK // LAT
+    blocks = jax.ShapeDtypeStruct((N_DP, packed, LAT), bf16)
+    capacity = picks.shape[0] // N_DP
+    width = hidden.shape[1]
+    chips = (SENDS, capacity, width)
     dma = pltpu.SemaphoreType.DMA
     chunks = SENDS // CHUNK
     return pl.pallas_call(
@@ -461,16 +493,17 @@
             jax.ShapeDtypeStruct(r.shape, bf16),
             jax.ShapeDtypeStruct(chips, bf16),
         ),
-        in_specs=[vmem, vmem, smem] + [hbm] * 5,
+        in_specs=[vmem] * 4 + [smem] + [hbm] * 5,
         out_specs=(hbm, hbm, hbm, hbm, vmem),
         scratch_shapes=[
+            pltpu.VMEM((N_DP, capacity, width), bf16),
             pltpu.VMEM(wg.shape, bf16),
             pltpu.VMEM(wu.shape, bf16),
             pltpu.VMEM(wd.shape, bf16),
             pltpu.VMEM(chips, bf16),
             pltpu.VMEM(chips, bf16),
             pltpu.VMEM(blocks.shape, bf16),
-            pltpu.VMEM((CHUNK * rows.shape[1], wg.shape[1]), bf16),
+            pltpu.VMEM((CHUNK * capacity, wg.shape[1]), bf16),
             pltpu.VMEM(chips, bf16),
             pltpu.VMEM(chips, bf16),
             pltpu.VMEM(chips, bf16),
@@ -487,7 +520,7 @@
             flops=11 * 10**9, bytes_accessed=24 * 2**20, transcendentals=2**19
         ),
         name="feed",
-    )(rows, cache, send, q, r, wg, wu, wd)
+    )(picks, hidden, latents, ropes, send, q, r, wg, wu, wd)
 
 
 def swap(value, axis):
@@ -519,28 +552,22 @@
     capacity = rows // 2
     slots = N_DP * capacity
 
-    flat_ids = expert_ids.reshape(-1)
-    onehot = (flat_ids[:, None] == jnp.arange(N_DP)[None, :]).astype(jnp.int32)
-    before = jnp.cumsum(onehot, axis=0) - onehot
-    target = flat_ids * capacity + jnp.sum(before * onehot, axis=1)
-    match = (target[:, None] == jnp.arange(slots)[None, :]).astype(jnp.float32)
-    picks = jnp.sum(match.reshape(rows, fan_count, slots), axis=1)
-    weights = jnp.sum(
-        (match * gate_vals.reshape(-1)[:, None]).reshape(rows, fan_count, slots), axis=1
+    experts = jnp.arange(N_DP, dtype=jnp.int32)
+    named = expert_ids.T[:, None, :] == experts[None, :, None]
+    hits = jnp.any(named, axis=0)
+    before = jnp.cumsum(hits.astype(jnp.int32), axis=1) - hits
+    picked = hits[:, None, :] & (
+        before[:, None, :] == jnp.arange(capacity, dtype=jnp.int32)[None, :, None]
     )
-    outgoing = lax.dot_general(
-        picks.astype(jnp.bfloat16),
+    picks = picked.astype(jnp.bfloat16).reshape(slots, rows)
+    gates = jnp.sum(jnp.where(named, gate_vals.T[:, None, :], 0.0), axis=0)
+    weights = jnp.where(picked, gates[:, None, :], 0.0).reshape(slots, rows)
+
+    own_kv, sib_kv, q_par, r_par, partial = feed(
+        picks,
         hidden_in,
-        (((0,), (0,)), ((), ())),
-        preferred_element_type=jnp.float32,
-    ).astype(jnp.bfloat16)
-    packed = jnp.concatenate(
-        [cache_rope[:, 16 * k : 16 * (k + 1), :] for k in range(LAT // BLOCK)], axis=2
-    )
-    cache = jnp.concatenate([cache_latent, packed], axis=1)
-    own_kv, sib_kv, q_par, r_par, partial = feed(
-        outgoing.reshape(N_DP, capacity, width),
-        cache,
+        cache_latent,
+        cache_rope,
         send_index,
         q_latent,
         q_rope,
@@ -560,9 +587,10 @@
     summed = jnp.sum(
         returned.reshape(N_DP, 2, capacity, width), axis=1, dtype=jnp.float32
     ).reshape(slots, width)
-    mixed = jnp.dot(
+    mixed = lax.dot_general(
         weights,
         summed,
+        (((0,), (0,)), ((), ())),
         precision=lax.Precision.HIGHEST,
         preferred_element_type=jnp.float32,
     )
@@ -585,20 +613,11 @@
     quad = jnp.where(zh == 0, quad, quad[::-1]).reshape(TOK, LAT + ROPE)
 
     where = jnp.stack([zh, core, lax.axis_index("dp") % 2]).astype(jnp.int32)
-    o_own, o_par, s_own, s_par = attend(
-        block_table.reshape(1, CHATS * MAXB),
-        cached_len,
-        new_counts,
-        where,
-        own_kv,
-        sib_kv,
-        q_latent,
-        q_par,
-        r_own,
-        r_par,
-    )
+    facts = (block_table.reshape(1, CHATS * MAXB), cached_len, new_counts, where, own_kv, sib_kv)
+    o_par, s_par = attend(*facts, q_par, r_par, q_latent, "attend_partner")
     o_back = swap(o_par, "zh")
     s_back = swap(s_par[:, :, 0], "zh")
+    o_own, s_own = attend(*facts, q_latent, r_own, o_par, "attend_own")
     s_back = jnp.broadcast_to(s_back[:, :, None], s_own.shape)
     tokens = jnp.arange(TOK, dtype=jnp.int32)
     ends = jnp.cumsum(counts)

time: 267 us -> 217 us (0.81)
  Pallas kernels: 186 us -> 152 us
  starting transfers between devices: 26.9 us -> 14.8 us
  local copies, waits for them, and re-layouts: 7.51 us -> 3.03 us
  waiting for transfers between devices: 26.4 us -> 29.3 us
    pallas_call x1 -> x2, Pallas kernels: 63.9 us -> 33.8 us  [attend(): pl.pallas_call(attend_kernel, out_shape=(jax.ShapeDtypeStruct((tok, heads...]
    all_to_all x1, starting transfers between devices: 22.1 us -> 9.44 us  [shards(): lax.all_to_all(partial, ('dp', 'zh'), split_axis=0, concat_axis=0, tiled=...]
    unnamed x34 -> x38, local copies, waits for them, and re-layouts: 4.75 us -> 1.09 us
    ppermute x4, waiting for transfers between devices: 26.4 us -> 29.3 us  [swap(): return lax.ppermute(value, axis, [(0, 1), (1, 0)])]
    pallas_call x1, Pallas kernels: 118 us -> 115 us  [feed(): pl.pallas_call(feed_kernel, out_shape=(blocks, blocks, jax.ShapeDtypeStru...]
  transfers between devices with their start and end apart: 5 -> 5, of which waited for: 3 -> 3; matrix products, arithmetic and copies ran while one was open for 4% -> 6% of each run, Pallas kernels for 24% -> 16%
where the time goes in v3:
time: 217 us; the launch traced here: 214 us
  Pallas kernels  152 us (70%)
  waiting for transfers between devices  29.3 us (14%)
  starting transfers between devices  14.8 us (7%)
  other arithmetic  7.85 us (4%)
  matrix products  5.21 us (2%)
  local copies, waits for them, and re-layouts  3.03 us (1%)
    pallas_call x1, Pallas kernels, feed(): pl.pallas_call(feed_kernel, out_shape=(blocks, blocks, jax.ShapeDtypeStru...  115 us
    pallas_call x2, Pallas kernels, attend(): pl.pallas_call(attend_kernel, out_shape=(jax.ShapeDtypeStruct((tok, heads...  33.8 us
    ppermute x4, waiting for transfers between devices, swap(): return lax.ppermute(value, axis, [(0, 1), (1, 0)])  29.3 us
    all_to_all x1, starting transfers between devices, shards(): lax.all_to_all(partial, ('dp', 'zh'), split_axis=0, concat_axis=0, tiled=...  9.44 us
    ppermute x4, starting transfers between devices, swap(): return lax.ppermute(value, axis, [(0, 1), (1, 0)])  5.37 us
  transfers between devices with their start and end apart: 5, of which 3 were waited for; matrix products, arithmetic and copies ran while one was open for 6% of the time, Pallas kernels for 16%

profile of v3, /device:TPU:23, one launch (start us, length us, event | category | flops | bytes accessed | tf_op | source)
XLA Modules:
  0.0 213.6 jit_solution(7768574842670179138)
XLA Ops:
  0.6 0.8 fusion.6
  1.9 0.7 fusion.4.picks
  2.6 115.0 %feed.1 = (bf16[32,144,512]{2,1,0:T(8,128)(2,1)}, bf16[32,144,512]{2,1,0:T(8,128)(2,1)}, bf16[64,16,512]{2,1,0:T(8,128)(2,1)}, bf16[64,1024]{1,0:T(8,128)(2,1)}, bf16[64,8,3584]{2,1,0:T(8,128)(2,1)}) custom-call(bf16[256,16]{1,0:T(8,128)(2,1)} %fusion.4.picks, bf16[16,3584]{1,0:T(8,128)(2,1)} %hidden.1, bf16[8,128,512]{2,1,0:T(8,128)(2,1)} %latents.1, ...), custom_call_target="tpu_custom_call" | custom-call | flops 11000000512 | bytes 25165824 | tf_op jit(solution)/shard_map/feed/pallas_call | solution.py:487
  117.7 9.4 %all-to-all-start = ((bf16[64,8,3584]{2,1,0:T(8,128)(2,1)}), bf16[64,8,3584]{2,1,0:T(8,128)(2,1)}, u32[]{:S(2)}, u32[]{:S(2)}) async-start(bf16[64,8,3584]{2,1,0:T(8,128)(2,1)} %get-tuple-element.13), calls=%async_computation | async-start | bytes 7340032 | tf_op jit(solution)/shard_map/all_to_all | solution.py:580
  127.6 17.4 %attend_partner.1 = (bf16[64,16,512]{2,1,0:T(8,128)(2,1)}, f32[64,16,128]{2,1,0:T(8,128)S(1)}) custom-call(s32[1,128]{1,0:T(1,128)S(1)} %reshape.88.table, s32[1,4]{1,0:T(1,128)S(1)} %copy-done.4, s32[1,4]{1,0:T(1,128)S(1)} %copy-done.5, s32[3]{0:T(128)S(1)} %pad_add_fusion.where, bf16[32,144,512]{2,1,0:T(8,128)(2,1)} %get-tuple-element.14.own_kv, ...), custom_call_target="tpu_custom_call" | custom-call | flops 5000000000 | bytes 41943040 | tf_op jit(solution)/shard_map/attend_partner/pallas_call | solution.py:196
  144.9 3.9 %collective-permute-start.2 = (bf16[64,16,512]{2,1,0:T(8,128)(2,1)}, bf16[64,16,512]{2,1,0:T(8,128)(2,1)S(1)}, u32[]{:S(2)}, u32[]{:S(2)}) collective-permute-start(bf16[64,16,512]{2,1,0:T(8,128)(2,1)} %get-tuple-element.18.after), channel_id=1, source_target_pairs={{0,2},{2,0},{1,3},{3,1},{4,6},{6,4},{5,7},{7,5},{8,10},{10,8},{9,1... | collective-permute-start | bytes 3145736 | tf_op jit(solution)/shard_map/ppermute | solution.py:527
  148.8 0.3 copy.43
  149.3 0.2 reduce-window.4
  149.9 0.5 add_convert_fusion
  150.5 16.4 %attend_own.1 = (bf16[64,16,512]{2,1,0:T(8,128)(2,1)S(1)}, f32[64,16,128]{2,1,0:T(8,128)S(1)}) custom-call(s32[1,128]{1,0:T(1,128)S(1)} %reshape.88.table, s32[1,4]{1,0:T(1,128)S(1)} %copy-done.4, s32[1,4]{1,0:T(1,128)S(1)} %copy-done.5, s32[3]{0:T(128)S(1)} %pad_add_fusion.where, bf16[32,144,512]{2,1,0:T(8,128)(2,1)} %get-tuple-element.14.own_kv, ...), custom_call_target="tpu_custom_call" | custom-call | flops 5000000000 | bytes 41943040 | tf_op jit(solution)/shard_map/attend_own/pallas_call | solution.py:196
  167.0 1.0 copy-done.2
  167.9 0.5 multiply_power_fusion
  168.5 25.2 %collective-permute-done.3 = f32[64,16]{0,1:T(8,128)} collective-permute-done((f32[64,16]{0,1:T(8,128)S(1)}, f32[64,16]{0,1:T(8,128)}, u32[]{:S(2)}, u32[]{:S(2)}) %collective-permute-start.3) | collective-permute-done | bytes 4128 | tf_op jit(solution)/shard_map/ppermute | solution.py:527
  193.7 0.8 copy.44
  194.5 3.2 %convert_reduce_fusion = f32[32,8,3584]{2,1,0:T(8,128)S(1)} fusion(bf16[64,8,3584]{2,1,0:T(8,128)(2,1)} %all-to-all-done), kind=kLoop, calls=%fused_computation | loop fusion | flops 2752512 | bytes 7340032 | tf_op jit(solution)/shard_map/reduce_sum | solution.py:587
  197.8 4.3 %fusion.1 = bf16[16,3584]{1,0:T(8,128)(2,1)S(1)} fusion(f32[32,8,3584]{2,1,0:T(8,128)S(1)} %convert_reduce_fusion, bf16[16,3584]{1,0:T(8,128)(2,1)S(1)} %copy-done.12, f32[32,16]{0,1:T(8,128)S(1)} %select_reduce_fusion, s32[32,16]{0,1:T(8,128)S(1)} %copy.39, pred[32,16]{0,1:T(8,128)(4,1)S(1)} %fusion.6), kind=kOutput, calls=%fused_computation.3 | convolution fusion | flops 176345088 | bytes 3904000 | tf_op jit(solution)/shard_map/dot_general | solution.py:590
  202.1 0.7 multiply_reduce_fusion
  202.8 0.2 fusion.26
  203.5 1.0 collective-permute-start
  204.5 0.7 pad_maximum_fusion.3
  205.3 0.5 collective-permute-start.1
  205.8 4.0 %collective-permute-done.1 = bf16[2,16,576]{2,1,0:T(8,128)(2,1)S(1)} collective-permute-done((bf16[2,16,576]{2,1,0:T(8,128)(2,1)S(1)}, bf16[2,16,576]{2,1,0:T(8,128)(2,1)S(1)}, u32[]{:S(2)}, u32[]{:S(2)}) %collective-permute-start.1) | collective-permute-done | bytes 36896 | tf_op jit(solution)/shard_map/ppermute | solution.py:527
  209.9 0.2 broadcast_in_dim.30.sb
  210.1 3.6 %finish.1 = bf16[64,16,512]{2,1,0:T(8,128)(2,1)} custom-call(bf16[64,16,512]{2,1,0:T(8,128)(2,1)S(1)} %copy-done.1, bf16[64,16,64]{2,1,0:T(8,128)(2,1)S(1)} %reshape.86.r_ref, bf16[64,512]{1,0:T(8,128)(2,1)S(1)} %slice.22.fresh_ref, bf16[64,64]{1,0:T(8,128)(2,1)S(1)} %slice.23.fresh_rope_ref, f32[64,64]{1,0:T(8,128)S(1)} %fusion.13.ok_ref, ...), custom_call_target="tpu_custom_call" | custom-call | tf_op jit(solution)/shard_map/finish/pallas_call | solution.py:253
  (71 shorter events, 2.2 us)
Async XLA Ops:
  0.6 202.2 %copy-start = (bf16[3584,64]{0,1:T(8,128)(2,1)S(1)}, bf16[3584,64]{0,1:T(8,128)(2,1)}, u32[]{:S(2)}) copy-start(bf16[3584,64]{0,1:T(8,128)(2,1)} %param.24) | copy-start | bytes 1376260
  117.6 9.5 %copy-start.11 = (bf16[64,1024]{1,0:T(8,128)(2,1)S(1)}, bf16[64,1024]{1,0:T(8,128)(2,1)}, u32[]{:S(2)}) copy-start(bf16[64,1024]{1,0:T(8,128)(2,1)} %get-tuple-element.17) | copy-start | bytes 393220
  117.6 9.7 %copy-start.16 = (s32[1,4,32]{2,1,0:T(4,128)S(1)}, s32[1,4,32]{2,1,0:T(4,128)}, u32[]{:S(2)}) copy-start(s32[1,4,32]{2,1,0:T(4,128)} %param.29) | copy-start | bytes 1540
  117.6 9.9 %copy-start.1 = (bf16[64,16,512]{2,1,0:T(8,128)(2,1)S(1)}, bf16[64,16,512]{2,1,0:T(8,128)(2,1)}, u32[]{:S(2)}) copy-start(bf16[64,16,512]{2,1,0:T(8,128)(2,1)} %q_ref.3) | copy-start | bytes 3145732
  117.6 9.9 %copy-start.4 = (s32[1,4]{1,0:T(1,128)S(1)}, s32[1,4]{1,0:T(1,128)}, u32[]{:S(2)}) copy-start(s32[1,4]{1,0:T(1,128)} %lengths.3) | copy-start | bytes 52
  117.7 9.9 %copy-start.5 = (s32[1,4]{1,0:T(1,128)S(1)}, s32[1,4]{1,0:T(1,128)}, u32[]{:S(2)}) copy-start(s32[1,4]{1,0:T(1,128)} %counts.3) | copy-start | bytes 52
  117.7 9.8 %copy-start.6 = (bf16[64,16,512]{2,1,0:T(8,128)(2,1)S(1)}, bf16[64,16,512]{2,1,0:T(8,128)(2,1)}, u32[]{:S(2)}) copy-start(bf16[64,16,512]{2,1,0:T(8,128)(2,1)} %get-tuple-element.16.q_ref) | copy-start | bytes 3145732
  117.7 76.8 %all-to-all-start = ((bf16[64,8,3584]{2,1,0:T(8,128)(2,1)}), bf16[64,8,3584]{2,1,0:T(8,128)(2,1)}, u32[]{:S(2)}, u32[]{:S(2)}) async-start(bf16[64,8,3584]{2,1,0:T(8,128)(2,1)} %get-tuple-element.13), calls=%async_computation | async-start | bytes 7340032 | tf_op jit(solution)/shard_map/all_to_all | solution.py:580
  127.5 21.6 %copy-start.10 = (bf16[64,1024]{1,0:T(8,128)(2,1)S(1)}, bf16[64,1024]{1,0:T(8,128)(2,1)}, u32[]{:S(2)}) copy-start(bf16[64,1024]{1,0:T(8,128)(2,1)} %r.1) | copy-start | bytes 393220
  127.5 22.2 %copy-start.13 = (s32[16,8]{0,1:T(8,128)S(1)}, s32[16,8]{0,1:T(8,128)}, u32[]{:S(2)}) copy-start(s32[16,8]{0,1:T(8,128)} %param.18) | copy-start | bytes 1540
  127.5 22.2 %copy-start.14 = (f32[16,8]{0,1:T(8,128)S(1)}, f32[16,8]{0,1:T(8,128)}, u32[]{:S(2)}) copy-start(f32[16,8]{0,1:T(8,128)} %param.19) | copy-start | bytes 1540
  144.9 64.9 %collective-permute-start.2 = (bf16[64,16,512]{2,1,0:T(8,128)(2,1)}, bf16[64,16,512]{2,1,0:T(8,128)(2,1)S(1)}, u32[]{:S(2)}, u32[]{:S(2)}) collective-permute-start(bf16[64,16,512]{2,1,0:T(8,128)(2,1)} %get-tuple-element.18.after), channel_id=1, source_target_pairs={{0,2},{2,0},{1,3},{3,1},{4,6},{6,4},{5,7},{7,5},{8,10},{10,8},{9,1... | collective-permute-start | bytes 3145736 | tf_op jit(solution)/shard_map/ppermute | solution.py:527
  149.1 44.6 %collective-permute-start.3 = (f32[64,16]{0,1:T(8,128)S(1)}, f32[64,16]{0,1:T(8,128)}, u32[]{:S(2)}, u32[]{:S(2)}) collective-permute-start(f32[64,16]{0,1:T(8,128)S(1)} %bitcast.56), channel_id=1, source_target_pairs={{0,2},{2,0},{1,3},{3,1},{4,6},{6,4},{5,7},{7,5},{8,10},{10,8},{9,1... | collective-permute-start | bytes 12296 | tf_op jit(solution)/shard_map/ppermute | solution.py:527
  167.0 1.0 copy-start.2
  194.5 3.3 %copy-start.12 = (bf16[16,3584]{1,0:T(8,128)(2,1)S(1)}, bf16[16,3584]{1,0:T(8,128)(2,1)}, u32[]{:S(2)}) copy-start(bf16[16,3584]{1,0:T(8,128)(2,1)} %hidden.1) | copy-start | bytes 344068
  197.7 4.4 %copy-start.7 = (bf16[3584,512]{1,0:T(8,128)(2,1)S(1)}, bf16[3584,512]{1,0:T(8,128)(2,1)}, u32[]{:S(2)}) copy-start(bf16[3584,512]{1,0:T(8,128)(2,1)} %param.23) | copy-start | bytes 11010052
  197.8 5.3 %copy-start.15 = (f32[512]{0:T(512)S(1)}, f32[512]{0:T(512)}, u32[]{:S(2)}) copy-start(f32[512]{0:T(512)} %param.25) | copy-start | bytes 6148
  197.8 5.4 %copy-start.17 = (f32[16]{0:T(128)S(1)}, f32[16]{0:T(128)}, u32[]{:S(2)}) copy-start(f32[16]{0:T(128)} %add_convert_fusion) | copy-start | bytes 196
  197.8 5.4 %copy-start.18 = (f32[32]{0:T(128)S(1)}, f32[32]{0:T(128)}, u32[]{:S(2)}) copy-start(f32[32]{0:T(128)} %multiply_power_fusion) | copy-start | bytes 388
  202.1 11.5 %copy-start.8 = (bf16[16,3584]{1,0:T(8,128)(2,1)}, bf16[16,3584]{1,0:T(8,128)(2,1)S(1)}, u32[]{:S(2)}) copy-start(bf16[16,3584]{1,0:T(8,128)(2,1)S(1)} %fusion.1) | copy-start | bytes 344068
  202.1 7.9 %copy-start.3 = (bf16[64,16,512]{2,1,0:T(8,128)(2,1)S(1)}, bf16[64,16,512]{2,1,0:T(8,128)(2,1)}, u32[]{:S(2)}) copy-start(bf16[64,16,512]{2,1,0:T(8,128)(2,1)} %copy-done.2) | copy-start | bytes 3145732
  203.2 10.4 %copy-start.9 = (bf16[16,512]{1,0:T(8,128)(2,1)}, bf16[16,512]{1,0:T(8,128)(2,1)S(1)}, u32[]{:S(2)}) copy-start(bf16[16,512]{1,0:T(8,128)(2,1)S(1)} %multiply_convert_fusion) | copy-start | bytes 49156
  203.5 1.8 collective-permute-start
  205.3 4.4 %collective-permute-start.1 = (bf16[2,16,576]{2,1,0:T(8,128)(2,1)S(1)}, bf16[2,16,576]{2,1,0:T(8,128)(2,1)S(1)}, u32[]{:S(2)}, u32[]{:S(2)}) collective-permute-start(bf16[2,16,576]{2,1,0:T(8,128)(2,1)S(1)} %reverse_select_fusion.1), channel_id=1, source_target_pairs={{0,2},{2,0},{1,3},{3,1},{4,6},{6,4},{5,7},{7,5},{8,10},{10,8},{9,1... | collective-permute-start | bytes 110600 | tf_op jit(solution)/shard_map/ppermute | solution.py:527

commit v4 on v3

v4 whole, which is shorter than its diff:
```python
import functools

import jax
import jax.numpy as jnp
from jax import lax
from jax.experimental import pallas as pl
from jax.experimental.pallas import tpu as pltpu
from jax.sharding import Mesh
from jax.sharding import PartitionSpec as P

SCORE_SCALE = 192.0 ** (-0.5)
LOG2E = 1.4426950408889634
ROPE_BASE = 10000.0
NORM_EPS = 1e-06
BIG = -1e30

N_DP = 32
CHATS = 4
MAXB = 32
BLOCK = 128
LAT = 512
ROPE = 64
TOK = 64
HEADS_DEV = 16
GROUP = 4
TILE = 16
SLOTS = 2 * N_DP + CHATS * (GROUP - 1) + 2


def chat_positions(counts, lengths, local):
    ends = jnp.cumsum(counts)
    chat_of = jnp.sum((local[:, None] >= ends[None, :]).astype(jnp.int32), axis=1)
    starts = ends - counts
    onehot = (chat_of[:, None] == jnp.arange(counts.shape[0])[None, :]).astype(jnp.int32)
    return jnp.sum(onehot * (lengths - starts)[None, :], axis=1) + local


def attend_kernel(
    table, lengths, counts, where, kv, q_ref, r_ref, after,
    o_ref, s_ref, held, place, sems, scores,
):
    zh, core, low = where[0], where[1], where[2]
    heads = q_ref.shape[1]
    rows = TILE * heads

    def copy_in(source, slot):
        return pltpu.make_async_copy(kv.at[source], held.at[slot], sems.at[slot])

    def fetch(holder, slot):
        source = lax.shift_right_logical(holder, 2) + ((holder & 1) ^ core) * N_DP
        copy_in(source, slot).start()

    def list_blocks(chat, begin):
        length = lengths[0, chat]

        def step(j, carry):
            slot, last = carry
            holder = table[0, chat * MAXB + j]
            z = (lax.shift_right_logical(holder, 1) & 1) * 2 + (
                lax.shift_right_logical(holder, 2) & 1
            )
            step_z = jnp.where((z & 1) == low, 0, 1 + 2 * (holder & 1))
            mine = lax.shift_right_logical((z + step_z) & 3, 1) == zh

            @pl.when(mine)
            def _():
                place[slot] = jnp.clip(length - j * BLOCK, 0, BLOCK)
                fetch(holder, slot)

            return jnp.where(mine, slot + 1, slot), jnp.where(mine, holder, last)

        count = lax.shift_right_logical(length + BLOCK - 1, 7)
        slot, last = lax.fori_loop(0, count, step, (begin, jnp.int32(0)))
        pad = lax.rem(GROUP - lax.rem(slot, GROUP), GROUP)

        def fill(i, carry):
            place[carry] = 0
            fetch(last, carry)
            return carry + 1

        return lax.fori_loop(0, pad, fill, slot)

    def arrive(i, carry):
        copy_in(0, i).wait()
        return carry

    begins = [jnp.int32(0)]
    begins.append(list_blocks(0, begins[0]))
    start = jnp.int32(0)
    lane = lax.broadcasted_iota(jnp.int32, (1, BLOCK), 1)
    contract = (((1,), (1,)), ((), ()))
    for chat in range(CHATS):
        if chat + 1 < CHATS:
            begins.append(list_blocks(chat + 1, begins[chat + 1]))
        count = counts[0, chat]
        first_group = lax.div(begins[chat], GROUP)
        n_groups = lax.div(begins[chat + 1] - begins[chat], GROUP)
        lax.fori_loop(begins[chat], begins[chat + 1], arrive, 0)

        def tile(t, carry):
            base = jnp.minimum(start + t * TILE, TOK - TILE)
            ql = q_ref[pl.ds(base, TILE)].reshape(rows, LAT)
            qr = r_ref[pl.ds(base, TILE)].reshape(rows, ROPE)

            def keys_of(g):
                at = (first_group + g) * GROUP
                blocks = [held[at + i] for i in range(GROUP)]
                return blocks, jnp.concatenate([b[:BLOCK] for b in blocks], axis=0)

            def score(g, best):
                blocks, keys = keys_of(g)
                ropes = jnp.concatenate(
                    [
                        jnp.concatenate(
                            [b[BLOCK:, k * BLOCK : (k + 1) * BLOCK] for k in range(LAT // BLOCK)],
                            axis=0,
                        )
                        for b in blocks
                    ],
                    axis=1,
                )
                at = (first_group + g) * GROUP
                valid = jnp.concatenate([lane < place[at + i] for i in range(GROUP)], axis=1)
                s = lax.dot_general(ql, keys, contract, preferred_element_type=jnp.float32)
                s = s + jnp.dot(qr, ropes, preferred_element_type=jnp.float32)
                s = jnp.where(valid, s * (SCORE_SCALE * LOG2E), BIG)
                scores[g] = s
                for i in range(GROUP):
                    best = jnp.maximum(best, s[:, i * BLOCK : (i + 1) * BLOCK])
                return best

            def blend(g, state, top):
                total, acc = state
                _, keys = keys_of(g)
                p = jnp.exp2(scores[g] - top)
                for i in range(GROUP):
                    total = total + p[:, i * BLOCK : (i + 1) * BLOCK]
                acc = acc + jnp.dot(p.astype(jnp.bfloat16), keys, preferred_element_type=jnp.float32)
                return total, acc

            def over(step, state):
                def two(g, state):
                    return step(2 * g + 1, step(2 * g, state))

                state = lax.fori_loop(0, lax.div(n_groups, 2), two, state)
                return lax.fori_loop(n_groups - lax.rem(n_groups, 2), n_groups, step, state)

            best = over(score, jnp.full((rows, BLOCK), BIG, jnp.float32))
            top = jnp.max(best, axis=1, keepdims=True)
            total, acc = over(
                lambda g, state: blend(g, state, top),
                (jnp.zeros((rows, BLOCK), jnp.float32), jnp.zeros((rows, LAT), jnp.float32)),
            )
            total = jnp.sum(total, axis=1, keepdims=True)
            token = base + lax.broadcasted_iota(jnp.int32, (TILE, 1, 1), 0)
            keep = (token >= start) & (token < start + count)
            some = total > 0.0
            safe = jnp.where(some, total, 1.0)
            value = (acc / safe).astype(jnp.bfloat16).reshape(TILE, heads, LAT)
            lse = jnp.where(some, top + jnp.log2(safe), BIG)
            lse = jnp.broadcast_to(lse, (rows, BLOCK)).reshape(TILE, heads, BLOCK)
            at = pl.ds(base, TILE)
            o_ref[at] = jnp.where(keep, value, o_ref[at])
            s_ref[at] = jnp.where(keep, lse, s_ref[at])
            return carry

        lax.fori_loop(0, lax.div(count + TILE - 1, TILE), tile, 0)
        start = start + count


def attend(table, lengths, counts, where, kv, q, r, after, name):
    smem = pl.BlockSpec(memory_space=pltpu.SMEM)
    vmem = pl.BlockSpec(memory_space=pltpu.VMEM)
    hbm = pl.BlockSpec(memory_space=pl.ANY)
    tok, heads, width = q.shape
    return pl.pallas_call(
        attend_kernel,
        out_shape=(
            jax.ShapeDtypeStruct((tok, heads, width), jnp.bfloat16),
            jax.ShapeDtypeStruct((tok, heads, BLOCK), jnp.float32),
        ),
        in_specs=[smem] * 4 + [hbm] + [vmem] * 2 + [hbm],
        out_specs=(vmem,) * 2,
        scratch_shapes=[
            pltpu.VMEM((SLOTS,) + kv.shape[1:], jnp.bfloat16),
            pltpu.SMEM((SLOTS,), jnp.int32),
            pltpu.SemaphoreType.DMA((SLOTS,)),
            pltpu.VMEM((MAXB // GROUP, TILE * heads, GROUP * BLOCK), jnp.float32),
        ],
        compiler_params=pltpu.CompilerParams(vmem_limit_bytes=48 * 2**20),
        cost_estimate=pl.CostEstimate(
            flops=5 * 10**9, bytes_accessed=40 * 2**20, transcendentals=2 * 2**20
        ),
        name=name,
    )(table, lengths, counts, where, kv, q, r, after)


MESH = pl.DeviceIdType.MESH
AXES = ("plane", "zl", "zh", "core")
SENDS = 2 * N_DP
CHUNK = 32
ROW_ORDER = (
    0, 42, 46, 21, 11, 33, 58, 31, 49, 59, 45, 13, 47, 10, 32, 6,
    27, 34, 8, 35, 9, 51, 39, 5, 55, 52, 18, 56, 50, 24, 37, 3,
    40, 2, 44, 14, 36, 15, 53, 61, 28, 30, 63, 23, 43, 22, 48, 7,
    41, 54, 29, 20, 1, 60, 62, 57, 17, 12, 19, 4, 16, 26, 38, 25,
)
BLOCK_ORDER = (
    0, 22, 18, 29, 25, 15, 11, 4, 27, 13, 31, 14, 28, 26, 21, 3,
    19, 1, 12, 9, 5, 23, 10, 24, 7, 8, 6, 16, 2, 20, 30, 17,
)


def place_of():
    return tuple(lax.axis_index(name) for name in AXES)


def shifted(dy, dx, dz, sign):
    plane, zl, zh, _ = place_of()
    y = lax.rem(lax.div(plane, 4) + 4 + sign * dy, 4)
    x = lax.rem(lax.rem(plane, 4) + 4 + sign * dx, 4)
    z = lax.rem(zh * 2 + zl + 4 + sign * dz, 4)
    return y * 4 + x, lax.rem(z, 2), lax.div(z, 2)


def row_place_of(j):
    return shifted(lax.div(j, 16), lax.rem(lax.div(j, 4), 4), lax.rem(j, 4), 1)


def row_place(j, sign):
    sign = sign * (1 - 2 * lax.axis_index("core"))
    return shifted(j // 16, j // 4 % 4, j % 4, sign)


def block_place(j, sign):
    sign = sign * (1 - 2 * lax.axis_index("core"))
    return shifted(j // 8, j % 4, j // 4 % 2, sign)


def feed_kernel(
    picks, hidden, latents, ropes, send, q, r, wg_hbm, wu_hbm, wd_hbm, mine_w,
    kv, q_par, r_par, out, near_w,
    rows, wg, wu, wd, arr, arr_sib, stage, acts, part, part_sib, part_in,
    w_sem, row_send, row_recv, fwd_send, fwd_recv, part_send, part_recv,
    kv_send, kv_recv, kvf_send, kvf_recv, misc_send, misc_recv,
):
    plane, zl, zh, core = place_of()
    dp, z = plane * 2 + zl, zh * 2 + zl
    sibling = (plane, zl, zh, 1 - core)
    partner = (plane, zl, 1 - zh, core)
    loads = [
        pltpu.make_async_copy(a, b, w_sem.at[i])
        for i, (a, b) in enumerate(((wg_hbm, wg), (wu_hbm, wu), (wd_hbm, wd)))
    ]
    for load in loads:
        load.start()

    barrier = pltpu.get_barrier_semaphore()

    def greet(i, carry):
        to = row_place_of(i)
        pl.semaphore_signal(barrier, inc=1, device_id=(*to, core), device_id_type=MESH)
        return carry

    lax.fori_loop(1, SENDS, greet, 0)
    pl.semaphore_signal(barrier, inc=1, device_id=sibling, device_id_type=MESH)

    def pick(n, carry):
        cut = pl.ds(pl.multiple_of(n * 512, 512), 512)
        value = lax.dot_general(
            picks[...],
            hidden[:, cut],
            (((0,), (0,)), ((), ())),
            preferred_element_type=jnp.float32,
        )
        rows[:, :, cut] = value.astype(jnp.bfloat16).reshape(rows.shape[0], rows.shape[1], 512)
        return carry

    lax.fori_loop(0, hidden.shape[1] // 512, pick, 0)
    pl.semaphore_wait(barrier, SENDS)

    def remote(src, dst, send_sem, recv_sem, device):
        return pltpu.make_async_remote_copy(
            src_ref=src, dst_ref=dst, send_sem=send_sem, recv_sem=recv_sem,
            device_id=device, device_id_type=MESH,
        )

    def row_copy(i, to=(0, 0, 0)):
        source = rows.at[to[1] * (N_DP // 2) + to[0]]
        return remote(source, arr.at[i], row_send.at[i], row_recv.at[i], (*to, core))

    def fwd_copy(i):
        return remote(arr.at[i], arr_sib.at[i], fwd_send.at[i], fwd_recv.at[i], sibling)

    def part_copy(c):
        at = pl.ds(c * CHUNK, CHUNK)
        return remote(
            part_sib.at[at], part_in.at[at], part_send.at[c], part_recv.at[c], sibling
        )

    def kv_copy(i, to=(0, 0, 0)):
        return remote(
            stage.at[i], kv.at[dp], kv_send.at[i], kv_recv.at[i], (*to, core)
        )

    def kvf_copy(i, source=0):
        return remote(
            kv.at[source], kv.at[N_DP + source], kvf_send.at[i], kvf_recv.at[i], sibling
        )

    for i in range(1, SENDS):
        row_copy(i, row_place(ROW_ORDER[i], 1)).start()
    arr[0] = rows[zl * (N_DP // 2) + plane]

    q_copy = remote(q, q_par, misc_send.at[0], misc_recv.at[0], partner)
    r_copy = remote(r, r_par, misc_send.at[1], misc_recv.at[1], partner)
    q_copy.start()
    r_copy.start()

    def weight_copy(dz):
        to = shifted(0, 0, dz, 1)
        return remote(
            mine_w.at[to[1]], near_w.at[z], misc_send.at[1 + dz], misc_recv.at[1 + dz], (*to, core)
        )

    for dz in (1, 2, 3):
        weight_copy(dz).start()
    near_w[z] = mine_w[zl]

    def load_block(i, to):
        index = send[0, to]
        stage[i, :BLOCK] = latents[index]
        rope = ropes[index]
        for k in range(LAT // BLOCK):
            stage[i, BLOCK:, k * BLOCK : (k + 1) * BLOCK] = rope[16 * k : 16 * (k + 1)]

    for i in range(1, N_DP):
        to = block_place(BLOCK_ORDER[i], 1)
        load_block(i, to[0] * 2 + to[1])
        kv_copy(i, to).start()
    load_block(0, dp)
    mine = pltpu.make_async_copy(stage.at[0], kv.at[dp], kv_send.at[0])
    mine.start()
    mine_fwd = remote(stage.at[0], kv.at[N_DP + dp], kvf_send.at[0], kvf_recv.at[0], sibling)
    mine_fwd.start()
    for load in loads:
        load.wait()

    def experts(source, target, c):
        at = pl.ds(c * CHUNK, CHUNK)
        x = source[at].reshape(CHUNK * source.shape[1], source.shape[2])
        for n in range(2):
            cut = slice(n * 256, (n + 1) * 256)
            gate = jnp.dot(x, wg[:, cut], preferred_element_type=jnp.float32)
            lifted = jnp.dot(x, wu[:, cut], preferred_element_type=jnp.float32)
            acts[:, cut] = (gate / (1.0 + jnp.exp(-gate)) * lifted).astype(jnp.bfloat16)

        def down(n, carry):
            cut = pl.ds(pl.multiple_of(n * 512, 512), 512)
            value = jnp.dot(acts[...], wd[:, cut], preferred_element_type=jnp.float32)
            target[at, :, cut] = value.astype(jnp.bfloat16).reshape(CHUNK, source.shape[1], 512)
            return carry

        lax.fori_loop(0, source.shape[2] // 512, down, 0)

    def chunk(c, carry):
        first = c * CHUNK

        def pass_on(i, carry):
            @pl.when(i > 0)
            def _():
                row_copy(i).wait_recv()

            fwd_copy(i).start()
            return carry

        lax.fori_loop(first, first + CHUNK, pass_on, 0)
        experts(arr, part, c)

        def await_sib(i, carry):
            fwd_copy(i).wait_recv()
            return carry

        lax.fori_loop(first, first + CHUNK, await_sib, 0)
        experts(arr_sib, part_sib, c)
        part_copy(c).start()
        return carry

    lax.fori_loop(0, SENDS // CHUNK, chunk, 0)

    for i in range(1, N_DP):
        kv_copy(i).wait_recv()
        source = block_place(BLOCK_ORDER[i], -1)
        kvf_copy(i, source[0] * 2 + source[1]).start()

    for i in range(SENDS):
        if i % CHUNK == 0:
            part_copy(i // CHUNK).wait()
        source = row_place(ROW_ORDER[i], -1)
        total = part[i].astype(jnp.float32) + part_in[i].astype(jnp.float32)
        out[source[0] * 4 + source[2] * 2 + source[1]] = total.astype(jnp.bfloat16)

    def end_rows(i, carry):
        row_copy(i).wait_send()
        return carry

    lax.fori_loop(1, SENDS, end_rows, 0)

    def end_fwd(i, carry):
        fwd_copy(i).wait_send()
        return carry

    lax.fori_loop(0, SENDS, end_fwd, 0)

    def end_blocks(i, carry):
        kv_copy(i).wait_send()
        kvf_copy(i).wait()
        return carry

    lax.fori_loop(1, N_DP, end_blocks, 0)
    mine.wait()
    mine_fwd.wait()
    q_copy.wait()
    r_copy.wait()
    for dz in (1, 2, 3):
        weight_copy(dz).wait()


def feed(picks, hidden, latents, ropes, send, q, r, wg, wu, wd, weights):
    smem = pl.BlockSpec(memory_space=pltpu.SMEM)
    vmem = pl.BlockSpec(memory_space=pltpu.VMEM)
    hbm = pl.BlockSpec(memory_space=pl.ANY)
    bf16 = jnp.bfloat16
    packed = BLOCK + ropes.shape[1] * BLOCK // LAT
    blocks = jax.ShapeDtypeStruct((2 * N_DP, packed, LAT), bf16)
    capacity = picks.shape[1] // N_DP
    width = hidden.shape[1]
    chips = (SENDS, capacity, width)
    dma = pltpu.SemaphoreType.DMA
    chunks = SENDS // CHUNK
    return pl.pallas_call(
        feed_kernel,
        out_shape=(
            blocks,
            jax.ShapeDtypeStruct(q.shape, bf16),
            jax.ShapeDtypeStruct(r.shape, bf16),
            jax.ShapeDtypeStruct(chips, bf16),
            jax.ShapeDtypeStruct((4,) + weights.shape[1:], bf16),
        ),
        in_specs=[vmem] * 4 + [smem] + [hbm] * 5 + [vmem],
        out_specs=(hbm, hbm, hbm, vmem, vmem),
        scratch_shapes=[
            pltpu.VMEM((N_DP, capacity, width), bf16),
            pltpu.VMEM(wg.shape, bf16),
            pltpu.VMEM(wu.shape, bf16),
            pltpu.VMEM(wd.shape, bf16),
            pltpu.VMEM(chips, bf16),
            pltpu.VMEM(chips, bf16),
            pltpu.VMEM((N_DP, packed, LAT), bf16),
            pltpu.VMEM((CHUNK * capacity, wg.shape[1]), bf16),
            pltpu.VMEM(chips, bf16),
            pltpu.VMEM(chips, bf16),
            pltpu.VMEM(chips, bf16),
            dma((3,)),
            dma((SENDS,)), dma((SENDS,)), dma((SENDS,)), dma((SENDS,)),
            dma((chunks,)), dma((chunks,)),
            dma((N_DP,)), dma((N_DP,)), dma((N_DP,)), dma((N_DP,)),
            dma((5,)), dma((5,)),
        ],
        compiler_params=pltpu.CompilerParams(
            collective_id=1, has_side_effects=True, vmem_limit_bytes=56 * 2**20
        ),
        cost_estimate=pl.CostEstimate(
            flops=11 * 10**9, bytes_accessed=24 * 2**20, transcendentals=2**19
        ),
        name="feed",
    )(picks, hidden, latents, ropes, send, q, r, wg, wu, wd, weights)


def close_kernel(
    returned_hbm, w_lat_hbm, q_hbm, r_hbm, oa_hbm, ob_hbm, sa_hbm, sb_hbm,
    near_w, hidden, w_rope_ref, w_turn_ref, gain, cosine, sine, ok_ref,
    hidden_out, new_latent, new_rope, out_ref,
    returned, w_lat, q_ref, r_ref, oa, ob, sa, sb,
    sums, sums_out, inbox, fresh, load_sem, sum_send, sum_recv, fresh_send, fresh_recv,
):
    plane, zl, zh, core = place_of()
    z = zh * 2 + zl
    pool = zh * 2 + core
    heads = q_ref.shape[1]
    rows, width = hidden.shape
    loads = [
        pltpu.make_async_copy(a, b, load_sem.at[i])
        for i, (a, b) in enumerate(
            (
                (returned_hbm, returned), (w_lat_hbm, w_lat), (q_hbm, q_ref), (r_hbm, r_ref),
                (oa_hbm, oa), (ob_hbm, ob), (sa_hbm, sa), (sb_hbm, sb),
            )
        )
    ]
    for load in loads:
        load.start()
    column = [(*shifted(0, 0, dz, 1), core) for dz in (1, 2, 3)]
    others = [(plane, zl, zh, 1 - core), (plane, zl, 1 - zh, core), (plane, zl, 1 - zh, 1 - core)]
    barrier = pltpu.get_barrier_semaphore()
    for device in column + [others[0], others[2]]:
        pl.semaphore_signal(barrier, inc=1, device_id=device, device_id_type=MESH)
    pl.semaphore_wait(barrier, 5)
    loads[0].wait()

    def add(at):
        weights = near_w[at]

        for n in range(width // 512):
            cut = slice(n * 512, (n + 1) * 512)
            x = returned[:, at, :, cut].reshape(weights.shape[1], 512)
            both = jnp.dot(weights, x, preferred_element_type=jnp.float32)
            total = both[:rows] + both[rows:]
            sums[at, :, cut] = total
            sums_out[at, :, cut] = total.astype(jnp.bfloat16)

    def sum_copy(dz):
        to = lax.rem(z + dz, 4)
        return pltpu.make_async_remote_copy(
            src_ref=sums_out.at[to], dst_ref=inbox.at[dz - 1],
            send_sem=sum_send.at[dz - 1], recv_sem=sum_recv.at[dz - 1],
            device_id=column[dz - 1], device_id_type=MESH,
        )

    for dz in (2, 1, 3):
        add(lax.rem(z + dz, 4))
        sum_copy(dz).start()
    add(z)
    for dz in (1, 2, 3):
        sum_copy(dz).wait()

    total = hidden[...].astype(jnp.float32) + sums[z]
    for i in range(3):
        total = total + inbox[i].astype(jnp.float32)
    x = total.astype(jnp.bfloat16)
    hidden_out[...] = x
    loads[1].wait()
    latent = jnp.dot(x, w_lat[...], preferred_element_type=jnp.float32)
    plain = jnp.dot(x, w_rope_ref[...], preferred_element_type=jnp.float32)
    turned = jnp.dot(x, w_turn_ref[...], preferred_element_type=jnp.float32)
    scale = lax.rsqrt(jnp.mean(latent * latent, axis=1, keepdims=True) + NORM_EPS)
    latent = (latent * scale * gain[...]).astype(jnp.bfloat16)
    rope = (plain * cosine[...] + turned * sine[...]).astype(jnp.bfloat16)
    new_latent[...] = latent
    new_rope[...] = rope
    blank = jnp.zeros((rows, BLOCK - ROPE), jnp.bfloat16)
    fresh[pool] = jnp.concatenate([latent, rope, blank], axis=1)

    def fresh_copy(i):
        return pltpu.make_async_remote_copy(
            src_ref=fresh.at[pool], dst_ref=fresh.at[pool],
            send_sem=fresh_send.at[i], recv_sem=fresh_recv.at[i],
            device_id=others[i], device_id_type=MESH,
        )

    for i in range(3):
        fresh_copy(i).start()
    for load in loads[2:]:
        load.wait()
    for i in range(3):
        fresh_copy(i).wait()

    contract = (((1,), (1,)), ((), ()))
    keys = fresh[...].reshape(TOK, LAT + BLOCK)
    lat_keys = keys[:, :LAT]
    rope_keys = keys[:, LAT : LAT + ROPE]

    def tile(t, carry):
        at = pl.ds(t * TILE, TILE)
        size = TILE * heads
        s = lax.dot_general(
            q_ref[at].reshape(size, LAT), lat_keys, contract, preferred_element_type=jnp.float32
        ) + lax.dot_general(
            r_ref[at].reshape(size, ROPE), rope_keys, contract, preferred_element_type=jnp.float32
        )
        ok = ok_ref[at]
        ok = jnp.broadcast_to(ok[:, None, :], (TILE, heads, TOK)).reshape(size, TOK)
        s = jnp.where(ok > 0.0, s * (SCORE_SCALE * LOG2E), BIG)
        la = sa[at].reshape(size, BLOCK)[:, :1]
        lb = sb[at].reshape(size, BLOCK)[:, :1]
        m = jnp.maximum(jnp.maximum(la, lb), jnp.max(s, axis=1, keepdims=True))
        p = jnp.where(ok > 0.0, jnp.exp2(s - m), 0.0)
        wa = jnp.exp2(la - m)
        wb = jnp.exp2(lb - m)
        weight = wa + wb + jnp.sum(p, axis=1, keepdims=True)
        mixed = jnp.dot(p.astype(jnp.bfloat16), lat_keys, preferred_element_type=jnp.float32)
        mixed = mixed + wa * oa[at].reshape(size, LAT).astype(jnp.float32)
        mixed = mixed + wb * ob[at].reshape(size, LAT).astype(jnp.float32)
        out_ref[at] = (mixed / weight).astype(jnp.bfloat16).reshape(TILE, heads, LAT)
        return carry

    lax.fori_loop(0, TOK // TILE, tile, 0)


def close(large, small):
    vmem = pl.BlockSpec(memory_space=pltpu.VMEM)
    hbm = pl.BlockSpec(memory_space=pl.ANY)
    q, hidden = large[2], small[1]
    rows, width = hidden.shape
    bf16 = jnp.bfloat16
    dma = pltpu.SemaphoreType.DMA
    return pl.pallas_call(
        close_kernel,
        out_shape=(
            jax.ShapeDtypeStruct(hidden.shape, bf16),
            jax.ShapeDtypeStruct((rows, LAT), bf16),
            jax.ShapeDtypeStruct((rows, ROPE), bf16),
            jax.ShapeDtypeStruct(q.shape, bf16),
        ),
        in_specs=[hbm] * len(large) + [vmem] * len(small),
        out_specs=(vmem,) * 4,
        scratch_shapes=[
            *(pltpu.VMEM(a.shape, a.dtype) for a in large),
            pltpu.VMEM((4, rows, width), jnp.float32),
            pltpu.VMEM((4, rows, width), bf16),
            pltpu.VMEM((3, rows, width), bf16),
            pltpu.VMEM((4, rows, LAT + BLOCK), bf16),
            dma((len(large),)),
            dma((3,)), dma((3,)),
            dma((3,)), dma((3,)),
        ],
        compiler_params=pltpu.CompilerParams(
            collective_id=2, has_side_effects=True, vmem_limit_bytes=48 * 2**20
        ),
        name="close",
    )(*large, *small)


def swap(value, axis):
    return lax.ppermute(value, axis, [(0, 1), (1, 0)])


def shards(
    hidden_in,
    expert_ids,
    gate_vals,
    w_gate,
    w_up,
    w_down,
    w_latent,
    w_rope,
    latent_gain,
    cache_latent,
    cache_rope,
    send_index,
    block_table,
    cached_len,
    new_counts,
    q_latent,
    q_rope,
):
    _, zl, zh, core = place_of()
    rows, width = hidden_in.shape
    capacity = rows // 2

    turn = jnp.arange(N_DP, dtype=jnp.int32)
    experts = turn % (N_DP // 2) * 2 + turn // (N_DP // 2)
    named = expert_ids[:, :, None] == experts[None, None, :]
    hits = jnp.any(named, axis=1)
    before = jnp.cumsum(hits.astype(jnp.int32), axis=0) - hits
    picked = hits[:, :, None] & (
        before[:, :, None] == jnp.arange(capacity, dtype=jnp.int32)[None, None, :]
    )
    picks = picked.astype(jnp.bfloat16).reshape(rows, N_DP * capacity)
    gates = jnp.sum(jnp.where(named, gate_vals[:, :, None], 0.0), axis=1)
    weights = jnp.where(picked, gates[:, :, None], 0.0).reshape(rows, 2, -1)
    high = weights.astype(jnp.bfloat16)
    low = (weights - high.astype(jnp.float32)).astype(jnp.bfloat16)
    split = jnp.concatenate([high, low], axis=0).transpose(1, 0, 2)

    kv, q_par, r_par, partial, near_w = feed(
        picks,
        hidden_in,
        cache_latent,
        cache_rope,
        send_index,
        q_latent,
        q_rope,
        w_gate[0],
        w_up[0],
        w_down[0],
        split,
    )
    r_own = q_rope.reshape(TOK, HEADS_DEV, ROPE)
    r_par = r_par.reshape(TOK, HEADS_DEV, ROPE)
    returned = lax.all_to_all(partial, "plane", split_axis=0, concat_axis=0, tiled=True)

    where = jnp.stack([zh, core, zl]).astype(jnp.int32)
    facts = (block_table.reshape(1, CHATS * MAXB), cached_len, new_counts, where, kv)
    o_par, s_par = attend(*facts, q_par, r_par, q_latent, "attend_partner")
    o_back = swap(o_par, "zh")
    s_back = swap(s_par[:, :, 0], "zh")
    o_own, s_own = attend(*facts, q_latent, r_own, o_par, "attend_own")
    s_back = jnp.broadcast_to(s_back[:, :, None], s_own.shape)
    counts = new_counts[0]
    local = (zh * 2 + core) * rows + jnp.arange(rows, dtype=jnp.int32)
    positions = chat_positions(counts, cached_len[0], local)
    half = ROPE // 2
    exponent = jnp.arange(half).astype(jnp.float32) * (-2.0 / ROPE)
    frequency = jnp.power(jnp.float32(ROPE_BASE), exponent)
    angle = positions.astype(jnp.float32)[:, None] * frequency[None, :]
    cosine = jnp.tile(jnp.cos(angle), (1, 2))
    sine = jnp.tile(jnp.sin(angle), (1, 2))
    w_turn = jnp.concatenate([-w_rope[:, half:], w_rope[:, :half]], axis=1)
    tokens = jnp.arange(TOK, dtype=jnp.int32)
    ends = jnp.cumsum(counts)
    chat_of = jnp.sum((tokens[:, None] >= ends[None, :]).astype(jnp.int32), axis=1)
    ok = (chat_of[:, None] == chat_of[None, :]) & (tokens[None, :] <= tokens[:, None])
    return close(
        (
            returned.reshape(N_DP // 2, 4, capacity, width),
            w_latent,
            q_latent,
            r_own,
            o_own,
            o_back,
            s_own,
            s_back,
        ),
        (
            near_w,
            hidden_in,
            w_rope,
            w_turn,
            latent_gain[None, :],
            cosine,
            sine,
            ok.astype(jnp.float32),
        ),
    )


def solution(mesh):
    whole = Mesh(mesh.devices.reshape(N_DP // 2, 2, 2, 2), AXES)
    every = AXES
    dp = ("plane", "zl")
    pool = ("zh", "core")
    return jax.shard_map(
        shards,
        mesh=whole,
        in_specs=(
            P(every, None),
            P(every, None),
            P(every, None),
            P(dp, None, pool),
            P(dp, None, pool),
            P(dp, pool, None),
            P(),
            P(),
            P(),
            P(every, None, None),
            P(every, None, None),
            P(every, None),
            P(dp, None, None),
            P(dp, None),
            P(dp, None),
            P(dp, pool, None),
            P(dp, pool),
        ),
        out_specs=(
            P(every, None),
            P(every, None),
            P(every, None),
            P(dp, pool, None),
        ),
        check_vma=False,
    )
```

time: 217 us -> 207 us (0.954)
  local copies, waits for them, and re-layouts: 3.03 us -> 9.64 us
  waiting for transfers between devices: 29.3 us -> 23.9 us
  matrix products: 5.21 us -> 0 us
  other arithmetic: 7.85 us -> 3.12 us
  starting transfers between devices: 14.8 us -> 11.8 us
    ppermute x4 -> x2, waiting for transfers between devices: 29.3 us -> 8.8 us  [swap(): return lax.ppermute(value, axis, [(0, 1), (1, 0)])]
    pallas_call x2, Pallas kernels: 119 us -> 134 us  [the longest x1 116 us: feed(): pl.pallas_call(feed_kernel, out_shape=(blocks, jax.ShapeDtypeStruct(q.sha...]
    all_to_all x1, waiting for transfers between devices: 0.01 us -> 15.1 us  [shards(): lax.all_to_all(partial, 'plane', split_axis=0, concat_axis=0, tiled=True)]
    pallas_call x2, Pallas kernels: 33.8 us -> 20.6 us  [attend(): pl.pallas_call(attend_kernel, out_shape=(jax.ShapeDtypeStruct((tok, heads...]
    unnamed x38 -> x35, local copies, waits for them, and re-layouts: 1.09 us -> 7.63 us
    dot_general x3 -> x0, matrix products: 5.21 us -> none  [the longest x1 4.31 us: shards(): lax.dot_general(weights, summed, (((0,), (0,)), ((), ())), precision=lax....]
    reduce_sum x2 -> x1, other arithmetic: 3.34 us -> 0.11 us  [shards(): gates = jnp.sum(jnp.where(named, gate_vals[:, :, None], 0.0), axis=1)]
    ppermute x4 -> x2, starting transfers between devices: 5.37 us -> 3.96 us  [swap(): return lax.ppermute(value, axis, [(0, 1), (1, 0)])]
  transfers between devices with their start and end apart: 5 -> 3, of which waited for: 3 -> 2; matrix products, arithmetic and copies ran while one was open for 6% -> 1% of each run, Pallas kernels for 16% -> 10%
where the time goes in v4:
time: 207 us; the launch traced here: 204 us
  Pallas kernels  154 us (74%)
  waiting for transfers between devices  23.9 us (12%)
  starting transfers between devices  11.8 us (6%)
  local copies, waits for them, and re-layouts  9.64 us (5%)
  other arithmetic  3.12 us (2%)
    pallas_call x1, Pallas kernels, feed(): pl.pallas_call(feed_kernel, out_shape=(blocks, jax.ShapeDtypeStruct(q.sha...  116 us
    pallas_call x2, Pallas kernels, attend(): pl.pallas_call(attend_kernel, out_shape=(jax.ShapeDtypeStruct((tok, heads...  20.6 us
    pallas_call x1, Pallas kernels, close(): pl.pallas_call(close_kernel, out_shape=(jax.ShapeDtypeStruct(hidden.shape...  17.7 us
    all_to_all x1, waiting for transfers between devices, shards(): lax.all_to_all(partial, 'plane', split_axis=0, concat_axis=0, tiled=True)  15.1 us
    ppermute x2, waiting for transfers between devices, swap(): return lax.ppermute(value, axis, [(0, 1), (1, 0)])  8.8 us
    all_to_all x1, starting transfers between devices, shards(): lax.all_to_all(partial, 'plane', split_axis=0, concat_axis=0, tiled=True)  7.88 us
    unnamed x35, local copies, waits for them, and re-layouts  7.63 us
  transfers between devices with their start and end apart: 3, of which 2 were waited for; matrix products, arithmetic and copies ran while one was open for 1% of the time, Pallas kernels for 10%

profile of v4, /device:TPU:23, one launch (start us, length us, event | category | flops | bytes accessed | tf_op | source)
XLA Modules:
  0.0 203.7 jit_solution(7286233101194664677)
XLA Ops:
  0.6 0.8 copy.40
  1.9 0.8 copy.47
  3.4 0.6 maximum_bitcast_fusion.mine_w
  4.0 0.6 and_convert_fusion.picks
  4.6 116.0 %feed.1 = (bf16[64,144,512]{2,1,0:T(8,128)(2,1)}, bf16[64,16,512]{2,1,0:T(8,128)(2,1)}, bf16[64,1024]{1,0:T(8,128)(2,1)}, bf16[64,8,3584]{2,1,0:T(8,128)(2,1)}, bf16[4,32,128]{2,1,0:T(8,128)(2,1)}) custom-call(bf16[16,256]{1,0:T(8,128)(2,1)} %and_convert_fusion.picks, bf16[16,3584]{1,0:T(8,128)(2,1)} %hidden.3, bf16[8,128,512]{2,1,0:T(8,128)(2,1)} %latents.1, ...), custom_call_target="tpu_custom_call" | custom-call | flops 11000000512 | bytes 25165824 | tf_op jit(solution)/shard_map/feed/pallas_call | solution.py:441
  120.6 7.9 %all-to-all-start = ((bf16[64,8,3584]{2,1,0:T(8,128)(2,1)}), bf16[64,8,3584]{2,1,0:T(8,128)(2,1)}, u32[]{:S(2)}, u32[]{:S(2)}) async-start(bf16[64,8,3584]{2,1,0:T(8,128)(2,1)} %get-tuple-element.13), calls=%async_computation | async-start | bytes 7340032 | tf_op jit(solution)/shard_map/all_to_all | solution.py:691
  128.9 10.7 %attend_partner.1 = (bf16[64,16,512]{2,1,0:T(8,128)(2,1)}, f32[64,16,128]{2,1,0:T(8,128)S(1)}) custom-call(s32[1,128]{1,0:T(1,128)S(1)} %reshape.159.table, s32[1,4]{1,0:T(1,128)S(1)} %copy-done.7, s32[1,4]{1,0:T(1,128)S(1)} %copy-done.8, s32[3]{0:T(128)S(1)} %pad_add_fusion.where, bf16[64,144,512]{2,1,0:T(8,128)(2,1)} %get-tuple-element.14.kv, ...), custom_call_target="tpu_custom_call" | custom-call | flops 5000000000 | bytes 41943040 | tf_op jit(solution)/shard_map/attend_partner/pallas_call | solution.py:176
  139.6 3.9 %collective-permute-start = (bf16[64,16,512]{2,1,0:T(8,128)(2,1)}, bf16[64,16,512]{2,1,0:T(8,128)(2,1)}, u32[]{:S(2)}, u32[]{:S(2)}) collective-permute-start(bf16[64,16,512]{2,1,0:T(8,128)(2,1)} %get-tuple-element.17.after), channel_id=1, source_target_pairs={{0,2},{2,0},{1,3},{3,1},{4,6},{6,4},{5,7},{7,5},{8,10},{10,8},{9,1... | collective-permute-start | bytes 3145736 | tf_op jit(solution)/shard_map/ppermute | solution.py:635
  143.6 0.3 copy.50
  144.3 0.4 copy.54.w_rope_ref
  145.1 0.4 slice_negate_fusion
  145.5 9.9 %attend_own.1 = (bf16[64,16,512]{2,1,0:T(8,128)(2,1)S(1)}, f32[64,16,128]{2,1,0:T(8,128)S(1)}) custom-call(s32[1,128]{1,0:T(1,128)S(1)} %reshape.159.table, s32[1,4]{1,0:T(1,128)S(1)} %copy-done.7, s32[1,4]{1,0:T(1,128)S(1)} %copy-done.8, s32[3]{0:T(128)S(1)} %pad_add_fusion.where, bf16[64,144,512]{2,1,0:T(8,128)(2,1)} %get-tuple-element.14.kv, ...), custom_call_target="tpu_custom_call" | custom-call | flops 5000000000 | bytes 41943040 | tf_op jit(solution)/shard_map/attend_own/pallas_call | solution.py:176
  155.4 1.0 copy-done.1
  156.4 0.8 copy-done.2
  157.2 0.5 pad_maximum_fusion.w_turn_ref
  158.0 8.8 %collective-permute-done.1 = f32[64,16]{0,1:T(8,128)S(1)} collective-permute-done((f32[64,16]{0,1:T(8,128)S(1)}, f32[64,16]{0,1:T(8,128)S(1)}, u32[]{:S(2)}, u32[]{:S(2)}) %collective-permute-start.1) | collective-permute-done | bytes 4128 | tf_op jit(solution)/shard_map/ppermute | solution.py:635
  166.9 15.1 %all-to-all-done = bf16[64,8,3584]{2,1,0:T(8,128)(2,1)} async-done(((bf16[64,8,3584]{2,1,0:T(8,128)(2,1)}), bf16[64,8,3584]{2,1,0:T(8,128)(2,1)}, u32[]{:S(2)}, u32[]{:S(2)}) %all-to-all-start) | async-done | bytes 3670048 | tf_op jit(solution)/shard_map/all_to_all | solution.py:691
  181.9 0.2 broadcast_in_dim.35.sb_hbm
  182.2 1.0 copy-done.3
  183.2 17.7 %close.1 = (bf16[16,3584]{1,0:T(8,128)(2,1)S(1)}, bf16[16,512]{1,0:T(8,128)(2,1)S(1)}, bf16[16,64]{1,0:T(8,128)(2,1)S(1)}, bf16[64,16,512]{2,1,0:T(8,128)(2,1)S(1)}) custom-call(bf16[16,4,8,3584]{3,2,1,0:T(8,128)(2,1)} %bitcast.9.returned_hbm, bf16[3584,512]{1,0:T(8,128)(2,1)} %w_lat_hbm.1, bf16[64,16,512]{2,1,0:T(8,128)(2,1)S(1)} %copy-done, ...), custom_call_target="tpu_custom_call" | custom-call | tf_op jit(solution)/shard_map/close/pallas_call | solution.py:607
  200.9 0.6 copy.59
  201.6 0.6 copy.60
  202.2 0.6 copy.61
  202.8 1.0 copy.62
  (71 shorter events, 2.7 us)
Async XLA Ops:
  120.6 7.9 %copy-start.12 = (bf16[64,1024]{1,0:T(8,128)(2,1)S(1)}, bf16[64,1024]{1,0:T(8,128)(2,1)}, u32[]{:S(2)}) copy-start(bf16[64,1024]{1,0:T(8,128)(2,1)} %get-tuple-element.16) | copy-start | bytes 393220
  120.6 8.1 %copy-start.13 = (s32[1,4,32]{2,1,0:T(4,128)S(1)}, s32[1,4,32]{2,1,0:T(4,128)}, u32[]{:S(2)}) copy-start(s32[1,4,32]{2,1,0:T(4,128)} %param.29) | copy-start | bytes 1540
  120.6 8.3 %copy-start = (bf16[64,16,512]{2,1,0:T(8,128)(2,1)S(1)}, bf16[64,16,512]{2,1,0:T(8,128)(2,1)}, u32[]{:S(2)}) copy-start(bf16[64,16,512]{2,1,0:T(8,128)(2,1)} %q_hbm.1) | copy-start | bytes 3145732
  120.6 8.3 %copy-start.7 = (s32[1,4]{1,0:T(1,128)S(1)}, s32[1,4]{1,0:T(1,128)}, u32[]{:S(2)}) copy-start(s32[1,4]{1,0:T(1,128)} %lengths.3) | copy-start | bytes 52
  120.6 8.3 %copy-start.8 = (s32[1,4]{1,0:T(1,128)S(1)}, s32[1,4]{1,0:T(1,128)}, u32[]{:S(2)}) copy-start(s32[1,4]{1,0:T(1,128)} %counts.3) | copy-start | bytes 52
  120.6 8.3 %copy-start.9 = (bf16[64,16,512]{2,1,0:T(8,128)(2,1)S(1)}, bf16[64,16,512]{2,1,0:T(8,128)(2,1)}, u32[]{:S(2)}) copy-start(bf16[64,16,512]{2,1,0:T(8,128)(2,1)} %get-tuple-element.15.q_ref) | copy-start | bytes 3145732
  120.6 61.3 %all-to-all-start = ((bf16[64,8,3584]{2,1,0:T(8,128)(2,1)}), bf16[64,8,3584]{2,1,0:T(8,128)(2,1)}, u32[]{:S(2)}, u32[]{:S(2)}) async-start(bf16[64,8,3584]{2,1,0:T(8,128)(2,1)} %get-tuple-element.13), calls=%async_computation | async-start | bytes 7340032 | tf_op jit(solution)/shard_map/all_to_all | solution.py:691
  128.9 15.0 %copy-start.11 = (bf16[64,1024]{1,0:T(8,128)(2,1)S(1)}, bf16[64,1024]{1,0:T(8,128)(2,1)}, u32[]{:S(2)}) copy-start(bf16[64,1024]{1,0:T(8,128)(2,1)} %r.1) | copy-start | bytes 393220
  128.9 15.3 %copy-start.10 = (bf16[3584,64]{0,1:T(8,128)(2,1)S(1)}, bf16[3584,64]{0,1:T(8,128)(2,1)}, u32[]{:S(2)}) copy-start(bf16[3584,64]{0,1:T(8,128)(2,1)} %param.24) | copy-start | bytes 1376260
  139.6 27.2 %collective-permute-start = (bf16[64,16,512]{2,1,0:T(8,128)(2,1)}, bf16[64,16,512]{2,1,0:T(8,128)(2,1)}, u32[]{:S(2)}, u32[]{:S(2)}) collective-permute-start(bf16[64,16,512]{2,1,0:T(8,128)(2,1)} %get-tuple-element.17.after), channel_id=1, source_target_pairs={{0,2},{2,0},{1,3},{3,1},{4,6},{6,4},{5,7},{7,5},{8,10},{10,8},{9,1... | collective-permute-start | bytes 3145736 | tf_op jit(solution)/shard_map/ppermute | solution.py:635
  143.8 23.0 %collective-permute-start.1 = (f32[64,16]{0,1:T(8,128)S(1)}, f32[64,16]{0,1:T(8,128)S(1)}, u32[]{:S(2)}, u32[]{:S(2)}) collective-permute-start(f32[64,16]{0,1:T(8,128)S(1)} %bitcast.35), channel_id=1, source_target_pairs={{0,2},{2,0},{1,3},{3,1},{4,6},{6,4},{5,7},{7,5},{8,10},{10,8},{9,1... | collective-permute-start | bytes 12296 | tf_op jit(solution)/shard_map/ppermute | solution.py:635
  145.4 36.7 %copy-start.4 = (bf16[16,3584]{1,0:T(8,128)(2,1)S(1)}, bf16[16,3584]{1,0:T(8,128)(2,1)}, u32[]{:S(2)}) copy-start(bf16[16,3584]{1,0:T(8,128)(2,1)} %hidden.3) | copy-start | bytes 344068
  145.5 36.7 %copy-start.5 = (bf16[4,32,128]{2,1,0:T(8,128)(2,1)S(1)}, bf16[4,32,128]{2,1,0:T(8,128)(2,1)}, u32[]{:S(2)}) copy-start(bf16[4,32,128]{2,1,0:T(8,128)(2,1)} %get-tuple-element.21.near_w) | copy-start | bytes 98308
  145.5 36.7 %copy-start.6 = (f32[512]{0:T(512)S(1)}, f32[512]{0:T(512)}, u32[]{:S(2)}) copy-start(f32[512]{0:T(512)} %param.25) | copy-start | bytes 6148
  155.4 1.0 copy-start.1
  156.4 0.8 copy-start.2
  182.2 1.0 copy-start.3

commit v5 on v4

--- a/solution.py
+++ b/solution.py
@@ -215,37 +215,47 @@
     return tuple(lax.axis_index(name) for name in AXES)
 
 
-def shifted(dy, dx, dz, sign):
+def neighbours():
     plane, zl, zh, _ = place_of()
-    y = lax.rem(lax.div(plane, 4) + 4 + sign * dy, 4)
-    x = lax.rem(lax.rem(plane, 4) + 4 + sign * dx, 4)
-    z = lax.rem(zh * 2 + zl + 4 + sign * dz, 4)
-    return y * 4 + x, lax.rem(z, 2), lax.div(z, 2)
-
-
-def row_place_of(j):
-    return shifted(lax.div(j, 16), lax.rem(lax.div(j, 4), 4), lax.rem(j, 4), 1)
-
-
-def row_place(j, sign):
-    sign = sign * (1 - 2 * lax.axis_index("core"))
-    return shifted(j // 16, j // 4 % 4, j % 4, sign)
-
-
-def block_place(j, sign):
-    sign = sign * (1 - 2 * lax.axis_index("core"))
-    return shifted(j // 8, j % 4, j // 4 % 2, sign)
+    y, x, z = lax.div(plane, 4), lax.rem(plane, 4), zh * 2 + zl
+    ys = [lax.rem(y + d, 4) * 4 for d in range(4)]
+    xs = [lax.rem(x + d, 4) for d in range(4)]
+    zs = [lax.rem(z + d, 4) for d in range(4)]
+    lows, highs = [lax.rem(v, 2) for v in zs], [lax.div(v, 2) for v in zs]
+
+    def shifted(dy, dx, dz):
+        return ys[dy % 4] + xs[dx % 4], lows[dz % 4], highs[dz % 4]
+
+    return shifted
+
+
+def facing(shifted, core):
+    def either(dy, dx, dz, sign):
+        ahead = shifted(sign * dy, sign * dx, sign * dz)
+        back = shifted(-sign * dy, -sign * dx, -sign * dz)
+        return tuple(a + core * (b - a) for a, b in zip(ahead, back))
+
+    return either
 
 
 def feed_kernel(
-    picks, hidden, latents, ropes, send, q, r, wg_hbm, wu_hbm, wd_hbm, mine_w,
+    ids, gate_vals, hidden, latents, ropes, send, q, r, wg_hbm, wu_hbm, wd_hbm,
     kv, q_par, r_par, out, near_w,
-    rows, wg, wu, wd, arr, arr_sib, stage, acts, part, part_sib, part_in,
+    rows, mine_w, wg, wu, wd, arr, arr_sib, stage, acts, part, part_sib, part_in,
     w_sem, row_send, row_recv, fwd_send, fwd_recv, part_send, part_recv,
     kv_send, kv_recv, kvf_send, kvf_recv, misc_send, misc_recv,
 ):
     plane, zl, zh, core = place_of()
     dp, z = plane * 2 + zl, zh * 2 + zl
+    shifted = neighbours()
+    either = facing(shifted, core)
+
+    def row_place(j, sign):
+        return either(j // 16, j // 4 % 4, j % 4, sign)
+
+    def block_place(j, sign):
+        return either(j // 8, j % 4, j // 4 % 2, sign)
+
     sibling = (plane, zl, zh, 1 - core)
     partner = (plane, zl, 1 - zh, core)
     loads = [
@@ -257,22 +267,45 @@
 
     barrier = pltpu.get_barrier_semaphore()
 
-    def greet(i, carry):
-        to = row_place_of(i)
-        pl.semaphore_signal(barrier, inc=1, device_id=(*to, core), device_id_type=MESH)
-        return carry
-
-    lax.fori_loop(1, SENDS, greet, 0)
+    for j in range(1, SENDS):
+        to = (*shifted(j // 16, j // 4 % 4, j % 4), core)
+        pl.semaphore_signal(barrier, inc=1, device_id=to, device_id_type=MESH)
     pl.semaphore_signal(barrier, inc=1, device_id=sibling, device_id_type=MESH)
+
+    fan, count = ids.shape
+    capacity = rows.shape[1]
+    slots = N_DP * capacity
+    slot = lax.broadcasted_iota(jnp.int32, (slots, count), 0)
+    turn = lax.div(slot, capacity)
+    half = N_DP // 2
+    expert = lax.rem(turn, half) * 2 + lax.div(turn, half)
+    hits = jnp.zeros((slots, count), jnp.float32)
+    gates = jnp.zeros((slots, count), jnp.float32)
+    for k in range(fan):
+        same = ids[k : k + 1, :] == expert
+        hits = hits + jnp.where(same, 1.0, 0.0)
+        gates = gates + jnp.where(same, gate_vals[k : k + 1, :], 0.0)
+    line = lax.broadcasted_iota(jnp.int32, (count, count), 0)
+    across = lax.broadcasted_iota(jnp.int32, (count, count), 1)
+    earlier = jnp.where(line < across, 1.0, 0.0).astype(jnp.bfloat16)
+    before = jnp.dot(hits.astype(jnp.bfloat16), earlier, preferred_element_type=jnp.float32)
+    wanted = lax.rem(slot, capacity).astype(jnp.float32)
+    picked = jnp.where(before == wanted, hits, 0.0)
+    picks = picked.astype(jnp.bfloat16)
+    weight = picked * gates
+    high = weight.astype(jnp.bfloat16)
+    low = (weight - high.astype(jnp.float32)).astype(jnp.bfloat16)
+    unit = jnp.where(line == across, 1.0, 0.0).astype(jnp.bfloat16)
+    turned = (((1,), (1,)), ((), ()))
+    for side in range(2):
+        at = slice(side * slots // 2, (side + 1) * slots // 2)
+        for i, term in enumerate((high, low)):
+            value = lax.dot_general(unit, term[at], turned, preferred_element_type=jnp.float32)
+            mine_w[side, i * count : (i + 1) * count] = value.astype(jnp.bfloat16)
 
     def pick(n, carry):
         cut = pl.ds(pl.multiple_of(n * 512, 512), 512)
-        value = lax.dot_general(
-            picks[...],
-            hidden[:, cut],
-            (((0,), (0,)), ((), ())),
-            preferred_element_type=jnp.float32,
-        )
+        value = jnp.dot(picks, hidden[:, cut], preferred_element_type=jnp.float32)
         rows[:, :, cut] = value.astype(jnp.bfloat16).reshape(rows.shape[0], rows.shape[1], 512)
         return carry
 
@@ -318,7 +351,7 @@
     r_copy.start()
 
     def weight_copy(dz):
-        to = shifted(0, 0, dz, 1)
+        to = shifted(0, 0, dz)
         return remote(
             mine_w.at[to[1]], near_w.at[z], misc_send.at[1 + dz], misc_recv.at[1 + dz], (*to, core)
         )
@@ -426,15 +459,16 @@
         weight_copy(dz).wait()
 
 
-def feed(picks, hidden, latents, ropes, send, q, r, wg, wu, wd, weights):
+def feed(ids, gate_vals, hidden, latents, ropes, send, q, r, wg, wu, wd):
     smem = pl.BlockSpec(memory_space=pltpu.SMEM)
     vmem = pl.BlockSpec(memory_space=pltpu.VMEM)
     hbm = pl.BlockSpec(memory_space=pl.ANY)
     bf16 = jnp.bfloat16
     packed = BLOCK + ropes.shape[1] * BLOCK // LAT
     blocks = jax.ShapeDtypeStruct((2 * N_DP, packed, LAT), bf16)
-    capacity = picks.shape[1] // N_DP
-    width = hidden.shape[1]
+    count, width = hidden.shape
+    capacity = count // 2
+    weights = (2 * count, N_DP * capacity // 2)
     chips = (SENDS, capacity, width)
     dma = pltpu.SemaphoreType.DMA
     chunks = SENDS // CHUNK
@@ -445,12 +479,13 @@
             jax.ShapeDtypeStruct(q.shape, bf16),
             jax.ShapeDtypeStruct(r.shape, bf16),
             jax.ShapeDtypeStruct(chips, bf16),
-            jax.ShapeDtypeStruct((4,) + weights.shape[1:], bf16),
-        ),
-        in_specs=[vmem] * 4 + [smem] + [hbm] * 5 + [vmem],
+            jax.ShapeDtypeStruct((4,) + weights, bf16),
+        ),
+        in_specs=[vmem] * 5 + [smem] + [hbm] * 5,
         out_specs=(hbm, hbm, hbm, vmem, vmem),
         scratch_shapes=[
             pltpu.VMEM((N_DP, capacity, width), bf16),
+            pltpu.VMEM((2,) + weights, bf16),
             pltpu.VMEM(wg.shape, bf16),
             pltpu.VMEM(wu.shape, bf16),
             pltpu.VMEM(wd.shape, bf16),
@@ -474,7 +509,7 @@
             flops=11 * 10**9, bytes_accessed=24 * 2**20, transcendentals=2**19
         ),
         name="feed",
-    )(picks, hidden, latents, ropes, send, q, r, wg, wu, wd, weights)
+    )(ids, gate_vals, hidden, latents, ropes, send, q, r, wg, wu, wd)
 
 
 def close_kernel(
@@ -500,7 +535,8 @@
     ]
     for load in loads:
         load.start()
-    column = [(*shifted(0, 0, dz, 1), core) for dz in (1, 2, 3)]
+    shifted = neighbours()
+    column = [(*shifted(0, 0, dz), core) for dz in (1, 2, 3)]
     others = [(plane, zl, zh, 1 - core), (plane, zl, 1 - zh, core), (plane, zl, 1 - zh, 1 - core)]
     barrier = pltpu.get_barrier_semaphore()
     for device in column + [others[0], others[2]]:
@@ -658,23 +694,9 @@
     rows, width = hidden_in.shape
     capacity = rows // 2
 
-    turn = jnp.arange(N_DP, dtype=jnp.int32)
-    experts = turn % (N_DP // 2) * 2 + turn // (N_DP // 2)
-    named = expert_ids[:, :, None] == experts[None, None, :]
-    hits = jnp.any(named, axis=1)
-    before = jnp.cumsum(hits.astype(jnp.int32), axis=0) - hits
-    picked = hits[:, :, None] & (
-        before[:, :, None] == jnp.arange(capacity, dtype=jnp.int32)[None, None, :]
-    )
-    picks = picked.astype(jnp.bfloat16).reshape(rows, N_DP * capacity)
-    gates = jnp.sum(jnp.where(named, gate_vals[:, :, None], 0.0), axis=1)
-    weights = jnp.where(picked, gates[:, :, None], 0.0).reshape(rows, 2, -1)
-    high = weights.astype(jnp.bfloat16)
-    low = (weights - high.astype(jnp.float32)).astype(jnp.bfloat16)
-    split = jnp.concatenate([high, low], axis=0).transpose(1, 0, 2)
-
     kv, q_par, r_par, partial, near_w = feed(
-        picks,
+        expert_ids.T,
+        gate_vals.T,
         hidden_in,
         cache_latent,
         cache_rope,
@@ -684,7 +706,6 @@
         w_gate[0],
         w_up[0],
         w_down[0],
-        split,
     )
     r_own = q_rope.reshape(TOK, HEADS_DEV, ROPE)
     r_par = r_par.reshape(TOK, HEADS_DEV, ROPE)

time: 207 us -> 201 us (0.971)
  waiting for transfers between devices: 23.9 us -> 17.3 us
  starting transfers between devices: 11.8 us -> 14.4 us
  local copies, waits for them, and re-layouts: 9.64 us -> 7.26 us
    all_to_all x1, waiting for transfers between devices: 15.1 us -> 10.1 us  [shards(): lax.all_to_all(partial, 'plane', split_axis=0, concat_axis=0, tiled=True)]
    pallas_call x1, Pallas kernels: 116 us -> 113 us  [feed(): pl.pallas_call(feed_kernel, out_shape=(blocks, jax.ShapeDtypeStruct(q.sha...]
    pallas_call x2, Pallas kernels: 20.6 us -> 23.7 us  [attend(): pl.pallas_call(attend_kernel, out_shape=(jax.ShapeDtypeStruct((tok, heads...]
    ppermute x2, starting transfers between devices: 3.96 us -> 6.46 us  [swap(): return lax.ppermute(value, axis, [(0, 1), (1, 0)])]
    unnamed x35 -> x33, local copies, waits for them, and re-layouts: 7.63 us -> 6.12 us
  transfers between devices with their start and end apart: 3 -> 3, of which waited for: 2 -> 2; matrix products, arithmetic and copies ran while one was open for 1% -> 2% of each run, Pallas kernels for 10% -> 12%
where the time goes in v5:
time: 201 us; the launch traced here: 198 us
  Pallas kernels  156 us (78%)
  waiting for transfers between devices  17.3 us (9%)
  starting transfers between devices  14.4 us (7%)
  local copies, waits for them, and re-layouts  7.26 us (4%)
    pallas_call x1, Pallas kernels, feed(): pl.pallas_call(feed_kernel, out_shape=(blocks, jax.ShapeDtypeStruct(q.sha...  113 us
    pallas_call x2, Pallas kernels, attend(): pl.pallas_call(attend_kernel, out_shape=(jax.ShapeDtypeStruct((tok, heads...  23.7 us
    pallas_call x1, Pallas kernels, close(): pl.pallas_call(close_kernel, out_shape=(jax.ShapeDtypeStruct(hidden.shape...  19.6 us
    all_to_all x1, waiting for transfers between devices, shards(): lax.all_to_all(partial, 'plane', split_axis=0, concat_axis=0, tiled=True)  10.1 us
    all_to_all x1, starting transfers between devices, shards(): lax.all_to_all(partial, 'plane', split_axis=0, concat_axis=0, tiled=True)  7.95 us
    ppermute x2, waiting for transfers between devices, swap(): return lax.ppermute(value, axis, [(0, 1), (1, 0)])  7.19 us
    ppermute x2, starting transfers between devices, swap(): return lax.ppermute(value, axis, [(0, 1), (1, 0)])  6.46 us
    unnamed x33, local copies, waits for them, and re-layouts  6.12 us
  transfers between devices with their start and end apart: 3, of which 2 were waited for; matrix products, arithmetic and copies ran while one was open for 2% of the time, Pallas kernels for 12%

profile of v5, /device:TPU:23, one launch (start us, length us, event | category | flops | bytes accessed | tf_op | source)
XLA Modules:
  0.0 197.5 jit_solution(15432663871740333283)
XLA Ops:
  0.6 112.8 %feed.1 = (bf16[64,144,512]{2,1,0:T(8,128)(2,1)}, bf16[64,16,512]{2,1,0:T(8,128)(2,1)}, bf16[64,1024]{1,0:T(8,128)(2,1)}, bf16[64,8,3584]{2,1,0:T(8,128)(2,1)}, bf16[4,32,128]{2,1,0:T(8,128)(2,1)}) custom-call(s32[8,16]{1,0:T(8,128)} %bitcast.31, f32[8,16]{1,0:T(8,128)} %bitcast.32, bf16[16,3584]{1,0:T(8,128)(2,1)} %hidden.3, bf16[8,128,512]{2,1,0:T(8,128)(2,1)} %latents.1, ...), custom_call_target="tpu_custom_call" | custom-call | flops 11000000512 | bytes 25165824 | tf_op jit(solution)/shard_map/feed/pallas_call | solution.py:475
  113.5 7.9 %all-to-all-start = ((bf16[64,8,3584]{2,1,0:T(8,128)(2,1)}), bf16[64,8,3584]{2,1,0:T(8,128)(2,1)}, u32[]{:S(2)}, u32[]{:S(2)}) async-start(bf16[64,8,3584]{2,1,0:T(8,128)(2,1)} %get-tuple-element.13), calls=%async_computation | async-start | bytes 7340032 | tf_op jit(solution)/shard_map/all_to_all | solution.py:712
  121.4 0.2 reshape.112.r_ref
  121.8 12.3 %attend_partner.1 = (bf16[64,16,512]{2,1,0:T(8,128)(2,1)}, f32[64,16,128]{2,1,0:T(8,128)S(1)}) custom-call(s32[1,128]{1,0:T(1,128)S(1)} %reshape.111.table, s32[1,4]{1,0:T(1,128)S(1)} %copy-done.7, s32[1,4]{1,0:T(1,128)S(1)} %copy-done.8, s32[3]{0:T(128)S(1)} %pad_add_fusion.where, bf16[64,144,512]{2,1,0:T(8,128)(2,1)} %get-tuple-element.14.kv, ...), custom_call_target="tpu_custom_call" | custom-call | flops 5000000000 | bytes 41943040 | tf_op jit(solution)/shard_map/attend_partner/pallas_call | solution.py:176
  134.2 6.4 %collective-permute-start = (bf16[64,16,512]{2,1,0:T(8,128)(2,1)}, bf16[64,16,512]{2,1,0:T(8,128)(2,1)}, u32[]{:S(2)}, u32[]{:S(2)}) collective-permute-start(bf16[64,16,512]{2,1,0:T(8,128)(2,1)} %get-tuple-element.17.after), channel_id=1, source_target_pairs={{0,2},{2,0},{1,3},{3,1},{4,6},{6,4},{5,7},{7,5},{8,10},{10,8},{9,1... | collective-permute-start | bytes 3145736 | tf_op jit(solution)/shard_map/ppermute | solution.py:671
  140.6 0.3 copy.29
  140.9 0.2 reshape.110.r_ref.r_hbm
  141.1 0.4 copy.33.w_rope_ref
  141.6 0.2 reduce-window.4
  142.1 0.4 slice_negate_fusion
  142.5 11.4 %attend_own.1 = (bf16[64,16,512]{2,1,0:T(8,128)(2,1)S(1)}, f32[64,16,128]{2,1,0:T(8,128)S(1)}) custom-call(s32[1,128]{1,0:T(1,128)S(1)} %reshape.111.table, s32[1,4]{1,0:T(1,128)S(1)} %copy-done.7, s32[1,4]{1,0:T(1,128)S(1)} %copy-done.8, s32[3]{0:T(128)S(1)} %pad_add_fusion.where, bf16[64,144,512]{2,1,0:T(8,128)(2,1)} %get-tuple-element.14.kv, ...), custom_call_target="tpu_custom_call" | custom-call | flops 5000000000 | bytes 41943040 | tf_op jit(solution)/shard_map/attend_own/pallas_call | solution.py:176
  153.9 1.0 copy-done.1
  154.9 0.8 copy-done.2
  155.7 0.5 pad_maximum_fusion.w_turn_ref
  156.2 0.1 multiply_sine_fusion
  156.5 7.2 %collective-permute-done.1 = f32[64,16]{0,1:T(8,128)S(1)} collective-permute-done((f32[64,16]{0,1:T(8,128)S(1)}, f32[64,16]{0,1:T(8,128)S(1)}, u32[]{:S(2)}, u32[]{:S(2)}) %collective-permute-start.1) | collective-permute-done | bytes 4128 | tf_op jit(solution)/shard_map/ppermute | solution.py:671
  163.8 10.1 %all-to-all-done = bf16[64,8,3584]{2,1,0:T(8,128)(2,1)} async-done(((bf16[64,8,3584]{2,1,0:T(8,128)(2,1)}), bf16[64,8,3584]{2,1,0:T(8,128)(2,1)}, u32[]{:S(2)}, u32[]{:S(2)}) %all-to-all-start) | async-done | bytes 3670048 | tf_op jit(solution)/shard_map/all_to_all | solution.py:712
  173.9 0.2 broadcast_in_dim.4.sb_hbm
  174.1 1.0 copy-done.3
  175.1 19.6 %close.1 = (bf16[16,3584]{1,0:T(8,128)(2,1)S(1)}, bf16[16,512]{1,0:T(8,128)(2,1)S(1)}, bf16[16,64]{1,0:T(8,128)(2,1)S(1)}, bf16[64,16,512]{2,1,0:T(8,128)(2,1)S(1)}) custom-call(bf16[16,4,8,3584]{3,2,1,0:T(8,128)(2,1)} %bitcast.5.returned_hbm, bf16[3584,512]{1,0:T(8,128)(2,1)} %w_lat_hbm.1, bf16[64,16,512]{2,1,0:T(8,128)(2,1)S(1)} %copy-done, ...), custom_call_target="tpu_custom_call" | custom-call | tf_op jit(solution)/shard_map/close/pallas_call | solution.py:643
  194.7 0.6 copy.38
  195.4 0.6 copy.39
  196.0 0.6 copy.40
  196.6 1.0 copy.41
  (42 shorter events, 0.9 us)
Async XLA Ops:
  113.4 8.0 %copy-start.12 = (bf16[64,1024]{1,0:T(8,128)(2,1)S(1)}, bf16[64,1024]{1,0:T(8,128)(2,1)}, u32[]{:S(2)}) copy-start(bf16[64,1024]{1,0:T(8,128)(2,1)} %get-tuple-element.16) | copy-start | bytes 393220
  113.4 8.2 %copy-start.13 = (s32[1,4,32]{2,1,0:T(4,128)S(1)}, s32[1,4,32]{2,1,0:T(4,128)}, u32[]{:S(2)}) copy-start(s32[1,4,32]{2,1,0:T(4,128)} %param.29) | copy-start | bytes 1540
  113.4 8.4 %copy-start = (bf16[64,16,512]{2,1,0:T(8,128)(2,1)S(1)}, bf16[64,16,512]{2,1,0:T(8,128)(2,1)}, u32[]{:S(2)}) copy-start(bf16[64,16,512]{2,1,0:T(8,128)(2,1)} %q_hbm.1) | copy-start | bytes 3145732
  113.4 8.3 %copy-start.7 = (s32[1,4]{1,0:T(1,128)S(1)}, s32[1,4]{1,0:T(1,128)}, u32[]{:S(2)}) copy-start(s32[1,4]{1,0:T(1,128)} %lengths.3) | copy-start | bytes 52
  113.5 8.3 %copy-start.8 = (s32[1,4]{1,0:T(1,128)S(1)}, s32[1,4]{1,0:T(1,128)}, u32[]{:S(2)}) copy-start(s32[1,4]{1,0:T(1,128)} %counts.3) | copy-start | bytes 52
  113.5 8.3 %copy-start.9 = (bf16[64,16,512]{2,1,0:T(8,128)(2,1)S(1)}, bf16[64,16,512]{2,1,0:T(8,128)(2,1)}, u32[]{:S(2)}) copy-start(bf16[64,16,512]{2,1,0:T(8,128)(2,1)} %get-tuple-element.15.q_ref) | copy-start | bytes 3145732
  113.5 60.4 %all-to-all-start = ((bf16[64,8,3584]{2,1,0:T(8,128)(2,1)}), bf16[64,8,3584]{2,1,0:T(8,128)(2,1)}, u32[]{:S(2)}, u32[]{:S(2)}) async-start(bf16[64,8,3584]{2,1,0:T(8,128)(2,1)} %get-tuple-element.13), calls=%async_computation | async-start | bytes 7340032 | tf_op jit(solution)/shard_map/all_to_all | solution.py:712
  121.8 19.1 %copy-start.11 = (bf16[64,1024]{1,0:T(8,128)(2,1)S(1)}, bf16[64,1024]{1,0:T(8,128)(2,1)}, u32[]{:S(2)}) copy-start(bf16[64,1024]{1,0:T(8,128)(2,1)} %r.1) | copy-start | bytes 393220
  121.8 19.3 %copy-start.10 = (bf16[3584,64]{0,1:T(8,128)(2,1)S(1)}, bf16[3584,64]{0,1:T(8,128)(2,1)}, u32[]{:S(2)}) copy-start(bf16[3584,64]{0,1:T(8,128)(2,1)} %param.24) | copy-start | bytes 1376260
  134.2 29.6 %collective-permute-start = (bf16[64,16,512]{2,1,0:T(8,128)(2,1)}, bf16[64,16,512]{2,1,0:T(8,128)(2,1)}, u32[]{:S(2)}, u32[]{:S(2)}) collective-permute-start(bf16[64,16,512]{2,1,0:T(8,128)(2,1)} %get-tuple-element.17.after), channel_id=1, source_target_pairs={{0,2},{2,0},{1,3},{3,1},{4,6},{6,4},{5,7},{7,5},{8,10},{10,8},{9,1... | collective-permute-start | bytes 3145736 | tf_op jit(solution)/shard_map/ppermute | solution.py:671
  140.9 22.8 %collective-permute-start.1 = (f32[64,16]{0,1:T(8,128)S(1)}, f32[64,16]{0,1:T(8,128)S(1)}, u32[]{:S(2)}, u32[]{:S(2)}) collective-permute-start(f32[64,16]{0,1:T(8,128)S(1)} %bitcast.25), channel_id=1, source_target_pairs={{0,2},{2,0},{1,3},{3,1},{4,6},{6,4},{5,7},{7,5},{8,10},{10,8},{9,1... | collective-permute-start | bytes 12296 | tf_op jit(solution)/shard_map/ppermute | solution.py:671
  142.5 31.6 %copy-start.4 = (bf16[16,3584]{1,0:T(8,128)(2,1)S(1)}, bf16[16,3584]{1,0:T(8,128)(2,1)}, u32[]{:S(2)}) copy-start(bf16[16,3584]{1,0:T(8,128)(2,1)} %hidden.3) | copy-start | bytes 344068
  142.5 31.6 %copy-start.5 = (bf16[4,32,128]{2,1,0:T(8,128)(2,1)S(1)}, bf16[4,32,128]{2,1,0:T(8,128)(2,1)}, u32[]{:S(2)}) copy-start(bf16[4,32,128]{2,1,0:T(8,128)(2,1)} %get-tuple-element.21.near_w) | copy-start | bytes 98308
  142.5 31.6 %copy-start.6 = (f32[512]{0:T(512)S(1)}, f32[512]{0:T(512)}, u32[]{:S(2)}) copy-start(f32[512]{0:T(512)} %param.25) | copy-start | bytes 6148
  153.9 1.0 copy-start.1
  154.9 0.8 copy-start.2
  174.1 1.0 copy-start.3

commit v6 on v5

--- a/solution.py
+++ b/solution.py
@@ -187,7 +187,7 @@
             pltpu.SemaphoreType.DMA((SLOTS,)),
             pltpu.VMEM((MAXB // GROUP, TILE * heads, GROUP * BLOCK), jnp.float32),
         ],
-        compiler_params=pltpu.CompilerParams(vmem_limit_bytes=48 * 2**20),
+        compiler_params=pltpu.CompilerParams(vmem_limit_bytes=56 * 2**20),
         cost_estimate=pl.CostEstimate(
             flops=5 * 10**9, bytes_accessed=40 * 2**20, transcendentals=2 * 2**20
         ),
@@ -514,7 +514,7 @@
 
 def close_kernel(
     returned_hbm, w_lat_hbm, q_hbm, r_hbm, oa_hbm, ob_hbm, sa_hbm, sb_hbm,
-    near_w, hidden, w_rope_ref, w_turn_ref, gain, cosine, sine, ok_ref,
+    near_w, hidden, w_rope_ref, gain, cosine, sine, ok_ref,
     hidden_out, new_latent, new_rope, out_ref,
     returned, w_lat, q_ref, r_ref, oa, ob, sa, sb,
     sums, sums_out, inbox, fresh, load_sem, sum_send, sum_recv, fresh_send, fresh_recv,
@@ -578,7 +578,8 @@
     loads[1].wait()
     latent = jnp.dot(x, w_lat[...], preferred_element_type=jnp.float32)
     plain = jnp.dot(x, w_rope_ref[...], preferred_element_type=jnp.float32)
-    turned = jnp.dot(x, w_turn_ref[...], preferred_element_type=jnp.float32)
+    half = ROPE // 2
+    turned = jnp.concatenate([-plain[:, half:], plain[:, :half]], axis=1)
     scale = lax.rsqrt(jnp.mean(latent * latent, axis=1, keepdims=True) + NORM_EPS)
     latent = (latent * scale * gain[...]).astype(jnp.bfloat16)
     rope = (plain * cosine[...] + turned * sine[...]).astype(jnp.bfloat16)
@@ -606,7 +607,7 @@
     lat_keys = keys[:, :LAT]
     rope_keys = keys[:, LAT : LAT + ROPE]
 
-    def tile(t, carry):
+    for t in range(TOK // TILE):
         at = pl.ds(t * TILE, TILE)
         size = TILE * heads
         s = lax.dot_general(
@@ -628,9 +629,6 @@
         mixed = mixed + wa * oa[at].reshape(size, LAT).astype(jnp.float32)
         mixed = mixed + wb * ob[at].reshape(size, LAT).astype(jnp.float32)
         out_ref[at] = (mixed / weight).astype(jnp.bfloat16).reshape(TILE, heads, LAT)
-        return carry
-
-    lax.fori_loop(0, TOK // TILE, tile, 0)
 
 
 def close(large, small):
@@ -661,7 +659,7 @@
             dma((3,)), dma((3,)),
         ],
         compiler_params=pltpu.CompilerParams(
-            collective_id=2, has_side_effects=True, vmem_limit_bytes=48 * 2**20
+            collective_id=2, has_side_effects=True, vmem_limit_bytes=56 * 2**20
         ),
         name="close",
     )(*large, *small)
@@ -727,7 +725,6 @@
     angle = positions.astype(jnp.float32)[:, None] * frequency[None, :]
     cosine = jnp.tile(jnp.cos(angle), (1, 2))
     sine = jnp.tile(jnp.sin(angle), (1, 2))
-    w_turn = jnp.concatenate([-w_rope[:, half:], w_rope[:, :half]], axis=1)
     tokens = jnp.arange(TOK, dtype=jnp.int32)
     ends = jnp.cumsum(counts)
     chat_of = jnp.sum((tokens[:, None] >= ends[None, :]).astype(jnp.int32), axis=1)
@@ -747,7 +744,6 @@
             near_w,
             hidden_in,
             w_rope,
-            w_turn,
             latent_gain[None, :],
             cosine,
             sine,

time: 201 us -> 208 us (1.035); the launches traced: 198 us -> 207 us
  Pallas kernels: 156 us -> 175 us
  waiting for transfers between devices: 17.3 us -> 5.24 us
  local copies, waits for them, and re-layouts: 7.26 us -> 13.8 us
  starting transfers between devices: 14.4 us -> 11 us
    pallas_call x2, Pallas kernels: 23.7 us -> 35.8 us  [attend(): pl.pallas_call(attend_kernel, out_shape=(jax.ShapeDtypeStruct((tok, heads...]
    ppermute x2, waiting for transfers between devices: 7.19 us -> 0.01 us  [swap(): return lax.ppermute(value, axis, [(0, 1), (1, 0)])]
    pallas_call x1, Pallas kernels: 19.6 us -> 25.9 us  [close(): pl.pallas_call(close_kernel, out_shape=(jax.ShapeDtypeStruct(hidden.shape...]
    all_to_all x1, waiting for transfers between devices: 10.1 us -> 5.23 us  [shards(): lax.all_to_all(partial, 'plane', split_axis=0, concat_axis=0, tiled=True)]
    ppermute x2, starting transfers between devices: 6.46 us -> 3.08 us  [swap(): return lax.ppermute(value, axis, [(0, 1), (1, 0)])]
    unnamed x33 -> x19, local copies, waits for them, and re-layouts: 6.12 us -> 7.67 us
  transfers between devices with their start and end apart: 3 -> 3, of which waited for: 2 -> 1; matrix products, arithmetic and copies ran while one was open for 2% -> 4% of each run, Pallas kernels for 12% -> 17%
where the time goes in v6:
time: 208 us; the launch traced here: 207 us
  Pallas kernels  175 us (84%)
  local copies, waits for them, and re-layouts  13.8 us (7%)
  starting transfers between devices  11 us (5%)
  waiting for transfers between devices  5.24 us (3%)
    pallas_call x1, Pallas kernels, feed(): pl.pallas_call(feed_kernel, out_shape=(blocks, jax.ShapeDtypeStruct(q.sha...  113 us
    pallas_call x2, Pallas kernels, attend(): pl.pallas_call(attend_kernel, out_shape=(jax.ShapeDtypeStruct((tok, heads...  35.8 us
    pallas_call x1, Pallas kernels, close(): pl.pallas_call(close_kernel, out_shape=(jax.ShapeDtypeStruct(hidden.shape...  25.9 us
    all_to_all x1, starting transfers between devices, shards(): lax.all_to_all(partial, 'plane', split_axis=0, concat_axis=0, tiled=True)  7.95 us
    unnamed x19, local copies, waits for them, and re-layouts  7.67 us
    all_to_all x1, waiting for transfers between devices, shards(): lax.all_to_all(partial, 'plane', split_axis=0, concat_axis=0, tiled=True)  5.23 us
  transfers between devices with their start and end apart: 3, of which 1 were waited for; matrix products, arithmetic and copies ran while one was open for 4% of the time, Pallas kernels for 17%

profile of v6, /device:TPU:23, one launch (start us, length us, event | category | flops | bytes accessed | tf_op | source)
XLA Modules:
  0.0 207.1 jit_solution(3262928855016726889)
XLA Ops:
  0.6 112.8 %feed.1 = (bf16[64,144,512]{2,1,0:T(8,128)(2,1)}, bf16[64,16,512]{2,1,0:T(8,128)(2,1)}, bf16[64,1024]{1,0:T(8,128)(2,1)}, bf16[64,8,3584]{2,1,0:T(8,128)(2,1)}, bf16[4,32,128]{2,1,0:T(8,128)(2,1)}) custom-call(s32[8,16]{1,0:T(8,128)} %bitcast.31, f32[8,16]{1,0:T(8,128)} %bitcast.32, bf16[16,3584]{1,0:T(8,128)(2,1)} %hidden.3, bf16[8,128,512]{2,1,0:T(8,128)(2,1)} %latents.1, ...), custom_call_target="tpu_custom_call" | custom-call | flops 11000000512 | bytes 25165824 | tf_op jit(solution)/shard_map/feed/pallas_call | solution.py:475
  113.4 7.9 %all-to-all-start = ((bf16[64,8,3584]{2,1,0:T(8,128)(2,1)}), bf16[64,8,3584]{2,1,0:T(8,128)(2,1)}, u32[]{:S(2)}, u32[]{:S(2)}) async-start(bf16[64,8,3584]{2,1,0:T(8,128)(2,1)} %get-tuple-element.13), calls=%async_computation | async-start | bytes 7340032 | tf_op jit(solution)/shard_map/all_to_all | solution.py:710
  121.4 0.9 reshape.112.r_ref
  122.3 0.6 reshape.111.table
  122.9 0.6 pad_add_fusion.where
  123.5 17.9 %attend_partner.1 = (bf16[64,16,512]{2,1,0:T(8,128)(2,1)}, f32[64,16,128]{2,1,0:T(8,128)}) custom-call(s32[1,128]{1,0:T(1,128)} %reshape.111.table, s32[1,4]{1,0:T(1,128)} %lengths.3, s32[1,4]{1,0:T(1,128)} %counts.3, s32[3]{0:T(128)} %pad_add_fusion.where, bf16[64,144,512]{2,1,0:T(8,128)(2,1)} %get-tuple-element.14.kv, ...), custom_call_target="tpu_custom_call" | custom-call | flops 5000000000 | bytes 41943040 | tf_op jit(solution)/shard_map/attend_partner/pallas_call | solution.py:176
  141.5 1.3 copy.25
  142.7 3.0 %collective-permute-start.1 = (f32[64,16]{0,1:T(8,128)S(1)}, f32[64,16]{0,1:T(8,128)S(1)}, u32[]{:S(2)}, u32[]{:S(2)}) collective-permute-start(f32[64,16]{0,1:T(8,128)S(1)} %bitcast.23), channel_id=1, source_target_pairs={{0,2},{2,0},{1,3},{3,1},{4,6},{6,4},{5,7},{7,5},{8,10},{10,8},{9,1... | collective-permute-start | bytes 12296 | tf_op jit(solution)/shard_map/ppermute | solution.py:669
  145.7 0.2 reduce-window.4
  145.9 0.1 convert_reduce_fusion.1
  146.1 0.9 reshape.110.r_ref.r_hbm
  147.1 0.7 fusion.1.ok_ref
  147.8 17.9 %attend_own.1 = (bf16[64,16,512]{2,1,0:T(8,128)(2,1)}, f32[64,16,128]{2,1,0:T(8,128)}) custom-call(s32[1,128]{1,0:T(1,128)} %reshape.111.table, s32[1,4]{1,0:T(1,128)} %lengths.3, s32[1,4]{1,0:T(1,128)} %counts.3, s32[3]{0:T(128)} %pad_add_fusion.where, bf16[64,144,512]{2,1,0:T(8,128)(2,1)} %get-tuple-element.14.kv, bf16[64,16,512]{2,1,0:T(8,128)(2,1)} %q_hbm.1, ...), custom_call_target="tpu_custom_call" | custom-call | flops 5000000000 | bytes 41943040 | tf_op jit(solution)/shard_map/attend_own/pallas_call | solution.py:176
  165.7 0.1 multiply_sine_fusion
  165.9 0.7 tile.21.sine
  166.6 0.7 tile.9.cosine
  167.2 1.2 copy.27.w_rope_ref
  168.6 5.2 %all-to-all-done = bf16[64,8,3584]{2,1,0:T(8,128)(2,1)} async-done(((bf16[64,8,3584]{2,1,0:T(8,128)(2,1)}), bf16[64,8,3584]{2,1,0:T(8,128)(2,1)}, u32[]{:S(2)}, u32[]{:S(2)}) %all-to-all-start) | async-done | bytes 3670048 | tf_op jit(solution)/shard_map/all_to_all | solution.py:710
  173.8 1.0 broadcast_in_dim.4.sb_hbm
  174.8 25.9 %close.1 = (bf16[16,3584]{1,0:T(8,128)(2,1)}, bf16[16,512]{1,0:T(8,128)(2,1)}, bf16[16,64]{1,0:T(8,128)(2,1)}, bf16[64,16,512]{2,1,0:T(8,128)(2,1)}) custom-call(bf16[16,4,8,3584]{3,2,1,0:T(8,128)(2,1)} %bitcast.5.returned_hbm, bf16[3584,512]{1,0:T(8,128)(2,1)} %w_lat_hbm.1, bf16[64,16,512]{2,1,0:T(8,128)(2,1)} %q_hbm.1, ...), custom_call_target="tpu_custom_call" | custom-call | tf_op jit(solution)/shard_map/close/pallas_call | solution.py:641
  200.7 1.6 copy.32
  202.3 1.3 copy.33
  203.6 1.3 copy.34
  204.9 2.3 %copy.35 = bf16[64,16,512]{2,1,0:T(8,128)(2,1)} copy(bf16[64,16,512]{2,1,0:T(8,128)(2,1)} %get-tuple-element.31) | data formatting | bytes 2097152
  (26 shorter events, 0.4 us)
Async XLA Ops:
  113.4 8.0 %copy-start.3 = (bf16[64,1024]{1,0:T(8,128)(2,1)S(1)}, bf16[64,1024]{1,0:T(8,128)(2,1)}, u32[]{:S(2)}) copy-start(bf16[64,1024]{1,0:T(8,128)(2,1)} %get-tuple-element.16) | copy-start | bytes 393220
  113.4 8.8 %copy-start.4 = (s32[1,4,32]{2,1,0:T(4,128)S(1)}, s32[1,4,32]{2,1,0:T(4,128)}, u32[]{:S(2)}) copy-start(s32[1,4,32]{2,1,0:T(4,128)} %param.29) | copy-start | bytes 1540
  113.4 60.4 %all-to-all-start = ((bf16[64,8,3584]{2,1,0:T(8,128)(2,1)}), bf16[64,8,3584]{2,1,0:T(8,128)(2,1)}, u32[]{:S(2)}, u32[]{:S(2)}) async-start(bf16[64,8,3584]{2,1,0:T(8,128)(2,1)} %get-tuple-element.13), calls=%async_computation | async-start | bytes 7340032 | tf_op jit(solution)/shard_map/all_to_all | solution.py:710
  123.5 22.3 %copy-start.6 = (s32[1,4]{1,0:T(1,128)S(1)}, s32[1,4]{1,0:T(1,128)}, u32[]{:S(2)}) copy-start(s32[1,4]{1,0:T(1,128)} %counts.3) | copy-start | bytes 52
  123.5 22.5 %copy-start.5 = (s32[1,4]{1,0:T(1,128)S(1)}, s32[1,4]{1,0:T(1,128)}, u32[]{:S(2)}) copy-start(s32[1,4]{1,0:T(1,128)} %lengths.3) | copy-start | bytes 52
  123.5 22.6 %copy-start.2 = (bf16[64,1024]{1,0:T(8,128)(2,1)S(1)}, bf16[64,1024]{1,0:T(8,128)(2,1)}, u32[]{:S(2)}) copy-start(bf16[64,1024]{1,0:T(8,128)(2,1)} %r.1) | copy-start | bytes 393220
  141.4 27.2 %collective-permute-start = (bf16[64,16,512]{2,1,0:T(8,128)(2,1)}, bf16[64,16,512]{2,1,0:T(8,128)(2,1)S(1)}, u32[]{:S(2)}, u32[]{:S(2)}) collective-permute-start(bf16[64,16,512]{2,1,0:T(8,128)(2,1)} %get-tuple-element.17.after), channel_id=1, source_target_pairs={{0,2},{2,0},{1,3},{3,1},{4,6},{6,4},{5,7},{7,5},{8,10},{10,8},{9,1... | collective-permute-start | bytes 3145736 | tf_op jit(solution)/shard_map/ppermute | solution.py:669
  142.7 25.7 %collective-permute-start.1 = (f32[64,16]{0,1:T(8,128)S(1)}, f32[64,16]{0,1:T(8,128)S(1)}, u32[]{:S(2)}, u32[]{:S(2)}) collective-permute-start(f32[64,16]{0,1:T(8,128)S(1)} %bitcast.23), channel_id=1, source_target_pairs={{0,2},{2,0},{1,3},{3,1},{4,6},{6,4},{5,7},{7,5},{8,10},{10,8},{9,1... | collective-permute-start | bytes 12296 | tf_op jit(solution)/shard_map/ppermute | solution.py:669
  147.8 19.5 %copy-start.1 = (bf16[3584,64]{0,1:T(8,128)(2,1)S(1)}, bf16[3584,64]{0,1:T(8,128)(2,1)}, u32[]{:S(2)}) copy-start(bf16[3584,64]{0,1:T(8,128)(2,1)} %param.24) | copy-start | bytes 1376260
  168.6 6.2 %copy-start = (bf16[64,16,512]{2,1,0:T(8,128)(2,1)}, bf16[64,16,512]{2,1,0:T(8,128)(2,1)S(1)}, u32[]{:S(2)}) copy-start(bf16[64,16,512]{2,1,0:T(8,128)(2,1)S(1)} %collective-permute-done.ob_hbm) | copy-start | bytes 3145732

commit v7 on v6

--- a/solution.py
+++ b/solution.py
@@ -187,7 +187,7 @@
             pltpu.SemaphoreType.DMA((SLOTS,)),
             pltpu.VMEM((MAXB // GROUP, TILE * heads, GROUP * BLOCK), jnp.float32),
         ],
-        compiler_params=pltpu.CompilerParams(vmem_limit_bytes=56 * 2**20),
+        compiler_params=pltpu.CompilerParams(vmem_limit_bytes=48 * 2**20),
         cost_estimate=pl.CostEstimate(
             flops=5 * 10**9, bytes_accessed=40 * 2**20, transcendentals=2 * 2**20
         ),
@@ -659,7 +659,7 @@
             dma((3,)), dma((3,)),
         ],
         compiler_params=pltpu.CompilerParams(
-            collective_id=2, has_side_effects=True, vmem_limit_bytes=56 * 2**20
+            collective_id=2, has_side_effects=True, vmem_limit_bytes=48 * 2**20
         ),
         name="close",
     )(*large, *small)

time: 208 us -> 201 us (0.966); the launches traced: 207 us -> 197 us
  Pallas kernels: 175 us -> 168 us
  local copies, waits for them, and re-layouts: 13.8 us -> 7.37 us
  waiting for transfers between devices: 5.24 us -> 8.72 us
    pallas_call x1, Pallas kernels: 25.9 us -> 19.2 us  [close(): pl.pallas_call(close_kernel, out_shape=(jax.ShapeDtypeStruct(hidden.shape...]
    all_to_all x1, waiting for transfers between devices: 5.23 us -> 7.7 us  [shards(): lax.all_to_all(partial, 'plane', split_axis=0, concat_axis=0, tiled=True)]
    unnamed x19 -> x29, local copies, waits for them, and re-layouts: 7.67 us -> 6.22 us
  transfers between devices with their start and end apart: 3 -> 3, of which waited for: 1 -> 2; matrix products, arithmetic and copies ran while one was open for 4% -> 2% of each run, Pallas kernels for 17% -> 18%
where the time goes in v7:
time: 201 us; the launch traced here: 197 us
  Pallas kernels  168 us (84%)
  starting transfers between devices  11 us (5%)
  waiting for transfers between devices  8.72 us (4%)
  local copies, waits for them, and re-layouts  7.37 us (4%)
    pallas_call x1, Pallas kernels, feed(): pl.pallas_call(feed_kernel, out_shape=(blocks, jax.ShapeDtypeStruct(q.sha...  113 us
    pallas_call x2, Pallas kernels, attend(): pl.pallas_call(attend_kernel, out_shape=(jax.ShapeDtypeStruct((tok, heads...  36.5 us
    pallas_call x1, Pallas kernels, close(): pl.pallas_call(close_kernel, out_shape=(jax.ShapeDtypeStruct(hidden.shape...  19.2 us
    all_to_all x1, starting transfers between devices, shards(): lax.all_to_all(partial, 'plane', split_axis=0, concat_axis=0, tiled=True)  7.95 us
    all_to_all x1, waiting for transfers between devices, shards(): lax.all_to_all(partial, 'plane', split_axis=0, concat_axis=0, tiled=True)  7.7 us
    unnamed x29, local copies, waits for them, and re-layouts  6.22 us
  transfers between devices with their start and end apart: 3, of which 2 were waited for; matrix products, arithmetic and copies ran while one was open for 2% of the time, Pallas kernels for 18%

profile of v7, /device:TPU:23, one launch (start us, length us, event | category | flops | bytes accessed | tf_op | source)
XLA Modules:
  0.0 197.1 jit_solution(3732631373424752033)
XLA Ops:
  0.6 112.8 %feed.1 = (bf16[64,144,512]{2,1,0:T(8,128)(2,1)}, bf16[64,16,512]{2,1,0:T(8,128)(2,1)}, bf16[64,1024]{1,0:T(8,128)(2,1)}, bf16[64,8,3584]{2,1,0:T(8,128)(2,1)}, bf16[4,32,128]{2,1,0:T(8,128)(2,1)}) custom-call(s32[8,16]{1,0:T(8,128)} %bitcast.31, f32[8,16]{1,0:T(8,128)} %bitcast.32, bf16[16,3584]{1,0:T(8,128)(2,1)} %hidden.3, bf16[8,128,512]{2,1,0:T(8,128)(2,1)} %latents.1, ...), custom_call_target="tpu_custom_call" | custom-call | flops 11000000512 | bytes 25165824 | tf_op jit(solution)/shard_map/feed/pallas_call | solution.py:475
  113.5 7.9 %all-to-all-start = ((bf16[64,8,3584]{2,1,0:T(8,128)(2,1)}), bf16[64,8,3584]{2,1,0:T(8,128)(2,1)}, u32[]{:S(2)}, u32[]{:S(2)}) async-start(bf16[64,8,3584]{2,1,0:T(8,128)(2,1)} %get-tuple-element.13), calls=%async_computation | async-start | bytes 7340032 | tf_op jit(solution)/shard_map/all_to_all | solution.py:710
  121.4 0.2 reshape.112.r_ref
  121.8 18.7 %attend_partner.1 = (bf16[64,16,512]{2,1,0:T(8,128)(2,1)}, f32[64,16,128]{2,1,0:T(8,128)S(1)}) custom-call(s32[1,128]{1,0:T(1,128)S(1)} %reshape.111.table, s32[1,4]{1,0:T(1,128)S(1)} %copy-done.6, s32[1,4]{1,0:T(1,128)S(1)} %copy-done.7, s32[3]{0:T(128)S(1)} %pad_add_fusion.where, bf16[64,144,512]{2,1,0:T(8,128)(2,1)} %get-tuple-element.14.kv, ...), custom_call_target="tpu_custom_call" | custom-call | flops 5000000000 | bytes 41943040 | tf_op jit(solution)/shard_map/attend_partner/pallas_call | solution.py:176
  140.5 2.3 %collective-permute-start = (bf16[64,16,512]{2,1,0:T(8,128)(2,1)}, bf16[64,16,512]{2,1,0:T(8,128)(2,1)}, u32[]{:S(2)}, u32[]{:S(2)}) collective-permute-start(bf16[64,16,512]{2,1,0:T(8,128)(2,1)} %get-tuple-element.17.after), channel_id=1, source_target_pairs={{0,2},{2,0},{1,3},{3,1},{4,6},{6,4},{5,7},{7,5},{8,10},{10,8},{9,1... | collective-permute-start | bytes 3145736 | tf_op jit(solution)/shard_map/ppermute | solution.py:669
  142.8 0.3 copy.25
  143.1 0.8 collective-permute-start.1
  143.9 0.2 reduce-window.4
  144.1 0.1 convert_reduce_fusion.1
  144.2 0.1 select_reduce_fusion
  144.3 0.2 reshape.110.r_ref.r_hbm
  144.6 17.8 %attend_own.1 = (bf16[64,16,512]{2,1,0:T(8,128)(2,1)S(1)}, f32[64,16,128]{2,1,0:T(8,128)S(1)}) custom-call(s32[1,128]{1,0:T(1,128)S(1)} %reshape.111.table, s32[1,4]{1,0:T(1,128)S(1)} %copy-done.6, s32[1,4]{1,0:T(1,128)S(1)} %copy-done.7, s32[3]{0:T(128)S(1)} %pad_add_fusion.where, bf16[64,144,512]{2,1,0:T(8,128)(2,1)} %get-tuple-element.14.kv, ...), custom_call_target="tpu_custom_call" | custom-call | flops 5000000000 | bytes 41943040 | tf_op jit(solution)/shard_map/attend_own/pallas_call | solution.py:176
  162.4 0.8 copy-done.1
  163.2 0.1 multiply_sine_fusion
  163.5 1.5 copy.27.w_rope_ref
  165.1 1.0 collective-permute-done.1
  166.2 7.7 %all-to-all-done = bf16[64,8,3584]{2,1,0:T(8,128)(2,1)} async-done(((bf16[64,8,3584]{2,1,0:T(8,128)(2,1)}), bf16[64,8,3584]{2,1,0:T(8,128)(2,1)}, u32[]{:S(2)}, u32[]{:S(2)}) %all-to-all-start) | async-done | bytes 3670048 | tf_op jit(solution)/shard_map/all_to_all | solution.py:710
  173.9 0.2 broadcast_in_dim.4.sb_hbm
  174.1 1.0 copy-done.2
  175.1 19.2 %close.1 = (bf16[16,3584]{1,0:T(8,128)(2,1)S(1)}, bf16[16,512]{1,0:T(8,128)(2,1)S(1)}, bf16[16,64]{1,0:T(8,128)(2,1)S(1)}, bf16[64,16,512]{2,1,0:T(8,128)(2,1)S(1)}) custom-call(bf16[16,4,8,3584]{3,2,1,0:T(8,128)(2,1)} %bitcast.5.returned_hbm, bf16[3584,512]{1,0:T(8,128)(2,1)} %w_lat_hbm.1, bf16[64,16,512]{2,1,0:T(8,128)(2,1)S(1)} %copy-done, ...), custom_call_target="tpu_custom_call" | custom-call | tf_op jit(solution)/shard_map/close/pallas_call | solution.py:641
  194.3 0.6 copy.32
  195.0 0.6 copy.33
  195.6 0.6 copy.34
  196.2 1.0 copy.35
  (36 shorter events, 0.7 us)
Async XLA Ops:
  113.4 8.0 %copy-start.10 = (bf16[64,1024]{1,0:T(8,128)(2,1)S(1)}, bf16[64,1024]{1,0:T(8,128)(2,1)}, u32[]{:S(2)}) copy-start(bf16[64,1024]{1,0:T(8,128)(2,1)} %get-tuple-element.16) | copy-start | bytes 393220
  113.4 8.2 %copy-start.11 = (s32[1,4,32]{2,1,0:T(4,128)S(1)}, s32[1,4,32]{2,1,0:T(4,128)}, u32[]{:S(2)}) copy-start(s32[1,4,32]{2,1,0:T(4,128)} %param.29) | copy-start | bytes 1540
  113.4 8.4 %copy-start = (bf16[64,16,512]{2,1,0:T(8,128)(2,1)S(1)}, bf16[64,16,512]{2,1,0:T(8,128)(2,1)}, u32[]{:S(2)}) copy-start(bf16[64,16,512]{2,1,0:T(8,128)(2,1)} %q_hbm.1) | copy-start | bytes 3145732
  113.4 8.3 %copy-start.6 = (s32[1,4]{1,0:T(1,128)S(1)}, s32[1,4]{1,0:T(1,128)}, u32[]{:S(2)}) copy-start(s32[1,4]{1,0:T(1,128)} %lengths.3) | copy-start | bytes 52
  113.5 8.3 %copy-start.7 = (s32[1,4]{1,0:T(1,128)S(1)}, s32[1,4]{1,0:T(1,128)}, u32[]{:S(2)}) copy-start(s32[1,4]{1,0:T(1,128)} %counts.3) | copy-start | bytes 52
  113.5 8.3 %copy-start.8 = (bf16[64,16,512]{2,1,0:T(8,128)(2,1)S(1)}, bf16[64,16,512]{2,1,0:T(8,128)(2,1)}, u32[]{:S(2)}) copy-start(bf16[64,16,512]{2,1,0:T(8,128)(2,1)} %get-tuple-element.15.q_ref) | copy-start | bytes 3145732
  113.5 60.4 %all-to-all-start = ((bf16[64,8,3584]{2,1,0:T(8,128)(2,1)}), bf16[64,8,3584]{2,1,0:T(8,128)(2,1)}, u32[]{:S(2)}, u32[]{:S(2)}) async-start(bf16[64,8,3584]{2,1,0:T(8,128)(2,1)} %get-tuple-element.13), calls=%async_computation | async-start | bytes 7340032 | tf_op jit(solution)/shard_map/all_to_all | solution.py:710
  121.8 22.4 %copy-start.9 = (bf16[64,1024]{1,0:T(8,128)(2,1)S(1)}, bf16[64,1024]{1,0:T(8,128)(2,1)}, u32[]{:S(2)}) copy-start(bf16[64,1024]{1,0:T(8,128)(2,1)} %r.1) | copy-start | bytes 393220
  140.5 25.6 %collective-permute-start = (bf16[64,16,512]{2,1,0:T(8,128)(2,1)}, bf16[64,16,512]{2,1,0:T(8,128)(2,1)}, u32[]{:S(2)}, u32[]{:S(2)}) collective-permute-start(bf16[64,16,512]{2,1,0:T(8,128)(2,1)} %get-tuple-element.17.after), channel_id=1, source_target_pairs={{0,2},{2,0},{1,3},{3,1},{4,6},{6,4},{5,7},{7,5},{8,10},{10,8},{9,1... | collective-permute-start | bytes 3145736 | tf_op jit(solution)/shard_map/ppermute | solution.py:669
  143.1 23.0 %collective-permute-start.1 = (f32[64,16]{0,1:T(8,128)S(1)}, f32[64,16]{0,1:T(8,128)S(1)}, u32[]{:S(2)}, u32[]{:S(2)}) collective-permute-start(f32[64,16]{0,1:T(8,128)S(1)} %bitcast.25), channel_id=1, source_target_pairs={{0,2},{2,0},{1,3},{3,1},{4,6},{6,4},{5,7},{7,5},{8,10},{10,8},{9,1... | collective-permute-start | bytes 12296 | tf_op jit(solution)/shard_map/ppermute | solution.py:669
  144.6 29.4 %copy-start.3 = (bf16[16,3584]{1,0:T(8,128)(2,1)S(1)}, bf16[16,3584]{1,0:T(8,128)(2,1)}, u32[]{:S(2)}) copy-start(bf16[16,3584]{1,0:T(8,128)(2,1)} %hidden.3) | copy-start | bytes 344068
  144.6 29.4 %copy-start.4 = (bf16[4,32,128]{2,1,0:T(8,128)(2,1)S(1)}, bf16[4,32,128]{2,1,0:T(8,128)(2,1)}, u32[]{:S(2)}) copy-start(bf16[4,32,128]{2,1,0:T(8,128)(2,1)} %get-tuple-element.21.near_w) | copy-start | bytes 98308
  144.6 29.4 %copy-start.5 = (f32[512]{0:T(512)S(1)}, f32[512]{0:T(512)}, u32[]{:S(2)}) copy-start(f32[512]{0:T(512)} %param.25) | copy-start | bytes 6148
  162.4 0.8 copy-start.1
  174.1 1.0 copy-start.2
